TPU v7x, 512 devices: a whole 4x4x16 slice. The times are simulated.
512 devices in a mesh: region: 8 (over z_lo), sub: 64 (over x, y, z_hi, core).
Axes of the slice: x: 4, y: 4, z: 16 (z_hi: 2, z_lo: 8; z = z_hi * 8 + z_lo), core: 2. Of those that a mesh axis runs over, the one named last changes fastest.
Arguments:
- conn_x: int32 [2, 1048576], P(None, ('region', 'sub')), may hold values from 0 to 2175, as said below
- conn_y: int32 [2, 1048576], P(None, ('region', 'sub')), may hold values from 0 to 2559, as said below
- conn_z: int32 [2, 1048576], P(None, ('region', 'sub')), may hold values from 0 to 2111, as said below
- send_y: int32 [262144], P(('region', 'sub')), may hold values from 0 to 2047, as said below
- send_z: int32 [32768], P(('region', 'sub')), may hold values from 0 to 2047, as said below
- perm: float32 [2, 3, 1048576], P(None, None, ('region', 'sub')), may hold values from 0.1 to 10
- storage: float32 [2, 1048576], P(None, ('region', 'sub')), may hold values from 0.5 to 20
- sigma: float32 [1048576], P(('region', 'sub')), may hold values from 0.5 to 20
- source: float32 [2, 1048576], P(None, ('region', 'sub')), may hold values from -120 to 166
Outputs:
- trace: float32 [2, 3211264], P(None, ('region', 'sub'))
- pressure: float32 [2, 1048576], P(None, ('region', 'sub'))
- flux: float32 [2, 6, 1048576], P(None, None, ('region', 'sub'))
Inputs may be any that keep to these rules, and one draw needn't show every extreme that they name: `conn_x`: each device's hexahedra form a block of 16 x 4 x 32, stored in a drawn order; its faces of each family are stored in a drawn order. Row 0 names the lower face along the first dimension, row 1 the upper. `conn_y`: values of 2048 and more name the block's lower-side faces, in the order of the lower device's send_y; the same owned face is named once as upper and at most once as lower. `conn_z`: values of 2048 and more name the block's lower-side faces, in the order of the lower device's send_z. `send_y`: distinct within a device: the block's upper-side faces along the second dimension. `send_z`: distinct within a device: the block's upper-side faces along the third dimension.
All inputs are finite; a program needn't handle non-finite values.
Results may differ from a plain program's by a relative error of at most 0.00013.
Values sent between devices are 32-bit elements; how exact they have to be, the bound alone decides.
A program may use at most 64 MiB of HBM per device.

v0:
```python
import jax
import jax.numpy as jnp
from jax import lax
from jax.sharding import PartitionSpec as P

ITERS = 3
NXF = 2176
NYF = 2048
NZF = 2048


def shifted(block, axis, distance):
    devices = range(lax.axis_size(axis))
    route = [(i - distance, i) for i in devices if i - distance in devices]
    return lax.ppermute(block, axis, route)


def element_terms(perm, storage, sigma):
    trans = 2.0 * perm
    total = 2.0 * jnp.sum(trans, axis=1)
    diag_a = total[0] + storage[0] + sigma
    diag_b = total[1] + storage[1] + sigma
    return (trans, diag_a, diag_b, diag_a * diag_b - sigma * sigma)


def solve_pair(load, sigma, diag_a, diag_b, determ):
    first = (diag_b * load[0] + sigma * load[1]) / determ
    second = (sigma * load[0] + diag_a * load[1]) / determ
    return jnp.stack([first, second])


def face_load(values, trans):
    return sum((trans[:, side] * (values[side][:, 0] + values[side][:, 1]) for side in range(3)))


def deposit(values, index, count):
    return jnp.zeros((2, count), jnp.float32).at[:, index].add(values)


def blend(first, factor, second):
    return tuple((a + factor * b for a, b in zip(first, second)))


def inner(first, second):
    return (
        jnp.sum(first[0] * second[0])
        + jnp.sum(first[1] * second[1])
        + jnp.sum(first[2] * second[2])
    )


def local(conn_x, conn_y, conn_z, send_y, send_z, perm, storage, sigma, source):
    trans, diag_a, diag_b, determ = element_terms(perm, storage, sigma)
    conns = (conn_x, conn_y, conn_z)
    counts = (NXF, NYF + send_y.shape[0], NZF + send_z.shape[0])

    def widen(vector):
        face_x, face_y, face_z = vector
        under_y = shifted(face_y[:, send_y], "sub", 1)
        under_z = shifted(face_z[:, send_z], "region", 1)
        return (
            face_x,
            jnp.concatenate([face_y, under_y], axis=1),
            jnp.concatenate([face_z, under_z], axis=1),
        )

    def settle(parts):
        part_x, part_y, part_z = parts
        own_y, rim_y = (part_y[:, :NYF], part_y[:, NYF:])
        own_z, rim_z = (part_z[:, :NZF], part_z[:, NZF:])
        above_y = shifted(rim_y, "sub", -1)
        above_z = shifted(rim_z, "region", -1)
        total_y = own_y.at[:, send_y].add(above_y)
        total_z = own_z.at[:, send_z].add(above_z)
        return (part_x, total_y, total_z)

    def pairs(load):
        return solve_pair(load, sigma, diag_a, diag_b, determ)

    def faces(vector):
        extended = widen(vector)
        return tuple((jnp.take(extended[side], conns[side], axis=1) for side in range(3)))

    def operate(vector):
        values = faces(vector)
        solved = pairs(face_load(values, trans))
        return settle(
            tuple(
                (
                    deposit(
                        trans[:, side][:, None] * (values[side] - solved[:, None]),
                        conns[side],
                        counts[side],
                    )
                    for side in range(3)
                )
            )
        )

    base = pairs(source)
    shape = (2, 2, base.shape[1])
    rhs = settle(
        tuple(
            (
                deposit(
                    jnp.broadcast_to((trans[:, side] * base)[:, None], shape),
                    conns[side],
                    counts[side],
                )
                for side in range(3)
            )
        )
    )
    trace = tuple((jnp.zeros_like(part) for part in rhs))
    resid = rhs

    def squares(vector):
        return lax.psum(inner(vector, vector), ("region", "sub"))

    direction = rhs
    norm_now = squares(resid)
    for step in range(ITERS):
        image = operate(direction)
        alpha = norm_now / lax.psum(inner(direction, image), ("region", "sub"))
        trace = blend(trace, alpha, direction)
        resid = blend(resid, -alpha, image)
        norm_next = squares(resid)
        direction = blend(resid, norm_next / norm_now, direction)
        norm_now = norm_next
    values = faces(trace)
    pressure = pairs(source + face_load(values, trans))
    flux = jnp.concatenate(
        [trans[:, side][:, None] * (pressure[:, None] - values[side]) for side in range(3)], axis=1
    )
    trace_out = jnp.concatenate([trace[0], trace[1], trace[2]], axis=1)
    return (trace_out, pressure, flux)


def solution(mesh):
    in_specs = (
        P(None, ("region", "sub")),
        P(None, ("region", "sub")),
        P(None, ("region", "sub")),
        P(("region", "sub")),
        P(("region", "sub")),
        P(None, None, ("region", "sub")),
        P(None, ("region", "sub")),
        P(("region", "sub")),
        P(None, ("region", "sub")),
    )
    out_specs = (
        P(None, ("region", "sub")),
        P(None, ("region", "sub")),
        P(None, None, ("region", "sub")),
    )
    return jax.shard_map(local, mesh=mesh, in_specs=in_specs, out_specs=out_specs, check_vma=False)
```

profile of v0, /device:TPU:1, one launch (start us, length us, event | category | flops | bytes accessed | tf_op | source)
XLA Modules:
  0.0 1181.3 jit_solution(8899645000437677779)
XLA Ops:
  6.5 22.7 %scatter_custom_fusion.1 = f32[2,2560]{0,1:T(8,128)S(1)} fusion(s32[4096]{0:T(1024)S(1)} %bitcast.301, f32[4096,2]{1,0:T(8,128)S(1)} %bitcast.285, f32[]{:T(128)} %constant.31.clone.1), kind=kCustom, calls=%fused_computation.54 | custom fusion | flops 8192 | bytes 20484 | tf_op jit(solution)/shard_map/scatter-add | solution.py:37
  30.0 8.8 collective-permute-start
  40.7 22.9 %scatter_custom_fusion.3 = f32[2,2112]{0,1:T(8,128)S(1)} fusion(s32[4096]{0:T(1024)S(1)} %bitcast.306, f32[4096,2]{1,0:T(8,128)} %bitcast.286, f32[]{:T(128)} %constant.31.clone.1), kind=kCustom, calls=%fused_computation.70 | custom fusion | flops 8192 | bytes 17408 | tf_op jit(solution)/shard_map/scatter-add | solution.py:37
  70.0 22.9 %scatter_custom_fusion = f32[2,2176]{0,1:T(8,128)S(1)} fusion(s32[4096]{0:T(1024)} %bitcast.312, f32[4096,2]{1,0:T(8,128)} %bitcast.287, f32[]{:T(128)} %constant.31.clone.1), kind=kCustom, calls=%fused_computation.62 | custom fusion | flops 8192 | bytes 17920 | tf_op jit(solution)/shard_map/scatter-add | solution.py:37
  92.9 15.4 %gather_fusion.8 = f32[4096,2]{1,0:T(8,128)} fusion(f32[2,2176]{0,1:T(8,128)S(1)} %scatter_custom_fusion, s32[4096]{0:T(1024)} %broadcast_clamp_fusion.2), kind=kCustom, calls=%fused_computation.clone | custom fusion | bytes 81920 | tf_op jit(solution)/shard_map/jit(_take)/gather | solution.py:82
  108.4 2.2 copy.134
  115.3 4.6 collective-permute-start.3
  121.1 4.1 scatter_custom_fusion.2
  125.2 1.6 gather_fusion
  126.9 10.7 collective-permute-start.2
  137.6 1.8 pad_maximum_fusion.1
  139.5 15.4 %gather_fusion.10 = f32[4096,2]{1,0:T(8,128)} fusion(f32[2,2112]{0,1:T(8,128)} %pad_maximum_fusion.1, s32[4096]{0:T(1024)S(1)} %copy-done.45), kind=kCustom, calls=%fused_computation.2.clone | custom fusion | bytes 81920 | tf_op jit(solution)/shard_map/jit(_take)/gather | solution.py:82
  154.8 2.2 copy.136
  157.4 2.1 pad_maximum_fusion
  159.5 15.4 %gather_fusion.9 = f32[4096,2]{1,0:T(8,128)} fusion(f32[2,2560]{0,1:T(8,128)} %pad_maximum_fusion, s32[4096]{0:T(1024)S(1)} %copy-done.41), kind=kCustom, calls=%fused_computation.1.clone | custom fusion | bytes 81920 | tf_op jit(solution)/shard_map/jit(_take)/gather | solution.py:82
  175.0 2.9 copy.135
  180.3 2.8 copy.139
  183.1 23.7 %scatter_custom_fusion.8 = f32[2,2112]{0,1:T(8,128)} fusion(s32[4096]{0:T(1024)} %bitcast.308, f32[4096,2]{1,0:T(8,128)} %copy.139, f32[]{:T(128)} %constant.31.clone.1), kind=kCustom, calls=%fused_computation.68 | custom fusion | flops 8192 | bytes 17408 | tf_op jit(solution)/shard_map/scatter-add | solution.py:37
  208.8 2.0 copy.137
  210.8 23.7 %scatter_custom_fusion.5 = f32[2,2176]{0,1:T(8,128)} fusion(s32[4096]{0:T(1024)} %bitcast.313, f32[4096,2]{1,0:T(8,128)} %copy.137, f32[]{:T(128)} %constant.31.clone.1), kind=kCustom, calls=%fused_computation.60 | custom fusion | flops 8192 | bytes 17920 | tf_op jit(solution)/shard_map/scatter-add | solution.py:37
  234.5 2.2 multiply_reduce_fusion
  237.8 2.0 copy.138
  239.8 23.7 %scatter_custom_fusion.6 = f32[2,2560]{0,1:T(8,128)} fusion(s32[4096]{0:T(1024)} %bitcast.302, f32[4096,2]{1,0:T(8,128)} %copy.138, f32[]{:T(128)} %constant.31.clone.1), kind=kCustom, calls=%fused_computation.52 | custom fusion | flops 8192 | bytes 20992 | tf_op jit(solution)/shard_map/scatter-add | solution.py:37
  263.6 1.8 slice.320
  265.7 1.9 collective-permute-start.4
  267.6 3.2 scatter_custom_fusion.9
  270.8 2.3 multiply_reduce_fusion.2
  274.6 8.1 collective-permute-done.4
  282.7 4.5 scatter_custom_fusion.7
  292.3 119.9 %all-reduce = (f32[]{:T(128)}, f32[]{:T(128)}) all-reduce(f32[]{:T(128)S(6)} %add.359, f32[]{:T(128)S(6)} %add.371), channel_id=1, replica_groups=mesh['region'=8,'sub'=64] {'region','sub'}, use_global_device_ids=true, to_apply=%region_9.0 | all-reduce | flops 2 | bytes 16 | tf_op jit(solution)/shard_map/psum | solution.py:118
  417.3 100.9 %psum.44 = f32[]{:T(128)} all-reduce(f32[]{:T(128)S(6)} %add.376), channel_id=1, replica_groups=mesh['region'=8,'sub'=64] {'region','sub'}, use_global_device_ids=true, to_apply=%region_22.26 | all-reduce | flops 1 | bytes 8 | tf_op jit(solution)/shard_map/psum | solution.py:118
  521.2 6.3 collective-permute-start.6
  528.8 2.8 collective-permute-start.7
  532.0 10.8 gather_fusion.11
  544.4 10.8 gather_fusion.13
  557.0 10.8 gather_fusion.12
  570.1 22.8 %scatter_custom_fusion.11 = f32[2,2560]{0,1:T(8,128)S(1)} fusion(s32[4096]{0:T(1024)} %bitcast.303, f32[4096,2]{1,0:T(8,128)S(1)} %copy.162, f32[]{:T(128)} %constant.31.clone.1), kind=kCustom, calls=%fused_computation.50 | custom fusion | flops 8192 | bytes 20992 | tf_op jit(solution)/shard_map/scatter-add | solution.py:37
  593.7 2.1 collective-permute-start.8
  595.8 2.0 copy.164
  597.9 22.9 %scatter_custom_fusion.13 = f32[2,2112]{0,1:T(8,128)S(1)} fusion(s32[4096]{0:T(1024)} %bitcast.309, f32[4096,2]{1,0:T(8,128)} %copy.164, f32[]{:T(128)} %constant.31.clone.1), kind=kCustom, calls=%fused_computation.66 | custom fusion | flops 8192 | bytes 17408 | tf_op jit(solution)/shard_map/scatter-add | solution.py:37
  622.7 2.0 copy.160
  624.7 22.9 %scatter_custom_fusion.10 = f32[2,2176]{0,1:T(8,128)S(1)} fusion(s32[4096]{0:T(1024)} %bitcast.314, f32[4096,2]{1,0:T(8,128)} %copy.160, f32[]{:T(128)} %constant.31.clone.1), kind=kCustom, calls=%fused_computation.58 | custom fusion | flops 8192 | bytes 17920 | tf_op jit(solution)/shard_map/scatter-add | solution.py:37
  652.7 4.1 scatter_custom_fusion.12
  659.7 108.5 %psum.45 = f32[]{:T(128)} all-reduce(f32[]{:T(128)S(6)} %add.391), channel_id=1, replica_groups=mesh['region'=8,'sub'=64] {'region','sub'}, use_global_device_ids=true, to_apply=%region_31.35 | all-reduce | flops 1 | bytes 8 | tf_op jit(solution)/shard_map/psum | solution.py:124
  773.4 99.4 %psum.46 = f32[]{:T(128)} all-reduce(f32[]{:T(128)S(6)} %add.397), channel_id=1, replica_groups=mesh['region'=8,'sub'=64] {'region','sub'}, use_global_device_ids=true, to_apply=%region_35.39 | all-reduce | flops 1 | bytes 8 | tf_op jit(solution)/shard_map/psum | solution.py:118
  875.7 8.9 collective-permute-start.10
  885.8 2.4 collective-permute-start.11
  888.6 10.8 gather_fusion.14
  901.1 10.8 gather_fusion.16
  913.7 10.8 gather_fusion.15
  926.8 22.8 %scatter_custom_fusion.16 = f32[2,2560]{0,1:T(8,128)S(1)} fusion(s32[4096]{0:T(1024)} %bitcast.304, f32[4096,2]{1,0:T(8,128)S(1)} %copy.181, f32[]{:T(128)} %constant.31.clone.1), kind=kCustom, calls=%fused_computation.48 | custom fusion | flops 8192 | bytes 20992 | tf_op jit(solution)/shard_map/scatter-add | solution.py:37
  950.4 1.9 collective-permute-start.12
  952.3 2.0 copy.183
  954.3 22.9 %scatter_custom_fusion.18 = f32[2,2112]{0,1:T(8,128)S(1)} fusion(s32[4096]{0:T(1024)} %bitcast.310, f32[4096,2]{1,0:T(8,128)} %copy.183, f32[]{:T(128)} %constant.31.clone.1), kind=kCustom, calls=%fused_computation.64 | custom fusion | flops 8192 | bytes 17408 | tf_op jit(solution)/shard_map/scatter-add | solution.py:37
  979.2 2.0 copy.179
  981.2 22.9 %scatter_custom_fusion.15 = f32[2,2176]{0,1:T(8,128)S(1)} fusion(s32[4096]{0:T(1024)} %bitcast.315, f32[4096,2]{1,0:T(8,128)} %copy.179, f32[]{:T(128)} %constant.31.clone.1), kind=kCustom, calls=%fused_computation.56 | custom fusion | flops 8192 | bytes 17920 | tf_op jit(solution)/shard_map/scatter-add | solution.py:37
  1009.2 4.3 scatter_custom_fusion.17
  1016.5 108.1 %psum.47 = f32[]{:T(128)} all-reduce(f32[]{:T(128)S(6)} %add.412), channel_id=1, replica_groups=mesh['region'=8,'sub'=64] {'region','sub'}, use_global_device_ids=true, to_apply=%region_44.48 | all-reduce | flops 1 | bytes 8 | tf_op jit(solution)/shard_map/psum | solution.py:124
  1127.9 1.6 gather_fusion.6
  1130.6 8.7 collective-permute-start.14
  1140.1 3.1 collective-permute-start.15
  1143.2 10.8 gather_fusion.17
  1155.7 10.8 gather_fusion.19
  1168.3 10.8 gather_fusion.18
  (429 shorter events, 76.8 us)
Async XLA Ops:
  6.5 32.3 %copy-start.108 = (s32[2,2048]{1,0:T(2,128)S(1)}, s32[2,2048]{1,0:T(2,128)}, u32[]{:S(2)}) copy-start(s32[2,2048]{1,0:T(2,128)} %param.17) | copy-start | bytes 49156
  29.2 90.7 %copy-start = (f32[2,2560]{0,1:T(8,128)}, f32[2,2560]{0,1:T(8,128)S(1)}, u32[]{:S(2)}) copy-start(f32[2,2560]{0,1:T(8,128)S(1)} %scatter_custom_fusion.1) | copy-start | bytes 61444
  30.0 90.7 %collective-permute-start = (f32[2,512]{0,1:T(8,128)}, f32[2,512]{0,1:T(8,128)}, u32[]{:S(2)}, u32[]{:S(2)}) collective-permute-start(f32[2,512]{0,1:T(8,128)} %slice.307), channel_id=1, source_target_pairs={{1,0},{2,1},{3,2},{4,3},{5,4},{6,5},{7,6},{8,7},{9,8},{10,9},{11,1... | collective-permute-start | bytes 12296 | tf_op jit(solution)/shard_map/ppermute | solution.py:15
  38.8 27.6 %copy-start.112 = (s32[1,16,2,128]{3,1,2,0:T(8,128)}, s32[1,16,2,128]{3,1,2,0:T(8,128)S(1)}, u32[]{:S(2)}) copy-start(s32[1,16,2,128]{3,1,2,0:T(8,128)S(1)} %copy.199) | copy-start | bytes 49156
  39.2 26.4 %copy-start.107 = (s32[2,2048]{1,0:T(2,128)S(1)}, s32[2,2048]{1,0:T(2,128)}, u32[]{:S(2)}) copy-start(s32[2,2048]{1,0:T(2,128)} %param.16) | copy-start | bytes 49156
  39.2 26.5 %copy-start.109 = (s32[2,2048]{1,0:T(2,128)S(1)}, s32[2,2048]{1,0:T(2,128)}, u32[]{:S(2)}) copy-start(s32[2,2048]{1,0:T(2,128)} %param.15) | copy-start | bytes 49156
  39.2 26.6 %copy-start.111 = (s32[1,16,2,128]{3,1,2,0:T(8,128)S(1)}, s32[1,16,2,128]{3,1,2,0:T(8,128)}, u32[]{:S(2)}) copy-start(s32[1,16,2,128]{3,1,2,0:T(8,128)} %copy-done.110) | copy-start | bytes 49156
  40.7 26.3 %copy-start.123 = (s32[64]{0:T(128)S(1)}, s32[64]{0:T(128)}, u32[]{:S(2)}) copy-start(s32[64]{0:T(128)} %param.19) | copy-start | bytes 772
  40.7 26.8 %copy-start.121 = (s32[512]{0:T(512)S(1)}, s32[512]{0:T(512)}, u32[]{:S(2)}) copy-start(s32[512]{0:T(512)} %param.18) | copy-start | bytes 6148
  64.3 48.3 %collective-permute-start.1 = (f32[2,64]{0,1:T(8,128)}, f32[2,64]{0,1:T(8,128)}, u32[]{:S(2)}, u32[]{:S(2)}) collective-permute-start(f32[2,64]{0,1:T(8,128)} %slice.310), channel_id=1, source_target_pairs={{64,0},{128,64},{192,128},{256,192},{320,256},{384,320},{448,384},... | collective-permute-start | bytes 1544 | tf_op jit(solution)/shard_map/ppermute | solution.py:15
  65.6 503.1 %copy-start.15 = (pred[2,2048]{1,0:T(4,128)(4,1)}, pred[2,2048]{1,0:T(4,128)(4,1)S(1)}, u32[]{:S(2)}) copy-start(pred[2,2048]{1,0:T(4,128)(4,1)S(1)} %compare_and_fusion.1) | copy-start | bytes 12292
  65.7 112.2 %copy-start.18 = (pred[2,2048]{1,0:T(4,128)(4,1)}, pred[2,2048]{1,0:T(4,128)(4,1)S(1)}, u32[]{:S(2)}) copy-start(pred[2,2048]{1,0:T(4,128)(4,1)S(1)} %compare_and_fusion) | copy-start | bytes 12292
  65.7 503.0 %copy-start.6 = (pred[2,2048]{1,0:T(4,128)(4,1)}, pred[2,2048]{1,0:T(4,128)(4,1)S(1)}, u32[]{:S(2)}) copy-start(pred[2,2048]{1,0:T(4,128)(4,1)S(1)} %compare_and_fusion.2) | copy-start | bytes 12292
  67.5 53.1 %copy-start.120 = (s32[512]{0:T(512)}, s32[512]{0:T(512)S(1)}, u32[]{:S(2)}) copy-start(s32[512]{0:T(512)S(1)} %compare_select_fusion.3) | copy-start | bytes 6148
  92.9 18.3 %copy-start.122 = (s32[64]{0:T(128)S(1)}, s32[64]{0:T(128)}, u32[]{:S(2)}) copy-start(s32[64]{0:T(128)} %compare_select_fusion.4) | copy-start | bytes 772
  115.3 22.3 %collective-permute-start.3 = (f32[2,64]{0,1:T(8,128)}, f32[2,64]{0,1:T(8,128)}, u32[]{:S(2)}, u32[]{:S(2)}) collective-permute-start(f32[2,64]{0,1:T(8,128)} %bitcast.343), channel_id=1, source_target_pairs={{0,64},{64,128},{128,192},{192,256},{256,320},{320,384},{384,448},... | collective-permute-start | bytes 1544 | tf_op jit(solution)/shard_map/ppermute | solution.py:15
  120.3 399.4 %copy-start.83 = (f32[2,2176]{1,0:T(2,128)}, f32[2,2176]{1,0:T(2,128)S(1)}, u32[]{:S(2)}) copy-start(f32[2,2176]{1,0:T(2,128)S(1)} %copy.140) | copy-start | bytes 52228
  120.6 398.9 %copy-start.87 = (f32[2,2048]{1,0:T(2,128)}, f32[2,2048]{1,0:T(2,128)S(1)}, u32[]{:S(2)}) copy-start(f32[2,2048]{1,0:T(2,128)S(1)} %copy.146) | copy-start | bytes 49156
  125.2 14.2 %copy-start.45 = (s32[4096]{0:T(1024)S(1)}, s32[4096]{0:T(1024)}, u32[]{:S(2)}) copy-start(s32[4096]{0:T(1024)} %broadcast_clamp_fusion) | copy-start | bytes 49156
  126.9 30.5 %collective-permute-start.2 = (f32[2,512]{0,1:T(8,128)}, f32[2,512]{0,1:T(8,128)}, u32[]{:S(2)}, u32[]{:S(2)}) collective-permute-start(f32[2,512]{0,1:T(8,128)} %bitcast.342), channel_id=1, source_target_pairs={{0,1},{1,2},{2,3},{3,4},{4,5},{5,6},{6,7},{7,8},{8,9},{9,10},{10,1... | collective-permute-start | bytes 12296 | tf_op jit(solution)/shard_map/ppermute | solution.py:15
  157.4 362.2 %copy-start.89 = (f32[2,2048]{1,0:T(2,128)}, f32[2,2048]{1,0:T(2,128)S(1)}, u32[]{:S(2)}) copy-start(f32[2,2048]{1,0:T(2,128)S(1)} %copy.144) | copy-start | bytes 49156
  180.3 28.5 %copy-start.98 = (f32[2,2,2048]{2,0,1:T(2,128)S(1)}, f32[2,2,2048]{2,0,1:T(2,128)}, u32[]{:S(2)}) copy-start(f32[2,2,2048]{2,0,1:T(2,128)} %get-tuple-element.67) | copy-start | bytes 98308
  207.5 60.1 %collective-permute-start.5 = (f32[2,64]{0,1:T(8,128)S(1)}, f32[2,64]{0,1:T(8,128)S(1)}, u32[]{:S(2)}, u32[]{:S(2)}) collective-permute-start(f32[2,64]{0,1:T(8,128)S(1)} %slice.322), channel_id=1, source_target_pairs={{64,0},{128,64},{192,128},{256,192},{320,256},{384,320},{448,384},... | collective-permute-start | bytes 1544 | tf_op jit(solution)/shard_map/ppermute | solution.py:15
  265.7 17.0 %collective-permute-start.4 = (f32[2,512]{0,1:T(8,128)}, f32[2,512]{0,1:T(8,128)}, u32[]{:S(2)}, u32[]{:S(2)}) collective-permute-start(f32[2,512]{0,1:T(8,128)} %slice.320), channel_id=1, source_target_pairs={{1,0},{2,1},{3,2},{4,3},{5,4},{6,5},{7,6},{8,7},{9,8},{10,9},{11,1... | collective-permute-start | bytes 12296 | tf_op jit(solution)/shard_map/ppermute | solution.py:15
  288.2 231.9 %copy-start.116 = (s32[1024]{0:T(1024)S(1)}, s32[1024]{0:T(1024)}, u32[]{:S(2)}) copy-start(s32[1024]{0:T(1024)} %copy-done.115) | copy-start | bytes 12292
  414.2 105.4 %copy-start.91 = (f32[2,2048]{1,0:T(2,128)}, f32[2,2048]{1,0:T(2,128)S(1)}, u32[]{:S(2)}) copy-start(f32[2,2048]{1,0:T(2,128)S(1)} %get-tuple-element.21) | copy-start | bytes 49156
  414.8 104.8 %copy-start.93 = (f32[2,2048]{1,0:T(2,128)}, f32[2,2048]{1,0:T(2,128)S(1)}, u32[]{:S(2)}) copy-start(f32[2,2048]{1,0:T(2,128)S(1)} %get-tuple-element.23) | copy-start | bytes 49156
  415.5 104.2 %copy-start.85 = (f32[2,2176]{1,0:T(2,128)}, f32[2,2176]{1,0:T(2,128)S(1)}, u32[]{:S(2)}) copy-start(f32[2,2176]{1,0:T(2,128)S(1)} %get-tuple-element.25) | copy-start | bytes 52228
  519.6 24.4 %copy-start.12 = (f32[2,2048]{1,0:T(2,128)}, f32[2,2048]{1,0:T(2,128)S(1)}, u32[]{:S(2)}) copy-start(f32[2,2048]{1,0:T(2,128)S(1)} %multiply_add_fusion.11) | copy-start | bytes 49156
  519.6 36.9 %copy-start.9 = (f32[2,2048]{1,0:T(2,128)}, f32[2,2048]{1,0:T(2,128)S(1)}, u32[]{:S(2)}) copy-start(f32[2,2048]{1,0:T(2,128)S(1)} %multiply_add_fusion.12) | copy-start | bytes 49156
  521.2 35.3 %collective-permute-start.6 = (f32[2,512]{1,0:T(2,128)S(1)}, f32[2,512]{1,0:T(2,128)S(1)}, u32[]{:S(2)}, u32[]{:S(2)}) collective-permute-start(f32[2,512]{1,0:T(2,128)S(1)} %bitcast.337), channel_id=1, source_target_pairs={{0,1},{1,2},{2,3},{3,4},{4,5},{5,6},{6,7},{7,8},{8,9},{9,10},{10,1... | collective-permute-start | bytes 12296 | tf_op jit(solution)/shard_map/ppermute | solution.py:15
  528.8 15.3 %collective-permute-start.7 = (f32[2,64]{1,0:T(2,128)S(1)}, f32[2,64]{1,0:T(2,128)S(1)}, u32[]{:S(2)}, u32[]{:S(2)}) collective-permute-start(f32[2,64]{1,0:T(2,128)S(1)} %bitcast.339), channel_id=1, source_target_pairs={{0,64},{64,128},{128,192},{192,256},{256,320},{320,384},{384,448},... | collective-permute-start | bytes 1544 | tf_op jit(solution)/shard_map/ppermute | solution.py:15
  570.1 25.7 %copy-start.99 = (f32[2,2,2048]{2,0,1:T(2,128)S(1)}, f32[2,2,2048]{2,0,1:T(2,128)}, u32[]{:S(2)}) copy-start(f32[2,2,2048]{2,0,1:T(2,128)} %get-tuple-element.60) | copy-start | bytes 98308
  593.0 57.0 %copy-start.3 = (f32[2,2560]{0,1:T(8,128)}, f32[2,2560]{0,1:T(8,128)S(1)}, u32[]{:S(2)}) copy-start(f32[2,2560]{0,1:T(8,128)S(1)} %scatter_custom_fusion.11) | copy-start | bytes 61444
  593.7 59.0 %collective-permute-start.8 = (f32[2,512]{0,1:T(8,128)}, f32[2,512]{0,1:T(8,128)}, u32[]{:S(2)}, u32[]{:S(2)}) collective-permute-start(f32[2,512]{0,1:T(8,128)} %slice.332), channel_id=1, source_target_pairs={{1,0},{2,1},{3,2},{4,3},{5,4},{6,5},{7,6},{8,7},{9,8},{10,9},{11,1... | collective-permute-start | bytes 12296 | tf_op jit(solution)/shard_map/ppermute | solution.py:15
  595.8 26.9 %copy-start.96 = (f32[2,2,2048]{2,0,1:T(2,128)S(1)}, f32[2,2,2048]{2,0,1:T(2,128)}, u32[]{:S(2)}) copy-start(f32[2,2,2048]{2,0,1:T(2,128)} %get-tuple-element.62) | copy-start | bytes 98308
  621.4 28.7 %collective-permute-start.9 = (f32[2,64]{0,1:T(8,128)}, f32[2,64]{0,1:T(8,128)}, u32[]{:S(2)}, u32[]{:S(2)}) collective-permute-start(f32[2,64]{0,1:T(8,128)} %slice.334), channel_id=1, source_target_pairs={{64,0},{128,64},{192,128},{256,192},{320,256},{384,320},{448,384},... | collective-permute-start | bytes 1544 | tf_op jit(solution)/shard_map/ppermute | solution.py:15
  652.0 117.5 %copy-start.92 = (f32[2,2048]{1,0:T(2,128)S(1)}, f32[2,2048]{1,0:T(2,128)}, u32[]{:S(2)}) copy-start(f32[2,2048]{1,0:T(2,128)} %copy-done.91) | copy-start | bytes 49156
  652.0 118.2 %copy-start.94 = (f32[2,2048]{1,0:T(2,128)S(1)}, f32[2,2048]{1,0:T(2,128)}, u32[]{:S(2)}) copy-start(f32[2,2048]{1,0:T(2,128)} %copy-done.93) | copy-start | bytes 49156
  652.0 118.8 %copy-start.82 = (f32[2,2176]{1,0:T(2,128)S(1)}, f32[2,2176]{1,0:T(2,128)}, u32[]{:S(2)}) copy-start(f32[2,2176]{1,0:T(2,128)} %copy.161) | copy-start | bytes 52228
  652.1 118.8 %copy-start.86 = (f32[2,2176]{1,0:T(2,128)S(1)}, f32[2,2176]{1,0:T(2,128)}, u32[]{:S(2)}) copy-start(f32[2,2176]{1,0:T(2,128)} %copy-done.85) | copy-start | bytes 52228
  652.1 222.0 %copy-start.23 = (f32[2,2176]{1,0:T(2,128)S(1)}, f32[2,2176]{1,0:T(2,128)}, u32[]{:S(2)}) copy-start(f32[2,2176]{1,0:T(2,128)} %copy-done.22) | copy-start | bytes 52228
  656.8 217.7 %copy-start.117 = (s32[1024]{0:T(1024)S(1)}, s32[1024]{0:T(1024)}, u32[]{:S(2)}) copy-start(s32[1024]{0:T(1024)} %copy-done.115) | copy-start | bytes 12292
  874.1 14.5 %copy-start.80 = (f32[2,2176]{1,0:T(2,128)}, f32[2,2176]{1,0:T(2,128)S(1)}, u32[]{:S(2)}) copy-start(f32[2,2176]{1,0:T(2,128)S(1)} %multiply_add_fusion.1) | copy-start | bytes 52228
  874.1 26.5 %copy-start.27 = (f32[2,2048]{1,0:T(2,128)}, f32[2,2048]{1,0:T(2,128)S(1)}, u32[]{:S(2)}) copy-start(f32[2,2048]{1,0:T(2,128)S(1)} %multiply_add_fusion.7) | copy-start | bytes 49156
  874.2 39.0 %copy-start.25 = (f32[2,2048]{1,0:T(2,128)}, f32[2,2048]{1,0:T(2,128)S(1)}, u32[]{:S(2)}) copy-start(f32[2,2048]{1,0:T(2,128)S(1)} %multiply_add_fusion.8) | copy-start | bytes 49156
  875.7 37.4 %collective-permute-start.10 = (f32[2,512]{1,0:T(2,128)S(1)}, f32[2,512]{1,0:T(2,128)S(1)}, u32[]{:S(2)}, u32[]{:S(2)}) collective-permute-start(f32[2,512]{1,0:T(2,128)S(1)} %bitcast.338), channel_id=1, source_target_pairs={{0,1},{1,2},{2,3},{3,4},{4,5},{5,6},{6,7},{7,8},{8,9},{9,10},{10,1... | collective-permute-start | bytes 12296 | tf_op jit(solution)/shard_map/ppermute | solution.py:15
  885.8 14.9 %collective-permute-start.11 = (f32[2,64]{1,0:T(2,128)S(1)}, f32[2,64]{1,0:T(2,128)S(1)}, u32[]{:S(2)}, u32[]{:S(2)}) collective-permute-start(f32[2,64]{1,0:T(2,128)S(1)} %bitcast.340), channel_id=1, source_target_pairs={{0,64},{64,128},{128,192},{192,256},{256,320},{320,384},{384,448},... | collective-permute-start | bytes 1544 | tf_op jit(solution)/shard_map/ppermute | solution.py:15
  926.8 25.5 %copy-start.97 = (f32[2,2,2048]{2,0,1:T(2,128)S(1)}, f32[2,2,2048]{2,0,1:T(2,128)}, u32[]{:S(2)}) copy-start(f32[2,2,2048]{2,0,1:T(2,128)} %get-tuple-element.55) | copy-start | bytes 98308
  949.6 56.9 %copy-start.2 = (f32[2,2560]{0,1:T(8,128)}, f32[2,2560]{0,1:T(8,128)S(1)}, u32[]{:S(2)}) copy-start(f32[2,2560]{0,1:T(8,128)S(1)} %scatter_custom_fusion.16) | copy-start | bytes 61444
  950.4 58.9 %collective-permute-start.12 = (f32[2,512]{0,1:T(8,128)}, f32[2,512]{0,1:T(8,128)}, u32[]{:S(2)}, u32[]{:S(2)}) collective-permute-start(f32[2,512]{0,1:T(8,128)} %slice.344), channel_id=1, source_target_pairs={{1,0},{2,1},{3,2},{4,3},{5,4},{6,5},{7,6},{8,7},{9,8},{10,9},{11,1... | collective-permute-start | bytes 12296 | tf_op jit(solution)/shard_map/ppermute | solution.py:15
  952.3 26.9 %copy-start.95 = (f32[2,2,2048]{2,0,1:T(2,128)S(1)}, f32[2,2,2048]{2,0,1:T(2,128)}, u32[]{:S(2)}) copy-start(f32[2,2,2048]{2,0,1:T(2,128)} %get-tuple-element.57) | copy-start | bytes 98308
  977.9 28.7 %collective-permute-start.13 = (f32[2,64]{0,1:T(8,128)}, f32[2,64]{0,1:T(8,128)}, u32[]{:S(2)}, u32[]{:S(2)}) collective-permute-start(f32[2,64]{0,1:T(8,128)} %slice.346), channel_id=1, source_target_pairs={{64,0},{128,64},{192,128},{256,192},{320,256},{384,320},{448,384},... | collective-permute-start | bytes 1544 | tf_op jit(solution)/shard_map/ppermute | solution.py:15
  1008.5 117.3 %copy-start.24 = (f32[2,2176]{1,0:T(2,128)S(1)}, f32[2,2176]{1,0:T(2,128)}, u32[]{:S(2)}) copy-start(f32[2,2176]{1,0:T(2,128)} %copy-done.22) | copy-start | bytes 52228
  1008.6 117.3 %copy-start.81 = (f32[2,2176]{1,0:T(2,128)S(1)}, f32[2,2176]{1,0:T(2,128)}, u32[]{:S(2)}) copy-start(f32[2,2176]{1,0:T(2,128)} %copy-done.80) | copy-start | bytes 52228
  1008.6 117.3 %copy-start.84 = (f32[2,2176]{1,0:T(2,128)S(1)}, f32[2,2176]{1,0:T(2,128)}, u32[]{:S(2)}) copy-start(f32[2,2176]{1,0:T(2,128)} %copy-done.83) | copy-start | bytes 52228
  1008.6 117.4 %copy-start.14 = (f32[2,2048]{1,0:T(2,128)S(1)}, f32[2,2048]{1,0:T(2,128)}, u32[]{:S(2)}) copy-start(f32[2,2048]{1,0:T(2,128)} %copy-done.12) | copy-start | bytes 49156
  1008.6 117.4 %copy-start.88 = (f32[2,2048]{1,0:T(2,128)S(1)}, f32[2,2048]{1,0:T(2,128)}, u32[]{:S(2)}) copy-start(f32[2,2048]{1,0:T(2,128)} %copy-done.87) | copy-start | bytes 49156
  1008.6 117.4 %copy-start.11 = (f32[2,2048]{1,0:T(2,128)S(1)}, f32[2,2048]{1,0:T(2,128)}, u32[]{:S(2)}) copy-start(f32[2,2048]{1,0:T(2,128)} %copy-done.9) | copy-start | bytes 49156
  1008.6 117.4 %copy-start.90 = (f32[2,2048]{1,0:T(2,128)S(1)}, f32[2,2048]{1,0:T(2,128)}, u32[]{:S(2)}) copy-start(f32[2,2048]{1,0:T(2,128)} %copy-done.89) | copy-start | bytes 49156
  1126.4 16.8 %copy-start.51 = (s32[4096]{0:T(1024)S(1)}, s32[4096]{0:T(1024)}, u32[]{:S(2)}) copy-start(s32[4096]{0:T(1024)} %broadcast_clamp_fusion.2) | copy-start | bytes 49156
  1130.6 24.1 %copy-start.8 = (pred[2,2048]{1,0:T(4,128)(4,1)S(1)}, pred[2,2048]{1,0:T(4,128)(4,1)}, u32[]{:S(2)}) copy-start(pred[2,2048]{1,0:T(4,128)(4,1)} %copy-done.6) | copy-start | bytes 12292
  1130.6 37.2 %collective-permute-start.14 = (f32[2,512]{1,0:T(2,128)S(1)}, f32[2,512]{1,0:T(2,128)S(1)}, u32[]{:S(2)}, u32[]{:S(2)}) collective-permute-start(f32[2,512]{1,0:T(2,128)S(1)} %bitcast.336), channel_id=1, source_target_pairs={{0,1},{1,2},{2,3},{3,4},{4,5},{5,6},{6,7},{7,8},{8,9},{9,10},{10,1... | collective-permute-start | bytes 12296 | tf_op jit(solution)/shard_map/ppermute | solution.py:15
  1140.1 15.2 %collective-permute-start.15 = (f32[2,64]{1,0:T(2,128)S(1)}, f32[2,64]{1,0:T(2,128)S(1)}, u32[]{:S(2)}, u32[]{:S(2)}) collective-permute-start(f32[2,64]{1,0:T(2,128)S(1)} %bitcast.341), channel_id=1, source_target_pairs={{0,64},{64,128},{128,192},{192,256},{256,320},{320,384},{384,448},... | collective-permute-start | bytes 1544 | tf_op jit(solution)/shard_map/ppermute | solution.py:15
  (80 other events, 358.0 us)
where the time goes:
time: 1190 us; the launch traced here: 1180 us
  blocking collectives  537 us (45%)
  other arithmetic  337 us (28%)
  local copies, waits for them, and re-layouts  210 us (18%)
  starting transfers between devices  67.4 us (6%)
  between operations  21.4 us (2%)
    psum x3, blocking collectives, squares(): return lax.psum(inner(vector, vector), ('region', 'sub'))  320 us
    scatter-add x12, other arithmetic, deposit(): return jnp.zeros((2, count), jnp.float32).at[:, index].add(values)  277 us
    psum x2, blocking collectives, local(): alpha = norm_now / lax.psum(inner(direction, image), ('region', 'sub'))  217 us
    gather x24, local copies, waits for them, and re-layouts, faces(): jnp.take(extended[side], conns[side], axis=1)  156 us
    ppermute x16, starting transfers between devices, shifted(): return lax.ppermute(block, axis, route)  67.4 us
  transfers between devices with their start and end apart: 16, of which 1 were waited for; matrix products, arithmetic and copies ran while one was open for 30% of the time, Pallas kernels for 0%

commit v1 on v0

v1 whole, which is shorter than its diff:
```python
import functools

import jax
import jax.numpy as jnp
from jax import lax
from jax.experimental import pallas as pl
from jax.experimental.pallas import tpu as pltpu
from jax.sharding import PartitionSpec as P

MESH = pl.DeviceIdType.MESH
F32 = jnp.float32
I32 = jnp.int32
ROWS = 16
LANES = 128
E_DEV = ROWS * LANES
NXF = 2176
ROUNDS = 3


def iota(shape, dim):
    return lax.broadcasted_iota(I32, shape, dim)


def inverse(pieces):
    total = None
    for ref, row, columns, first in pieces:
        step = min(256, columns)
        for start in range(0, columns, step):
            face = ref[row : row + 1, start : start + step]
            cell = iota((1, step), 1) + (first + start)
            spot = jnp.where(iota((LANES, step), 0) == (face & 127), 1.0, 0.0).astype(jnp.bfloat16)
            hit = iota((24, step), 0) == (face >> 7)
            low = jnp.where(hit, (cell & 127).astype(F32), 0.0)
            high = jnp.where(hit, ((cell >> 7) + 1).astype(F32), 0.0)
            left = jnp.concatenate([low, high], axis=0).astype(jnp.bfloat16)
            part = lax.dot_general(left, spot, (((1,), (1,)), ((), ())), preferred_element_type=F32)
            total = part if total is None else total + part
    whole = total.astype(I32)
    return (whole[24:] - 1) * 128 + whole[:24]


def lane_gather(rows, lane):
    numbers = lax.GatherDimensionNumbers(
        offset_dims=(),
        collapsed_slice_dims=(1,),
        start_index_map=(1,),
        operand_batching_dims=(0,),
        start_indices_batching_dims=(0,),
    )
    return lax.gather(
        rows, lane[..., None], numbers, (1, 1), mode=lax.GatherScatterMode.PROMISE_IN_BOUNDS
    )


def lookup(rows, index, start=None):
    lane, high = index & 127, index >> 7
    out = start
    for number, row in rows:
        wide = jnp.broadcast_to(row, index.shape)
        found = lane_gather(wide, lane)
        out = jnp.where(high == number, found, jnp.zeros_like(found) if out is None else out)
    return out


def table(ref, count=ROWS, first=0):
    return [(first + h, ref[h : h + 1, :]) for h in range(count)]


def total_row(parts):
    lane = iota((1, LANES), 1)
    row = jnp.zeros((1, LANES), F32)
    for number, part in enumerate(parts):
        flat = jnp.sum(part, axis=0, keepdims=True)
        row = jnp.where(lane == number, jnp.sum(flat, axis=1, keepdims=True), row)
    return row


def pick(row, number):
    return jnp.sum(jnp.where(iota((1, LANES), 1) == number, row, 0.0), axis=1, keepdims=True)


def kernel(
    n_region, n_sub,
    conn_x, conn_y, conn_z, send_y, send_z, perm, storage, sigma_ref, source,
    trace_out, pressure_out, flux_out,
    stage, istage, zlist, itable, tables,
    y_send, y_recv, z_send, z_recv, halo_send_sem, halo_recv_sem,
    a_send, a_recv, b_send, b_recv, a_send_sem, a_recv_sem, b_send_sem, b_recv_sem,
):
    region, sub = lax.axis_index("region"), lax.axis_index("sub")
    n_flat, n_deep = n_sub // 2, 2 * n_region
    core, deep = lax.rem(sub, 2), lax.rem(lax.div(sub, 2), 2)
    flat_me = lax.div(sub, 4) * 2 + core
    deep_me = deep * n_region + region
    sub_up, sub_down = lax.rem(sub + 1, n_sub), lax.rem(sub + n_sub - 1, n_sub)
    region_up, region_down = lax.rem(region + 1, n_region), lax.rem(region + n_region - 1, n_region)

    def flat_peer(offset):
        peer = lax.rem(flat_me + offset, n_flat)
        return (region, lax.div(peer, 2) * 4 + deep * 2 + lax.rem(peer, 2))

    def deep_peer(offset):
        peer = lax.rem(deep_me + offset, n_deep)
        return (lax.rem(peer, n_region), sub - deep * 2 + lax.div(peer, n_region) * 2)

    barrier = pltpu.get_barrier_semaphore()

    def greet(device):
        pl.semaphore_signal(barrier, inc=1, device_id=device, device_id_type=MESH)

    greet((region, sub_up))
    greet((region, sub_down))
    lax.fori_loop(1, n_flat, lambda j, c: (greet(flat_peer(j)), c)[1], 0)
    lax.fori_loop(1, n_deep, lambda j, c: (greet(deep_peer(j)), c)[1], 0)

    def unpack(ref, count, base):
        for i in range(ROWS):
            base[count * i : count * (i + 1), :] = ref(i)
        return [base[pl.ds(k, ROWS, stride=count), :] for k in range(count)]

    def lanes(i):
        return slice(LANES * i, LANES * (i + 1))

    faces_x = unpack(lambda i: conn_x[:, lanes(i)], 2, istage.at[0])
    faces_y = unpack(lambda i: conn_y[:, lanes(i)], 2, istage.at[1])
    faces_z = unpack(lambda i: conn_z[:, lanes(i)], 2, istage.at[2])
    trans = []
    for c in range(2):
        trans.append([2.0 * t for t in unpack(lambda i: perm[c, :, lanes(i)], 3, stage.at[c])])
    store = unpack(lambda i: storage[:, lanes(i)], 2, stage.at[2])
    origin = unpack(lambda i: source[:, lanes(i)], 2, stage.at[3])
    sigma = sigma_ref[...]

    zlist[0:1, :] = jnp.full((1, LANES), -1, I32)
    zlist[0:1, 0:64] = send_z[...]
    itable[0] = inverse([(conn_x, 0, E_DEV, 0)])
    itable[1] = inverse([(conn_x, 1, E_DEV, 0)])
    itable[2] = inverse([(conn_y, 0, E_DEV, 0), (send_y, 0, 512, E_DEV)])
    itable[3] = inverse([(conn_y, 1, E_DEV, 0)])
    itable[4] = inverse([(conn_z, 0, E_DEV, 0), (zlist, 0, LANES, E_DEV)])
    itable[5] = inverse([(conn_z, 1, E_DEV, 0)])

    def at_face(which, face, count=ROWS):
        return lookup(table(itable.at[which], count), face, jnp.full(face.shape, -1, I32))

    def own(which, face):
        return jnp.where(face >= E_DEV, face, at_face(which, face))

    up = [at_face(0, faces_x[1], 17), at_face(2, faces_y[1]), at_face(4, faces_z[1])]
    down = [at_face(1, faces_x[0], 17), own(3, faces_y[0]), own(5, faces_z[0])]
    last_y, last_z = sub == n_sub - 1, region == n_region - 1
    up[1] = jnp.where(jnp.logical_and(up[1] >= E_DEV, last_y), -1, up[1])
    up[2] = jnp.where(jnp.logical_and(up[2] >= E_DEV, last_z), -1, up[2])
    first_y = jnp.logical_and(down[1] >= E_DEV, sub == 0)
    first_z = jnp.logical_and(down[2] >= E_DEV, region == 0)
    lone_x = down[0] < 0
    for i in range(4):
        istage[3, i : i + 1, :] = send_y[:, lanes(i)]
    up_y_cells = at_face(3, istage[3, 0:4, :])
    down_y_cells = itable[2, ROWS : ROWS + 4, :]
    up_z_cells = at_face(5, zlist[0:1, :])
    down_z_cells = itable[4, ROWS : ROWS + 1, :]

    diag = [2.0 * (trans[c][0] + trans[c][1] + trans[c][2]) + store[c] + sigma for c in range(2)]
    determ = diag[0] * diag[1] - sigma * sigma
    solve_00, solve_01, solve_11 = diag[1] / determ, sigma / determ, diag[0] / determ

    def solve(load):
        return (solve_00 * load[0] + solve_01 * load[1], solve_01 * load[0] + solve_11 * load[1])

    def face_load(v):
        return [
            sum(trans[c][d] * (v[c][d][0] + v[c][d][1]) for d in range(3)) for c in range(2)
        ]

    def contributions(v, inner):
        return [
            [[trans[c][d] * (v[c][d][s] - inner[c]) for s in range(2)] for d in range(3)]
            for c in range(2)
        ]

    def copies(step):
        def one(kind, send, recv, device):
            return pltpu.make_async_remote_copy(
                src_ref=send,
                dst_ref=recv,
                send_sem=halo_send_sem.at[step, kind],
                recv_sem=halo_recv_sem.at[step, kind],
                device_id=device,
                device_id_type=MESH,
            )

        return [
            one(0, y_send.at[step, 0], y_recv.at[step, 0], (region, sub_up)),
            one(1, y_send.at[step, 1], y_recv.at[step, 1], (region, sub_down)),
            one(2, z_send.at[step, 0], z_recv.at[step, 0], (region_up, sub)),
            one(3, z_send.at[step, 1], z_recv.at[step, 1], (region_down, sub)),
        ]

    def publish(step, g, wait_first=None):
        for c in range(2):
            for d in range(3):
                for s in range(2):
                    tables[c * 6 + d * 2 + s] = g[c][d][s]
        for c in range(2):
            here = 4 * c
            y_send[step, 0, here : here + 4, :] = lookup(table(tables.at[c * 6 + 3]), up_y_cells)
            y_send[step, 1, here : here + 4, :] = lookup(table(tables.at[c * 6 + 2]), down_y_cells)
            z_send[step, 0, c : c + 1, :] = lookup(table(tables.at[c * 6 + 5]), up_z_cells)
            z_send[step, 1, c : c + 1, :] = lookup(table(tables.at[c * 6 + 4]), down_z_cells)
        if wait_first is not None:
            wait_first()
        for copy in copies(step):
            copy.start()

    def assemble(step, g):
        out = [[[None, None] for _ in range(3)] for _ in range(2)]
        for c in range(2):
            for d in range(3):
                base = c * 6 + d * 2
                out[c][d][1] = g[c][d][1] + lookup(table(tables.at[base]), up[d])
                out[c][d][0] = g[c][d][0] + lookup(table(tables.at[base + 1]), down[d])
        for copy in copies(step):
            copy.wait_recv()
        for c in range(2):
            from_below_y = table(y_recv.at[step, 0, pl.ds(4 * c, 4)], 4, ROWS)
            from_above_y = table(y_recv.at[step, 1, pl.ds(4 * c, 4)], 4, ROWS)
            from_below_z = table(z_recv.at[step, 0, pl.ds(c, 1)], 1, ROWS)
            from_above_z = table(z_recv.at[step, 1, pl.ds(c, 1)], 1, ROWS)
            out[c][1][1] = out[c][1][1] + lookup(from_above_y, up[1])
            out[c][2][1] = out[c][2][1] + lookup(from_above_z, up[2])
            out[c][1][0] = jnp.where(first_y, 0.0, out[c][1][0] + lookup(from_below_y, down[1]))
            out[c][2][0] = jnp.where(first_z, 0.0, out[c][2][0] + lookup(from_below_z, down[2]))
        return out

    def inner(u, v):
        total = sum(u[c][d][1] * v[c][d][1] for c in range(2) for d in range(3))
        edge = sum(u[c][0][0] * v[c][0][0] for c in range(2))
        return total + jnp.where(lone_x, edge, 0.0)

    def energy(v, load, solved):
        total = sum(
            trans[c][d] * (v[c][d][0] * v[c][d][0] + v[c][d][1] * v[c][d][1])
            for c in range(2)
            for d in range(3)
        )
        return total - (load[0] * solved[0] + load[1] * solved[1])

    def scatter(send, recv, send_sem, recv_sem, peer, count, row):
        send[0:1, :] = row
        recv[count - 1 : count, :] = row

        def one(j, carry):
            pltpu.make_async_remote_copy(
                src_ref=send.at[pl.ds(0, 1)],
                dst_ref=recv.at[pl.ds(j - 1, 1)],
                send_sem=send_sem,
                recv_sem=recv_sem,
                device_id=peer(j),
                device_id_type=MESH,
            ).start()
            return carry

        lax.fori_loop(1, count, one, 0)

    def drain(buffer, sem, count):
        rows = buffer.at[pl.ds(0, count - 1)]
        pltpu.make_async_copy(rows, rows, sem).wait()

    def flat_start(k, row):
        scatter(a_send.at[k], a_recv.at[k], a_send_sem.at[k], a_recv_sem.at[k], flat_peer, n_flat, row)

    def flat_done(k):
        drain(a_recv.at[k], a_recv_sem.at[k], n_flat)
        return jnp.sum(a_recv[k], axis=0, keepdims=True)

    def deep_start(k, row):
        scatter(b_send.at[k], b_recv.at[k], b_send_sem.at[k], b_recv_sem.at[k], deep_peer, n_deep, row)

    def deep_done(k):
        drain(b_recv.at[k], b_recv_sem.at[k], n_deep)
        return jnp.sum(b_recv[k], axis=0, keepdims=True)

    base = solve(origin)
    g = [[[trans[c][d] * base[c]] * 2 for d in range(3)] for c in range(2)]
    greetings = 2 + (n_flat - 1) + (n_deep - 1)
    publish(0, g, lambda: pl.semaphore_wait(barrier, greetings))
    b = assemble(0, g)

    load = face_load(b)
    solved = solve(load)
    g = contributions(b, solved)
    publish(1, g)
    flat_start(0, total_row([inner(b, b), energy(b, load, solved)]))
    w = assemble(1, g)

    g = contributions(w, solve(face_load(w)))
    publish(2, g)
    deep_start(0, flat_done(0))
    ww = assemble(2, g)

    first = deep_done(0)
    norm_0 = pick(first, 0)
    alpha_0 = norm_0 / pick(first, 1)

    def blend(u, factor, v):
        return [
            [[u[c][d][s] - factor * v[c][d][s] for s in range(2)] for d in range(3)]
            for c in range(2)
        ]

    r = blend(b, alpha_0, w)
    s = blend(w, alpha_0, ww)
    load = face_load(s)
    flat_start(1, total_row([inner(r, r), inner(r, s), inner(s, s), energy(s, load, solve(load))]))
    deep_start(1, flat_done(1))
    sums = deep_done(1)
    rr, rs, ss, sas = (pick(sums, k) for k in range(4))

    beta_0 = rr / norm_0
    alpha_1 = rr / (rs - beta_0 * rr / alpha_0)
    ws = -(rr / alpha_0 + rs) / alpha_0
    norm_2 = -alpha_1 * (rs - alpha_1 * ss - alpha_1 * beta_0 * ws)
    beta_1 = norm_2 / rr
    ratio = alpha_1 * beta_0 / alpha_0
    along = ss - alpha_1 * sas - ratio * (ws - ss)
    energy_2 = -norm_2 / alpha_1 * (1.0 + ratio) - alpha_1 * along
    alpha_2 = norm_2 / (energy_2 - beta_1 * norm_2 / alpha_1)
    on_b = alpha_0 + alpha_1 * beta_0 + alpha_2 * beta_1 * beta_0
    on_r = alpha_1 + alpha_2 * (1.0 + beta_1)
    on_s = -alpha_2 * alpha_1
    on_w = -alpha_2 * alpha_1 * beta_0
    trace = [
        [
            [
                on_b * b[c][d][k] + on_r * r[c][d][k] + on_s * s[c][d][k] + on_w * w[c][d][k]
                for k in range(2)
            ]
            for d in range(3)
        ]
        for c in range(2)
    ]

    load = face_load(trace)
    pressure = solve([origin[c] + load[c] for c in range(2)])
    for c in range(2):
        stage[0, pl.ds(c, ROWS, stride=2), :] = pressure[c]
    for i in range(ROWS):
        pressure_out[:, lanes(i)] = stage[0, 2 * i : 2 * i + 2, :]
    for c in range(2):
        for d in range(3):
            for k in range(2):
                flux = trans[c][d] * (pressure[c] - trace[c][d][k])
                stage[1 + c, pl.ds(2 * d + k, ROWS, stride=8), :] = flux
        for i in range(ROWS):
            flux_out[c, :, lanes(i)] = stage[1 + c, 8 * i : 8 * i + 6, :]

    for c in range(2):
        for d in range(3):
            for k in range(2):
                tables[c * 6 + d * 2 + k] = trace[c][d][k]
        by_x = lookup(table(tables.at[c * 6 + 1]), itable[1])
        by_x = jnp.where(itable[1] < 0, lookup(table(tables.at[c * 6]), itable[0]), by_x)
        by_y = lookup(table(tables.at[c * 6 + 3]), itable[3, 0:ROWS, :])
        by_z = lookup(table(tables.at[c * 6 + 5]), itable[5, 0:ROWS, :])
        stage[3, pl.ds(c, 17, stride=2), :] = by_x[0:17]
        stage[3, pl.ds(34 + c, ROWS, stride=2), :] = by_y
        stage[3, pl.ds(66 + c, ROWS, stride=2), :] = by_z
    for i in range(49):
        trace_out[:, lanes(i)] = stage[3, 2 * i : 2 * i + 2, :]

    for step in range(ROUNDS):
        for copy in copies(step):
            copy.wait_send()
    for k in range(2):
        drain(a_recv.at[k], a_send_sem.at[k], n_flat)
        drain(b_recv.at[k], b_send_sem.at[k], n_deep)


def solution(mesh):
    n_region, n_sub = mesh.shape["region"], mesh.shape["sub"]
    n_flat, n_deep = n_sub // 2, 2 * n_region

    def local(conn_x, conn_y, conn_z, send_y, send_z, perm, storage, sigma, source):
        vmem = pl.BlockSpec(memory_space=pltpu.VMEM)
        dma = pltpu.SemaphoreType.DMA
        return pl.pallas_call(
            functools.partial(kernel, n_region, n_sub),
            out_shape=(
                jax.ShapeDtypeStruct((2, NXF + 2 * E_DEV), F32),
                jax.ShapeDtypeStruct((2, E_DEV), F32),
                jax.ShapeDtypeStruct((2, 6, E_DEV), F32),
            ),
            in_specs=[vmem] * 9,
            out_specs=(vmem,) * 3,
            scratch_shapes=[
                pltpu.VMEM((4, LANES + 8, LANES), F32),
                pltpu.VMEM((4, 40, LANES), I32),
                pltpu.VMEM((8, LANES), I32),
                pltpu.VMEM((6, 24, LANES), I32),
                pltpu.VMEM((12, ROWS, LANES), F32),
                pltpu.VMEM((ROUNDS, 2, 8, LANES), F32),
                pltpu.VMEM((ROUNDS, 2, 8, LANES), F32),
                pltpu.VMEM((ROUNDS, 2, 2, LANES), F32),
                pltpu.VMEM((ROUNDS, 2, 2, LANES), F32),
                dma((ROUNDS, 4)),
                dma((ROUNDS, 4)),
                pltpu.VMEM((2, 8, LANES), F32),
                pltpu.VMEM((2, n_flat, LANES), F32),
                pltpu.VMEM((2, 8, LANES), F32),
                pltpu.VMEM((2, n_deep, LANES), F32),
                dma((2,)),
                dma((2,)),
                dma((2,)),
                dma((2,)),
            ],
            compiler_params=pltpu.CompilerParams(
                collective_id=0, has_side_effects=True, vmem_limit_bytes=32 * 1024 * 1024
            ),
        )(
            conn_x, conn_y, conn_z, send_y.reshape(1, 512), send_z.reshape(1, 64),
            perm, storage, sigma.reshape(ROWS, LANES), source,
        )

    both = ("region", "sub")
    return jax.shard_map(
        local,
        mesh=mesh,
        in_specs=(
            P(None, both), P(None, both), P(None, both), P(both), P(both),
            P(None, None, both), P(None, both), P(both), P(None, both),
        ),
        out_specs=(P(None, both), P(None, both), P(None, None, both)),
        check_vma=False,
    )
```

time: 1190 us -> 61.5 us (0.05)
  blocking collectives: 537 us -> 0 us
  other arithmetic: 337 us -> 0 us
  local copies, waits for them, and re-layouts: 210 us -> 2.86 us
  starting transfers between devices: 67.4 us -> 0 us
  Pallas kernels: 0 us -> 57.7 us
  between operations: 21.4 us -> 0.77 us
    psum x5 -> x0, blocking collectives: 537 us -> none  [the longest x3 320 us: squares(): return lax.psum(inner(vector, vector), ('region', 'sub'))]
    scatter-add x20 -> x0, other arithmetic: 302 us -> none  [the longest x12 277 us: deposit(): return jnp.zeros((2, count), jnp.float32).at[:, index].add(values)]
    gather x38 -> x0, local copies, waits for them, and re-layouts: 166 us -> none  [the longest x24 156 us: faces(): jnp.take(extended[side], conns[side], axis=1)]
    ppermute x16 -> x0, starting transfers between devices: 67.4 us -> none  [shifted(): return lax.ppermute(block, axis, route)]
    pallas_call x0 -> x1, Pallas kernels: none -> 57.7 us  [local(): pl.pallas_call(functools.partial(kernel, n_region, n_sub), out_shape=(jax...]
    mul x9 -> x0, local copies, waits for them, and re-layouts: 16.1 us -> none  [operate(): trans[:, side][:, None] * (values[side] - solved[:, None])]
    reduce_sum x16 -> x0, other arithmetic: 15.4 us -> none  [the longest x5 6.32 us: inner(): jnp.sum(first[0] * second[0]) + jnp.sum(first[1] * second[1])]
  transfers between devices with their start and end apart: 16 -> 0, of which waited for: 1 -> 0; matrix products, arithmetic and copies ran while one was open for 30% -> 0% of each run, Pallas kernels for 0% -> 0%
where the time goes in v1:
time: 61.5 us; the launch traced here: 61.3 us
  Pallas kernels  57.7 us (94%)
  local copies, waits for them, and re-layouts  2.86 us (5%)
  between operations  0.77 us (1%)
    pallas_call x1, Pallas kernels, local(): pl.pallas_call(functools.partial(kernel, n_region, n_sub), out_shape=(jax...  57.7 us
    unnamed x19, local copies, waits for them, and re-layouts  2.14 us

profile of v1, /device:TPU:1, one launch (start us, length us, event | category | flops | bytes accessed | tf_op | source)
XLA Modules:
  0.0 61.3 jit_solution(10825466583640982086)
XLA Ops:
  0.6 0.0 copy-start
  0.6 0.0 copy-start.1
  0.7 0.0 copy-start.2
  0.7 0.0 copy-start.3
  0.7 0.0 copy-start.4
  0.7 0.0 copy-start.5
  0.7 0.0 copy-start.6
  0.7 0.0 copy-start.7
  0.7 0.9 %copy.12.perm = f32[2,3,2048]{2,1,0:T(4,128)S(1)} copy(f32[2,3,2048]{2,0,1:T(2,128)} %param.14) | data formatting | bytes 98304 | tf_op args[5]
  1.6 0.0 copy-done
  1.6 0.0 copy-done.1
  1.6 0.0 copy-done.2
  1.6 0.0 copy-done.3
  1.6 0.0 copy-done.4
  1.6 0.0 copy-done.5
  1.7 0.0 copy-done.6
  1.7 0.0 copy-done.7
  1.7 57.7 %shard_map.112 = (f32[2,6272]{1,0:T(2,128)S(1)}, f32[2,2048]{1,0:T(2,128)S(1)}, f32[2,6,2048]{2,1,0:T(8,128)S(1)}) custom-call(s32[2,2048]{1,0:T(2,128)S(1)} %copy-done, s32[2,2048]{1,0:T(2,128)S(1)} %copy-done.1, s32[2,2048]{1,0:T(2,128)S(1)} %copy-done.2, s32[1,512]{1,0:T(1,128)S(1)} %bitcast.4, s32[1,64]{1,0:T(1,128)S(1)} %bitcast.5, ...), custom_call_target="tpu_custom_call" | custom-call | tf_op jit(solution)/shard_map/pallas_call | solution.py:387
  59.4 0.7 %copy.13 = f32[2,6,2048]{2,0,1:T(2,128)} copy(f32[2,6,2048]{2,1,0:T(8,128)S(1)} %get-tuple-element.5) | data formatting | bytes 196608 | tf_op jit(solution)/shard_map/pallas_call | solution.py:387
  60.1 0.6 %copy.16 = f32[2,6272]{1,0:T(2,128)} copy(f32[2,6272]{1,0:T(2,128)S(1)} %get-tuple-element.9) | data formatting | bytes 100352
  60.7 0.6 copy.17
Async XLA Ops:
  0.6 1.0 %copy-start = (s32[2,2048]{1,0:T(2,128)S(1)}, s32[2,2048]{1,0:T(2,128)}, u32[]{:S(2)}) copy-start(s32[2,2048]{1,0:T(2,128)} %conn_x.1) | copy-start | bytes 49156
  0.6 1.0 %copy-start.1 = (s32[2,2048]{1,0:T(2,128)S(1)}, s32[2,2048]{1,0:T(2,128)}, u32[]{:S(2)}) copy-start(s32[2,2048]{1,0:T(2,128)} %conn_y.1) | copy-start | bytes 49156
  0.7 1.0 %copy-start.2 = (s32[2,2048]{1,0:T(2,128)S(1)}, s32[2,2048]{1,0:T(2,128)}, u32[]{:S(2)}) copy-start(s32[2,2048]{1,0:T(2,128)} %conn_z.1) | copy-start | bytes 49156
  0.7 1.0 %copy-start.3 = (f32[2,2048]{1,0:T(2,128)S(1)}, f32[2,2048]{1,0:T(2,128)}, u32[]{:S(2)}) copy-start(f32[2,2048]{1,0:T(2,128)} %storage.1) | copy-start | bytes 49156
  0.7 1.0 %copy-start.4 = (f32[2,2048]{1,0:T(2,128)S(1)}, f32[2,2048]{1,0:T(2,128)}, u32[]{:S(2)}) copy-start(f32[2,2048]{1,0:T(2,128)} %source.1) | copy-start | bytes 49156
  0.7 1.0 %copy-start.5 = (f32[2048]{0:T(1024)S(1)}, f32[2048]{0:T(1024)}, u32[]{:S(2)}) copy-start(f32[2048]{0:T(1024)} %param.16) | copy-start | bytes 24580
  0.7 1.0 %copy-start.6 = (s32[512]{0:T(512)S(1)}, s32[512]{0:T(512)}, u32[]{:S(2)}) copy-start(s32[512]{0:T(512)} %param.12) | copy-start | bytes 6148
  0.7 1.0 %copy-start.7 = (s32[64]{0:T(128)S(1)}, s32[64]{0:T(128)}, u32[]{:S(2)}) copy-start(s32[64]{0:T(128)} %param.13) | copy-start | bytes 772

commit v2 on v1

--- a/solution.py
+++ b/solution.py
@@ -23,16 +23,19 @@
 
 def inverse(pieces):
     total = None
-    for ref, row, columns, first in pieces:
-        step = min(256, columns)
-        for start in range(0, columns, step):
-            face = ref[row : row + 1, start : start + step]
-            cell = iota((1, step), 1) + (first + start)
-            spot = jnp.where(iota((LANES, step), 0) == (face & 127), 1.0, 0.0).astype(jnp.bfloat16)
-            hit = iota((24, step), 0) == (face >> 7)
-            low = jnp.where(hit, (cell & 127).astype(F32), 0.0)
-            high = jnp.where(hit, ((cell >> 7) + 1).astype(F32), 0.0)
-            left = jnp.concatenate([low, high], axis=0).astype(jnp.bfloat16)
+    for ref, row, stride, count, first in pieces:
+        for start in range(0, count, 2):
+            spots, hits = [], []
+            for i in range(start, min(start + 2, count)):
+                face = ref[row + stride * i : row + stride * i + 1, :]
+                cell = iota((1, LANES), 1) + (first + LANES * i)
+                spots.append(jnp.where(iota((LANES, LANES), 0) == (face & 127), 1.0, 0.0))
+                hit = iota((24, LANES), 0) == (face >> 7)
+                low = jnp.where(hit, (cell & 127).astype(F32), 0.0)
+                high = jnp.where(hit, ((cell >> 7) + 1).astype(F32), 0.0)
+                hits.append(jnp.concatenate([low, high], axis=0))
+            left = jnp.concatenate(hits, axis=1).astype(jnp.bfloat16)
+            spot = jnp.concatenate(spots, axis=1).astype(jnp.bfloat16)
             part = lax.dot_general(left, spot, (((1,), (1,)), ((), ())), preferred_element_type=F32)
             total = part if total is None else total + part
     whole = total.astype(I32)
@@ -83,7 +86,7 @@
     n_region, n_sub,
     conn_x, conn_y, conn_z, send_y, send_z, perm, storage, sigma_ref, source,
     trace_out, pressure_out, flux_out,
-    stage, istage, zlist, itable, tables,
+    zlist, itable, tables, vtables, by_face,
     y_send, y_recv, z_send, z_recv, halo_send_sem, halo_recv_sem,
     a_send, a_recv, b_send, b_recv, a_send_sem, a_recv_sem, b_send_sem, b_recv_sem,
 ):
@@ -110,56 +113,17 @@
 
     greet((region, sub_up))
     greet((region, sub_down))
-    lax.fori_loop(1, n_flat, lambda j, c: (greet(flat_peer(j)), c)[1], 0)
-    lax.fori_loop(1, n_deep, lambda j, c: (greet(deep_peer(j)), c)[1], 0)
-
-    def unpack(ref, count, base):
-        for i in range(ROWS):
-            base[count * i : count * (i + 1), :] = ref(i)
-        return [base[pl.ds(k, ROWS, stride=count), :] for k in range(count)]
-
-    def lanes(i):
-        return slice(LANES * i, LANES * (i + 1))
-
-    faces_x = unpack(lambda i: conn_x[:, lanes(i)], 2, istage.at[0])
-    faces_y = unpack(lambda i: conn_y[:, lanes(i)], 2, istage.at[1])
-    faces_z = unpack(lambda i: conn_z[:, lanes(i)], 2, istage.at[2])
-    trans = []
-    for c in range(2):
-        trans.append([2.0 * t for t in unpack(lambda i: perm[c, :, lanes(i)], 3, stage.at[c])])
-    store = unpack(lambda i: storage[:, lanes(i)], 2, stage.at[2])
-    origin = unpack(lambda i: source[:, lanes(i)], 2, stage.at[3])
-    sigma = sigma_ref[...]
-
-    zlist[0:1, :] = jnp.full((1, LANES), -1, I32)
-    zlist[0:1, 0:64] = send_z[...]
-    itable[0] = inverse([(conn_x, 0, E_DEV, 0)])
-    itable[1] = inverse([(conn_x, 1, E_DEV, 0)])
-    itable[2] = inverse([(conn_y, 0, E_DEV, 0), (send_y, 0, 512, E_DEV)])
-    itable[3] = inverse([(conn_y, 1, E_DEV, 0)])
-    itable[4] = inverse([(conn_z, 0, E_DEV, 0), (zlist, 0, LANES, E_DEV)])
-    itable[5] = inverse([(conn_z, 1, E_DEV, 0)])
-
-    def at_face(which, face, count=ROWS):
-        return lookup(table(itable.at[which], count), face, jnp.full(face.shape, -1, I32))
-
-    def own(which, face):
-        return jnp.where(face >= E_DEV, face, at_face(which, face))
-
-    up = [at_face(0, faces_x[1], 17), at_face(2, faces_y[1]), at_face(4, faces_z[1])]
-    down = [at_face(1, faces_x[0], 17), own(3, faces_y[0]), own(5, faces_z[0])]
-    last_y, last_z = sub == n_sub - 1, region == n_region - 1
-    up[1] = jnp.where(jnp.logical_and(up[1] >= E_DEV, last_y), -1, up[1])
-    up[2] = jnp.where(jnp.logical_and(up[2] >= E_DEV, last_z), -1, up[2])
-    first_y = jnp.logical_and(down[1] >= E_DEV, sub == 0)
-    first_z = jnp.logical_and(down[2] >= E_DEV, region == 0)
-    lone_x = down[0] < 0
-    for i in range(4):
-        istage[3, i : i + 1, :] = send_y[:, lanes(i)]
-    up_y_cells = at_face(3, istage[3, 0:4, :])
-    down_y_cells = itable[2, ROWS : ROWS + 4, :]
-    up_z_cells = at_face(5, zlist[0:1, :])
-    down_z_cells = itable[4, ROWS : ROWS + 1, :]
+    for j in range(1, n_flat):
+        greet(flat_peer(j))
+    for j in range(1, n_deep):
+        greet(deep_peer(j))
+
+    def pair(ref, first=0):
+        return [ref[pl.ds(first + k, ROWS, stride=2), :] for k in range(2)]
+
+    by_side = [pair(perm, 32 * d) for d in range(3)]
+    trans = [[2.0 * by_side[d][c] for d in range(3)] for c in range(2)]
+    store, origin, sigma = pair(storage), pair(source), sigma_ref[...]
 
     diag = [2.0 * (trans[c][0] + trans[c][1] + trans[c][2]) + store[c] + sigma for c in range(2)]
     determ = diag[0] * diag[1] - sigma * sigma
@@ -178,6 +142,26 @@
             [[trans[c][d] * (v[c][d][s] - inner[c]) for s in range(2)] for d in range(3)]
             for c in range(2)
         ]
+
+    base = solve(origin)
+    rhs_g = [[[trans[c][d] * base[c]] * 2 for d in range(3)] for c in range(2)]
+
+    def at_face(which, face, count=ROWS):
+        return lookup(table(itable.at[which], count), face, jnp.full(face.shape, -1, I32))
+
+    def own(which, face):
+        return jnp.where(face >= E_DEV, face, at_face(which, face))
+
+    zlist[0:1, :] = jnp.full((1, LANES), -1, I32)
+    zlist[0:1, 0:64] = send_z[...]
+    itable[2] = inverse([(conn_y, 0, 2, ROWS, 0), (send_y, 0, 1, 4, E_DEV)])
+    itable[3] = inverse([(conn_y, 1, 2, ROWS, 0)])
+    itable[4] = inverse([(conn_z, 0, 2, ROWS, 0), (zlist, 0, 1, 1, E_DEV)])
+    itable[5] = inverse([(conn_z, 1, 2, ROWS, 0)])
+    up_y_cells = at_face(3, send_y[...])
+    down_y_cells = itable[2, ROWS : ROWS + 4, :]
+    up_z_cells = at_face(5, zlist[0:1, :])
+    down_z_cells = itable[4, ROWS : ROWS + 1, :]
 
     def copies(step):
         def one(kind, send, recv, device):
@@ -198,8 +182,8 @@
         ]
 
     def publish(step, g, wait_first=None):
-        for c in range(2):
-            for d in range(3):
+        for d in (1, 2, 0):
+            for c in range(2):
                 for s in range(2):
                     tables[c * 6 + d * 2 + s] = g[c][d][s]
         for c in range(2):
@@ -213,13 +197,28 @@
         for copy in copies(step):
             copy.start()
 
+    greetings = 2 + (n_flat - 1) + (n_deep - 1)
+    publish(0, rhs_g, lambda: pl.semaphore_wait(barrier, greetings))
+
+    itable[0] = inverse([(conn_x, 0, 2, ROWS, 0)])
+    itable[1] = inverse([(conn_x, 1, 2, ROWS, 0)])
+    faces_x, faces_y, faces_z = pair(conn_x), pair(conn_y), pair(conn_z)
+    up = [at_face(0, faces_x[1], 17), at_face(2, faces_y[1]), at_face(4, faces_z[1])]
+    down = [at_face(1, faces_x[0], 17), own(3, faces_y[0]), own(5, faces_z[0])]
+    last_y, last_z = sub == n_sub - 1, region == n_region - 1
+    up[1] = jnp.where(jnp.logical_and(up[1] >= E_DEV, last_y), -1, up[1])
+    up[2] = jnp.where(jnp.logical_and(up[2] >= E_DEV, last_z), -1, up[2])
+    first_y = jnp.logical_and(down[1] >= E_DEV, sub == 0)
+    first_z = jnp.logical_and(down[2] >= E_DEV, region == 0)
+    lone_x = down[0] < 0
+
     def assemble(step, g):
         out = [[[None, None] for _ in range(3)] for _ in range(2)]
         for c in range(2):
             for d in range(3):
-                base = c * 6 + d * 2
-                out[c][d][1] = g[c][d][1] + lookup(table(tables.at[base]), up[d])
-                out[c][d][0] = g[c][d][0] + lookup(table(tables.at[base + 1]), down[d])
+                at = c * 6 + d * 2
+                out[c][d][1] = g[c][d][1] + lookup(table(tables.at[at]), up[d])
+                out[c][d][0] = g[c][d][0] + lookup(table(tables.at[at + 1]), down[d])
         for copy in copies(step):
             copy.wait_recv()
         for c in range(2):
@@ -233,6 +232,17 @@
             out[c][2][0] = jnp.where(first_z, 0.0, out[c][2][0] + lookup(from_below_z, down[2]))
         return out
 
+    def by_faces(number, v):
+        for c in range(2):
+            parts = (v[c][0][0], v[c][0][1], v[c][1][1], v[c][2][1])
+            for k, part in enumerate(parts):
+                vtables[number, c * 4 + k] = part
+            x_low, x_up, y_up, z_up = (table(vtables.at[number, c * 4 + k]) for k in range(4))
+            by_x = jnp.where(itable[1] < 0, lookup(x_low, itable[0]), lookup(x_up, itable[1]))
+            by_face[number, pl.ds(c, 17, stride=2), :] = by_x[0:17]
+            by_face[number, pl.ds(34 + c, ROWS, stride=2), :] = lookup(y_up, itable[3, 0:ROWS, :])
+            by_face[number, pl.ds(66 + c, ROWS, stride=2), :] = lookup(z_up, itable[5, 0:ROWS, :])
+
     def inner(u, v):
         total = sum(u[c][d][1] * v[c][d][1] for c in range(2) for d in range(3))
         edge = sum(u[c][0][0] * v[c][0][0] for c in range(2))
@@ -249,8 +259,7 @@
     def scatter(send, recv, send_sem, recv_sem, peer, count, row):
         send[0:1, :] = row
         recv[count - 1 : count, :] = row
-
-        def one(j, carry):
+        for j in range(1, count):
             pltpu.make_async_remote_copy(
                 src_ref=send.at[pl.ds(0, 1)],
                 dst_ref=recv.at[pl.ds(j - 1, 1)],
@@ -259,9 +268,6 @@
                 device_id=peer(j),
                 device_id_type=MESH,
             ).start()
-            return carry
-
-        lax.fori_loop(1, count, one, 0)
 
     def drain(buffer, sem, count):
         rows = buffer.at[pl.ds(0, count - 1)]
@@ -281,23 +287,23 @@
         drain(b_recv.at[k], b_recv_sem.at[k], n_deep)
         return jnp.sum(b_recv[k], axis=0, keepdims=True)
 
-    base = solve(origin)
-    g = [[[trans[c][d] * base[c]] * 2 for d in range(3)] for c in range(2)]
-    greetings = 2 + (n_flat - 1) + (n_deep - 1)
-    publish(0, g, lambda: pl.semaphore_wait(barrier, greetings))
-    b = assemble(0, g)
-
-    load = face_load(b)
-    solved = solve(load)
-    g = contributions(b, solved)
-    publish(1, g)
-    flat_start(0, total_row([inner(b, b), energy(b, load, solved)]))
-    w = assemble(1, g)
-
-    g = contributions(w, solve(face_load(w)))
-    publish(2, g)
+    b = assemble(0, rhs_g)
+
+    load_b = face_load(b)
+    inside_b = solve(load_b)
+    g_b = contributions(b, inside_b)
+    publish(1, g_b)
+    flat_start(0, total_row([inner(b, b), energy(b, load_b, inside_b)]))
+    by_faces(0, b)
+    w = assemble(1, g_b)
+
+    load_w = face_load(w)
+    inside_w = solve(load_w)
+    g_w = contributions(w, inside_w)
+    publish(2, g_w)
     deep_start(0, flat_done(0))
-    ww = assemble(2, g)
+    by_faces(1, w)
+    ww = assemble(2, g_w)
 
     first = deep_done(0)
     norm_0 = pick(first, 0)
@@ -313,7 +319,17 @@
     s = blend(w, alpha_0, ww)
     load = face_load(s)
     flat_start(1, total_row([inner(r, r), inner(r, s), inner(s, s), energy(s, load, solve(load))]))
+    load_ww = face_load(ww)
+    inside_ww = solve(load_ww)
+    g_ww = contributions(ww, inside_ww)
+    by_faces(2, ww)
     deep_start(1, flat_done(1))
+    for step in range(ROUNDS):
+        for copy in copies(step):
+            copy.wait_send()
+    drain(a_recv.at[0], a_send_sem.at[0], n_flat)
+    drain(b_recv.at[0], b_send_sem.at[0], n_deep)
+    drain(a_recv.at[1], a_send_sem.at[1], n_flat)
     sums = deep_done(1)
     rr, rs, ss, sas = (pick(sums, k) for k in range(4))
 
@@ -326,55 +342,28 @@
     along = ss - alpha_1 * sas - ratio * (ws - ss)
     energy_2 = -norm_2 / alpha_1 * (1.0 + ratio) - alpha_1 * along
     alpha_2 = norm_2 / (energy_2 - beta_1 * norm_2 / alpha_1)
-    on_b = alpha_0 + alpha_1 * beta_0 + alpha_2 * beta_1 * beta_0
     on_r = alpha_1 + alpha_2 * (1.0 + beta_1)
     on_s = -alpha_2 * alpha_1
-    on_w = -alpha_2 * alpha_1 * beta_0
-    trace = [
-        [
-            [
-                on_b * b[c][d][k] + on_r * r[c][d][k] + on_s * s[c][d][k] + on_w * w[c][d][k]
-                for k in range(2)
-            ]
-            for d in range(3)
-        ]
-        for c in range(2)
-    ]
-
-    load = face_load(trace)
-    pressure = solve([origin[c] + load[c] for c in range(2)])
+    on_b = alpha_0 + alpha_1 * beta_0 + alpha_2 * beta_1 * beta_0 + on_r
+    on_w = -alpha_2 * alpha_1 * beta_0 - alpha_0 * on_r + on_s
+    on_ww = -alpha_0 * on_s
+
     for c in range(2):
-        stage[0, pl.ds(c, ROWS, stride=2), :] = pressure[c]
-    for i in range(ROWS):
-        pressure_out[:, lanes(i)] = stage[0, 2 * i : 2 * i + 2, :]
-    for c in range(2):
+        pressure_out[pl.ds(c, ROWS, stride=2), :] = base[c] + (
+            on_b * inside_b[c] + on_w * inside_w[c] + on_ww * inside_ww[c]
+        )
         for d in range(3):
             for k in range(2):
-                flux = trans[c][d] * (pressure[c] - trace[c][d][k])
-                stage[1 + c, pl.ds(2 * d + k, ROWS, stride=8), :] = flux
-        for i in range(ROWS):
-            flux_out[c, :, lanes(i)] = stage[1 + c, 8 * i : 8 * i + 6, :]
-
-    for c in range(2):
-        for d in range(3):
-            for k in range(2):
-                tables[c * 6 + d * 2 + k] = trace[c][d][k]
-        by_x = lookup(table(tables.at[c * 6 + 1]), itable[1])
-        by_x = jnp.where(itable[1] < 0, lookup(table(tables.at[c * 6]), itable[0]), by_x)
-        by_y = lookup(table(tables.at[c * 6 + 3]), itable[3, 0:ROWS, :])
-        by_z = lookup(table(tables.at[c * 6 + 5]), itable[5, 0:ROWS, :])
-        stage[3, pl.ds(c, 17, stride=2), :] = by_x[0:17]
-        stage[3, pl.ds(34 + c, ROWS, stride=2), :] = by_y
-        stage[3, pl.ds(66 + c, ROWS, stride=2), :] = by_z
+                flux = on_b * g_b[c][d][k] + on_w * g_w[c][d][k] + on_ww * g_ww[c][d][k]
+                flux_out[pl.ds(32 * (2 * d + k) + c, ROWS, stride=2), :] = rhs_g[c][d][k] - flux
+    by_face[0] = on_b * by_face[0] + on_w * by_face[1] + on_ww * by_face[2]
     for i in range(49):
-        trace_out[:, lanes(i)] = stage[3, 2 * i : 2 * i + 2, :]
-
-    for step in range(ROUNDS):
-        for copy in copies(step):
-            copy.wait_send()
-    for k in range(2):
-        drain(a_recv.at[k], a_send_sem.at[k], n_flat)
-        drain(b_recv.at[k], b_send_sem.at[k], n_deep)
+        trace_out[:, LANES * i : LANES * (i + 1)] = by_face[0, 2 * i : 2 * i + 2, :]
+    drain(b_recv.at[1], b_send_sem.at[1], n_deep)
+
+
+def pair_rows(array):
+    return array.reshape(2, ROWS, LANES).transpose(1, 0, 2).reshape(2 * ROWS, LANES)
 
 
 def solution(mesh):
@@ -384,21 +373,22 @@
     def local(conn_x, conn_y, conn_z, send_y, send_z, perm, storage, sigma, source):
         vmem = pl.BlockSpec(memory_space=pltpu.VMEM)
         dma = pltpu.SemaphoreType.DMA
-        return pl.pallas_call(
+        sides = perm.transpose(1, 0, 2).reshape(3, 2, ROWS, LANES).transpose(0, 2, 1, 3)
+        trace, pressure, flux = pl.pallas_call(
             functools.partial(kernel, n_region, n_sub),
             out_shape=(
                 jax.ShapeDtypeStruct((2, NXF + 2 * E_DEV), F32),
-                jax.ShapeDtypeStruct((2, E_DEV), F32),
-                jax.ShapeDtypeStruct((2, 6, E_DEV), F32),
+                jax.ShapeDtypeStruct((2 * ROWS, LANES), F32),
+                jax.ShapeDtypeStruct((12 * ROWS, LANES), F32),
             ),
             in_specs=[vmem] * 9,
             out_specs=(vmem,) * 3,
             scratch_shapes=[
-                pltpu.VMEM((4, LANES + 8, LANES), F32),
-                pltpu.VMEM((4, 40, LANES), I32),
                 pltpu.VMEM((8, LANES), I32),
                 pltpu.VMEM((6, 24, LANES), I32),
                 pltpu.VMEM((12, ROWS, LANES), F32),
+                pltpu.VMEM((3, 8, ROWS, LANES), F32),
+                pltpu.VMEM((3, 104, LANES), F32),
                 pltpu.VMEM((ROUNDS, 2, 8, LANES), F32),
                 pltpu.VMEM((ROUNDS, 2, 8, LANES), F32),
                 pltpu.VMEM((ROUNDS, 2, 2, LANES), F32),
@@ -418,9 +408,14 @@
                 collective_id=0, has_side_effects=True, vmem_limit_bytes=32 * 1024 * 1024
             ),
         )(
-            conn_x, conn_y, conn_z, send_y.reshape(1, 512), send_z.reshape(1, 64),
-            perm, storage, sigma.reshape(ROWS, LANES), source,
+            pair_rows(conn_x), pair_rows(conn_y), pair_rows(conn_z),
+            send_y.reshape(4, LANES), send_z.reshape(1, 64),
+            sides.reshape(6 * ROWS, LANES), pair_rows(storage), sigma.reshape(ROWS, LANES),
+            pair_rows(source),
         )
+        pressure = pressure.reshape(ROWS, 2, LANES).transpose(1, 0, 2).reshape(2, E_DEV)
+        flux = flux.reshape(6, ROWS, 2, LANES).transpose(2, 0, 1, 3).reshape(2, 6, E_DEV)
+        return trace, pressure, flux
 
     both = ("region", "sub")
     return jax.shard_map(

time: 61.5 us -> 65.7 us (1.068)
  local copies, waits for them, and re-layouts: 2.86 us -> 7.62 us
  Pallas kernels: 57.7 us -> 56.8 us
    unnamed x19 -> x21, local copies, waits for them, and re-layouts: 2.14 us -> 7.62 us
    pallas_call x1, Pallas kernels: 57.7 us -> 56.8 us  [local(): pl.pallas_call(functools.partial(kernel, n_region, n_sub), out_shape=(jax...]
    pallas_call x1 -> x0, local copies, waits for them, and re-layouts: 0.72 us -> none  [local(): pl.pallas_call(functools.partial(kernel, n_region, n_sub), out_shape=(jax...]
where the time goes in v2:
time: 65.7 us; the launch traced here: 65.1 us
  Pallas kernels  56.8 us (86%)
  local copies, waits for them, and re-layouts  7.62 us (12%)
  between operations  0.67 us (1%)
    pallas_call x1, Pallas kernels, local(): pl.pallas_call(functools.partial(kernel, n_region, n_sub), out_shape=(jax...  56.8 us
    unnamed x21, local copies, waits for them, and re-layouts  7.62 us

profile of v2, /device:TPU:1, one launch (start us, length us, event | category | flops | bytes accessed | tf_op | source)
XLA Modules:
  0.0 65.1 jit_solution(11486155918913579334)
XLA Ops:
  0.6 0.0 copy-start.1
  0.6 0.0 copy-start.8
  0.7 0.7 %copy-done.1 = s32[2,2048]{1,0:T(2,128)S(1)} copy-done((s32[2,2048]{1,0:T(2,128)S(1)}, s32[2,2048]{1,0:T(2,128)}, u32[]{:S(2)}) %copy-start.1) | copy-done | bytes 16408
  1.4 0.0 copy-done.8
  1.4 0.0 copy-start
  1.4 0.8 %copy-done = f32[2,3,2048]{2,0,1:T(2,128)S(1)} copy-done((f32[2,3,2048]{2,0,1:T(2,128)S(1)}, f32[2,3,2048]{2,0,1:T(2,128)}, u32[]{:S(2)}) %copy-start) | copy-done | bytes 49176
  2.2 0.0 copy-start.2
  2.2 0.7 %copy-done.2 = s32[2,2048]{1,0:T(2,128)S(1)} copy-done((s32[2,2048]{1,0:T(2,128)S(1)}, s32[2,2048]{1,0:T(2,128)}, u32[]{:S(2)}) %copy-start.2) | copy-done | bytes 16408
  2.9 0.0 copy-start.3
  2.9 0.7 %copy-done.3 = s32[2,2048]{1,0:T(2,128)S(1)} copy-done((s32[2,2048]{1,0:T(2,128)S(1)}, s32[2,2048]{1,0:T(2,128)}, u32[]{:S(2)}) %copy-start.3) | copy-done | bytes 16408
  3.6 0.0 copy-start.4
  3.6 0.7 %copy-done.4 = f32[2,2048]{1,0:T(2,128)S(1)} copy-done((f32[2,2048]{1,0:T(2,128)S(1)}, f32[2,2048]{1,0:T(2,128)}, u32[]{:S(2)}) %copy-start.4) | copy-done | bytes 16408
  4.3 0.0 copy-start.5
  4.3 0.7 %copy-done.5 = f32[2,2048]{1,0:T(2,128)S(1)} copy-done((f32[2,2048]{1,0:T(2,128)S(1)}, f32[2,2048]{1,0:T(2,128)}, u32[]{:S(2)}) %copy-start.5) | copy-done | bytes 16408
  5.0 0.0 copy-start.6
  5.0 0.7 %copy-done.6 = f32[2048]{0:T(1024)S(1)} copy-done((f32[2048]{0:T(1024)S(1)}, f32[2048]{0:T(1024)}, u32[]{:S(2)}) %copy-start.6) | copy-done | bytes 8216
  5.7 0.0 copy-start.7
  5.7 0.7 %copy-done.7 = s32[512]{0:T(512)S(1)} copy-done((s32[512]{0:T(512)S(1)}, s32[512]{0:T(512)}, u32[]{:S(2)}) %copy-start.7) | copy-done | bytes 2072
  6.4 56.8 %shard_map.112 = (f32[2,6272]{1,0:T(2,128)S(1)}, f32[32,128]{1,0:T(8,128)S(1)}, f32[192,128]{1,0:T(8,128)S(1)}) custom-call(s32[32,128]{1,0:T(8,128)S(1)} %bitcast.47, s32[32,128]{1,0:T(8,128)S(1)} %bitcast.48, s32[32,128]{1,0:T(8,128)S(1)} %bitcast.49, s32[4,128]{1,0:T(4,128)S(1)} %bitcast.54, s32[1,64]{1,0:T(1,128)S(1)} %bitcast.55, ...), custom_call_target="tpu_custom_call" | custom-call | tf_op jit(solution)/shard_map/pallas_call | solution.py:377
  63.2 0.6 copy.23
  63.8 0.6 copy.24
  64.5 0.6 copy.25
Async XLA Ops:
  0.6 0.7 %copy-start.1 = (s32[2,2048]{1,0:T(2,128)S(1)}, s32[2,2048]{1,0:T(2,128)}, u32[]{:S(2)}) copy-start(s32[2,2048]{1,0:T(2,128)} %param.9) | copy-start | bytes 49156
  0.6 0.7 %copy-start.8 = (s32[64]{0:T(128)S(1)}, s32[64]{0:T(128)}, u32[]{:S(2)}) copy-start(s32[64]{0:T(128)} %param.13) | copy-start | bytes 772
  1.4 0.8 %copy-start = (f32[2,3,2048]{2,0,1:T(2,128)S(1)}, f32[2,3,2048]{2,0,1:T(2,128)}, u32[]{:S(2)}) copy-start(f32[2,3,2048]{2,0,1:T(2,128)} %param.14) | copy-start | bytes 147460
  2.2 0.7 %copy-start.2 = (s32[2,2048]{1,0:T(2,128)S(1)}, s32[2,2048]{1,0:T(2,128)}, u32[]{:S(2)}) copy-start(s32[2,2048]{1,0:T(2,128)} %param.10) | copy-start | bytes 49156
  2.9 0.7 %copy-start.3 = (s32[2,2048]{1,0:T(2,128)S(1)}, s32[2,2048]{1,0:T(2,128)}, u32[]{:S(2)}) copy-start(s32[2,2048]{1,0:T(2,128)} %param.11) | copy-start | bytes 49156
  3.6 0.7 %copy-start.4 = (f32[2,2048]{1,0:T(2,128)S(1)}, f32[2,2048]{1,0:T(2,128)}, u32[]{:S(2)}) copy-start(f32[2,2048]{1,0:T(2,128)} %param.15) | copy-start | bytes 49156
  4.3 0.7 %copy-start.5 = (f32[2,2048]{1,0:T(2,128)S(1)}, f32[2,2048]{1,0:T(2,128)}, u32[]{:S(2)}) copy-start(f32[2,2048]{1,0:T(2,128)} %param.17) | copy-start | bytes 49156
  5.0 0.7 %copy-start.6 = (f32[2048]{0:T(1024)S(1)}, f32[2048]{0:T(1024)}, u32[]{:S(2)}) copy-start(f32[2048]{0:T(1024)} %param.16) | copy-start | bytes 24580
  5.7 0.7 %copy-start.7 = (s32[512]{0:T(512)S(1)}, s32[512]{0:T(512)}, u32[]{:S(2)}) copy-start(s32[512]{0:T(512)} %param.12) | copy-start | bytes 6148

commit v3 on v2

v3 whole, which is shorter than its diff:
```python
import functools

import jax
import jax.numpy as jnp
from jax import lax
from jax.experimental import pallas as pl
from jax.experimental.pallas import tpu as pltpu
from jax.sharding import PartitionSpec as P

MESH = pl.DeviceIdType.MESH
F32 = jnp.float32
I32 = jnp.int32
ROWS = 16
LANES = 128
E_DEV = ROWS * LANES
NXF = 2176
ROUNDS = 3


def iota(shape, dim):
    return lax.broadcasted_iota(I32, shape, dim)


def lane_gather(rows, lane):
    numbers = lax.GatherDimensionNumbers(
        offset_dims=(),
        collapsed_slice_dims=(1,),
        start_index_map=(1,),
        operand_batching_dims=(0,),
        start_indices_batching_dims=(0,),
    )
    return lax.gather(
        rows, lane[..., None], numbers, (1, 1), mode=lax.GatherScatterMode.PROMISE_IN_BOUNDS
    )


def lookup(rows, index, start=None):
    lane, high = index & 127, index >> 7
    out = start
    for number, row in rows:
        wide = jnp.broadcast_to(row, index.shape)
        found = lane_gather(wide, lane)
        out = jnp.where(high == number, found, jnp.zeros_like(found) if out is None else out)
    return out


def table(ref, count=ROWS, first=0):
    return [(first + h, ref[h : h + 1, :]) for h in range(count)]


def total_row(parts):
    lane = iota((1, LANES), 1)
    row = jnp.zeros((1, LANES), F32)
    for number, part in enumerate(parts):
        flat = jnp.sum(part, axis=0, keepdims=True)
        row = jnp.where(lane == number, jnp.sum(flat, axis=1, keepdims=True), row)
    return row


def pick(row, number):
    return jnp.sum(jnp.where(iota((1, LANES), 1) == number, row, 0.0), axis=1, keepdims=True)


def spots(place):
    return jnp.where(iota((LANES, LANES), 0) == (place & 127), 1.0, 0.0).astype(jnp.bfloat16)


def by_row(hit, *values):
    blocks = [jnp.where(hit, value, 0.0) for value in values]
    return jnp.concatenate(blocks, axis=0).astype(jnp.bfloat16)


def product(left, right):
    return lax.dot_general(left, right, (((1,), (1,)), ((), ())), preferred_element_type=F32)


def cut(value):
    scaled = value * 65537.0
    high = scaled - (scaled - value)
    rest = value - high
    scaled = rest * 65537.0
    middle = scaled - (scaled - rest)
    return high, middle, rest - middle


def kernel(
    n_region, n_sub,
    conn_x_in, conn_y_in, conn_z_in, send_y_in, send_z_in, perm_in, storage_in, sigma_in, source_in,
    trace_out, pressure_out, flux_out,
    conn_x, conn_y, conn_z, send_y, send_z, perm, storage, sigma_ref, source, in_sem,
    zlist, tables, place, ilist, cuts, left, spot, moved, by_face,
    y_send, y_recv, z_send, z_recv, halo_send_sem, halo_recv_sem,
    a_send, a_recv, b_send, b_recv, a_send_sem, a_recv_sem, b_send_sem, b_recv_sem,
):
    loads = [
        pltpu.make_async_copy(there, here, in_sem.at[k])
        for k, (there, here) in enumerate(
            (
                (conn_y_in, conn_y), (conn_z_in, conn_z), (conn_x_in, conn_x),
                (send_y_in, send_y), (send_z_in, send_z),
                (perm_in, perm), (storage_in, storage), (sigma_in, sigma_ref), (source_in, source),
            )
        )
    ]
    for load in loads:
        load.start()

    region, sub = lax.axis_index("region"), lax.axis_index("sub")
    n_flat, n_deep = n_sub // 2, 2 * n_region
    core, deep = lax.rem(sub, 2), lax.rem(lax.div(sub, 2), 2)
    flat_me = lax.div(sub, 4) * 2 + core
    deep_me = deep * n_region + region
    sub_up, sub_down = lax.rem(sub + 1, n_sub), lax.rem(sub + n_sub - 1, n_sub)
    region_up, region_down = lax.rem(region + 1, n_region), lax.rem(region + n_region - 1, n_region)

    def flat_peer(offset):
        peer = lax.rem(flat_me + offset, n_flat)
        return (region, lax.div(peer, 2) * 4 + deep * 2 + lax.rem(peer, 2))

    def deep_peer(offset):
        peer = lax.rem(deep_me + offset, n_deep)
        return (lax.rem(peer, n_region), sub - deep * 2 + lax.div(peer, n_region) * 2)

    barrier = pltpu.get_barrier_semaphore()

    def greet(device):
        pl.semaphore_signal(barrier, inc=1, device_id=device, device_id_type=MESH)

    greet((region, sub_up))
    greet((region, sub_down))
    for j in range(1, n_flat):
        greet(flat_peer(j))
    for j in range(1, n_deep):
        greet(deep_peer(j))
    for load in loads:
        load.wait()

    def pair(ref, first=0):
        return [ref[pl.ds(first + k, ROWS, stride=2), :] for k in range(2)]

    def chunk(i):
        return pl.ds(pl.multiple_of(i * LANES, LANES), LANES)

    def element_terms(trans, store, sigma):
        diag = [
            2.0 * (trans[c][0] + trans[c][1] + trans[c][2]) + store[c] + sigma for c in range(2)
        ]
        determ = diag[0] * diag[1] - sigma * sigma
        return diag[1] / determ, sigma / determ, diag[0] / determ

    def solve(terms, load):
        return (terms[0] * load[0] + terms[1] * load[1], terms[1] * load[0] + terms[2] * load[1])

    def faces_step(i, carry):
        lane, row = iota((1, LANES), 1).astype(F32), (i + 1).astype(F32)
        for k, (ref, side, count, first, at) in enumerate(
            (
                (conn_y, 1, 16, 0, 0), (conn_z, 1, 16, 0, 32), (conn_y, 0, 8, 16, 64),
                (conn_z, 0, 8, 16, 80), (conn_x, 1, 24, 0, 96),
            )
        ):
            face = ref[pl.ds(2 * i + side, 1), :]
            hit = iota((count, LANES), 0) == (face >> 7) - first
            left[at : at + 2 * count, chunk(i)] = by_row(hit, lane, row)
            spot[k, :, chunk(i)] = spots(face)
        return carry

    lax.fori_loop(0, ROWS, faces_step, 0)

    def cells(k, at, count):
        found = product(left[at : at + 2 * count, :], spot[k]).astype(I32)
        return (found[count:] - 1) * LANES + found[:count]

    cell_y, cell_z = cells(0, 0, 16), cells(1, 32, 16)
    side_y, side_z = cells(2, 64, 8), cells(3, 80, 8)
    cell_x = cells(4, 96, 24)
    place[0, 0:ROWS, :] = cell_y
    place[1, 0:ROWS, :] = cell_z
    place[2, 0:24, :] = cell_x
    zlist[0:1, :] = jnp.full((1, LANES), -1, I32)
    zlist[0:1, 0:64] = send_z[...]

    def find(ref, index, missing, count=ROWS):
        return lookup(table(ref, count), index, jnp.full(index.shape, missing, I32))

    up_y = find(place.at[0], send_y[...], -1)
    up_z = find(place.at[1], zlist[0:1, :], -1)
    down_y, down_z = side_y[0:4], side_z[0:1]

    def copies(step):
        def one(kind, send, recv, device):
            return pltpu.make_async_remote_copy(
                src_ref=send,
                dst_ref=recv,
                send_sem=halo_send_sem.at[step, kind],
                recv_sem=halo_recv_sem.at[step, kind],
                device_id=device,
                device_id_type=MESH,
            )

        return [
            one(0, y_send.at[step, 0], y_recv.at[step, 0], (region, sub_up)),
            one(1, y_send.at[step, 1], y_recv.at[step, 1], (region, sub_down)),
            one(2, z_send.at[step, 0], z_recv.at[step, 0], (region_up, sub)),
            one(3, z_send.at[step, 1], z_recv.at[step, 1], (region_down, sub)),
        ]

    def keep_sides(at):
        for c in range(2):
            ilist[at, 4 * c : 4 * c + 4, :] = up_y
            ilist[at + 1, 4 * c : 4 * c + 4, :] = down_y
            ilist[at + 2, c : c + 1, :] = up_z
            ilist[at + 2, 2 + c : 3 + c, :] = down_z

    def publish(step, at, y_low, y_up, z_low, z_up, before=None):
        for k, part in enumerate((*y_up, *y_low)):
            tables[k, 0:ROWS, :] = part
        second = iota((8, LANES), 0) >= 4
        for k in range(2):
            rows = [
                (h, jnp.where(second, tables[2 * k + 1, h : h + 1, :], tables[2 * k, h : h + 1, :]))
                for h in range(ROWS)
            ]
            y_send[step, k] = lookup(rows, ilist[at + k])
        for k, part in enumerate((*z_up, *z_low)):
            tables[4, pl.ds(k, ROWS, stride=4), :] = part
        rows = [(h, tables[4, 4 * h : 4 * h + 4, :]) for h in range(ROWS)]
        z_rows = lookup(rows, ilist[at + 2, 0:4, :])
        z_send[step, 0] = z_rows[0:2]
        z_send[step, 1] = z_rows[2:4]
        if before is not None:
            before()
        for copy in copies(step):
            copy.start()

    keep_sides(0)
    by_side = [pair(perm, 32 * d) for d in range(3)]
    trans = [[2.0 * by_side[d][c] for d in range(3)] for c in range(2)]
    store, origin, sigma = pair(storage), pair(source), sigma_ref[...]
    base = solve(element_terms(trans, store, sigma), origin)
    first_y = [trans[c][1] * base[c] for c in range(2)]
    first_z = [trans[c][2] * base[c] for c in range(2)]
    greetings = 2 + (n_flat - 1) + (n_deep - 1)
    publish(0, 0, first_y, first_y, first_z, first_z, lambda: pl.semaphore_wait(barrier, greetings))

    faces = (pair(conn_x), pair(conn_y), pair(conn_z))
    below = (
        find(place.at[2], faces[0][0], -1, 17),
        find(place.at[0], faces[1][0], -1),
        find(place.at[1], faces[2][0], -1),
    )
    words = [jnp.where(cell >= 0, cell + 4097, 0) for cell in below]
    for level in range(5):
        for d, levels in enumerate((4, 2, 5)):
            if level < levels:
                place[3 + d, 0:ROWS, :] = words[d]
                ahead = find(place.at[3 + d], (words[d] & 4095) - 1, 0)
                words[d] = (words[d] & ~4095) + ahead
    steps = [word >> 12 for word in words]
    place[3, 0:ROWS, :] = steps[0] * LANES + steps[1] * 32 + steps[2]

    values = [*trans[0], *trans[1], *store, sigma, *origin]
    for k, value in enumerate(values):
        for j, part in enumerate(cut(value)):
            cuts[3 * k + j] = part
    lists = [faces[0][1], faces[1][1], faces[2][1], faces[0][0]]
    lists += [jnp.maximum(faces[d][0] - E_DEV, 0) for d in (1, 2)]
    for k, face in enumerate(lists):
        cuts[33 + 2 * k] = (face >> 7).astype(F32)
        cuts[34 + 2 * k] = (face & 127).astype(F32)

    def order_step(i, carry):
        at = place[3, pl.ds(i, 1), :]
        hit = iota((ROWS, LANES), 0) == (at >> 7)
        spot[0, :, chunk(i)] = spots(at)
        for k in range(45):
            left[ROWS * k : ROWS * (k + 1), chunk(i)] = by_row(hit, cuts[k, pl.ds(i, 1), :])
        lane, row = iota((1, LANES), 1).astype(F32), i.astype(F32)
        left[ROWS * 45 : ROWS * 47, chunk(i)] = by_row(hit, row, lane)
        return carry

    lax.fori_loop(0, ROWS, order_step, 0)
    moved[0 : ROWS * 47, :] = product(left[0 : ROWS * 47, :], spot[0])

    def part(k):
        return moved[ROWS * k : ROWS * (k + 1), :]

    values = [part(3 * k) + part(3 * k + 1) + part(3 * k + 2) for k in range(11)]
    trans, store = [values[0:3], values[3:6]], values[6:8]
    sigma, origin = values[8], values[9:11]
    for k in range(7):
        ilist[8 + 2 * k : 10 + 2 * k] = (
            (part(33 + 2 * k) * 128.0 + part(34 + 2 * k)).astype(I32).reshape(2, 8, LANES)
        )

    def listed(k):
        return ilist[8 + 2 * k : 10 + 2 * k].reshape(ROWS, LANES)

    terms = element_terms(trans, store, sigma)

    lane, row = iota((ROWS, LANES), 1), iota((ROWS, LANES), 0)
    level = lane & 31
    place[4, 0:ROWS, :] = place[3, 0:ROWS, :]
    up_y, down_y = find(place.at[3], up_y, -1), find(place.at[3], down_y, -1)
    up_z, down_z = find(place.at[3], up_z, -1), find(place.at[3], down_z, -1)
    keep_sides(3)
    entry = iota((1, LANES), 1).astype(F32)
    lefts, rights = [], []
    for h in range(4):
        at = ilist[3, h : h + 1, :]
        hit = iota((ROWS, LANES), 0) == (at >> 7)
        lefts.append(by_row(hit, entry, jnp.full((1, LANES), h + 1.0, F32)))
        rights.append(spots(at))
    found = product(jnp.concatenate(lefts, axis=1), jnp.concatenate(rights, axis=1)).astype(I32)
    above_y = (found[ROWS:] - 1) * LANES + found[:ROWS]
    at = ilist[5, 0:1, :]
    hit = iota((ROWS, LANES), 0) == (at >> 7)
    found = product(by_row(hit, entry, jnp.full((1, LANES), 1.0, F32)), spots(at)).astype(I32)
    above_z = (found[ROWS:] - 1) * LANES + found[:ROWS]
    above_y = jnp.where(sub == n_sub - 1, -1, above_y)
    above_z = jnp.where(region == n_region - 1, -1, above_z)
    low_y, low_z = lane < 32, level == 0
    below_y, below_z = jnp.where(low_y, listed(4), -1), jnp.where(low_z, listed(5), -1)
    zero_y = jnp.logical_and(low_y, sub == 0)
    zero_z = jnp.logical_and(low_z, region == 0)

    def face_load(v):
        return [
            sum(trans[c][d] * (v[c][d][0] + v[c][d][1]) for d in range(3)) for c in range(2)
        ]

    def contributions(v, inside):
        return [
            [[trans[c][d] * (v[c][d][s] - inside[c]) for s in range(2)] for d in range(3)]
            for c in range(2)
        ]

    def send(step, g):
        publish(step, 3, *([g[c][d][s] for c in range(2)] for d in (1, 2) for s in range(2)))

    def assemble(step, g):
        out = [[[None, None] for _ in range(3)] for _ in range(2)]
        for c in range(2):
            (x_low, x_up), (y_low, y_up), (z_low, z_up) = g[c]
            out[c][0][1] = x_up + jnp.where(row == 15, 0.0, pltpu.roll(x_low, 15, 0))
            out[c][0][0] = x_low + jnp.where(row == 0, 0.0, pltpu.roll(x_up, 1, 0))
            out[c][1][1] = jnp.where(lane >= 96, 0.0, pltpu.roll(y_low, 96, 1))
            out[c][1][0] = jnp.where(low_y, 0.0, pltpu.roll(y_up, 32, 1))
            out[c][2][1] = jnp.where(level == 31, 0.0, pltpu.roll(z_low, 127, 1))
            out[c][2][0] = jnp.where(low_z, 0.0, pltpu.roll(z_up, 1, 1))
        for copy in copies(step):
            copy.wait_recv()
        for c in range(2):
            from_below_y = lookup(table(y_recv.at[step, 0, pl.ds(4 * c, 4)], 4), below_y)
            from_above_y = lookup(table(y_recv.at[step, 1, pl.ds(4 * c, 4)], 4), above_y)
            from_below_z = lookup(table(z_recv.at[step, 0, pl.ds(c, 1)], 1), below_z)
            from_above_z = lookup(table(z_recv.at[step, 1, pl.ds(c, 1)], 1), above_z)
            out[c][1][1] = g[c][1][1] + (out[c][1][1] + from_above_y)
            out[c][2][1] = g[c][2][1] + (out[c][2][1] + from_above_z)
            out[c][1][0] = jnp.where(zero_y, 0.0, g[c][1][0] + (out[c][1][0] + from_below_y))
            out[c][2][0] = jnp.where(zero_z, 0.0, g[c][2][0] + (out[c][2][0] + from_below_z))
        return out

    def inner(u, v):
        total = sum(u[c][d][1] * v[c][d][1] for c in range(2) for d in range(3))
        edge = sum(u[c][0][0] * v[c][0][0] for c in range(2))
        return total + jnp.where(row == 0, edge, 0.0)

    def energy(v, load, solved):
        total = sum(
            trans[c][d] * (v[c][d][0] * v[c][d][0] + v[c][d][1] * v[c][d][1])
            for c in range(2)
            for d in range(3)
        )
        return total - (load[0] * solved[0] + load[1] * solved[1])

    def scatter(send, recv, send_sem, recv_sem, peer, count, row):
        send[0:1, :] = row
        recv[count - 1 : count, :] = row
        for j in sorted(range(1, count), key=lambda j: -min(j, count - j)):
            pltpu.make_async_remote_copy(
                src_ref=send.at[pl.ds(0, 1)],
                dst_ref=recv.at[pl.ds(j - 1, 1)],
                send_sem=send_sem,
                recv_sem=recv_sem,
                device_id=peer(j),
                device_id_type=MESH,
            ).start()

    def drain(buffer, sem, count):
        rows = buffer.at[pl.ds(0, count - 1)]
        pltpu.make_async_copy(rows, rows, sem).wait()

    def flat_start(k, row):
        scatter(a_send.at[k], a_recv.at[k], a_send_sem.at[k], a_recv_sem.at[k], flat_peer, n_flat, row)

    def flat_done(k):
        drain(a_recv.at[k], a_recv_sem.at[k], n_flat)
        return jnp.sum(a_recv[k], axis=0, keepdims=True)

    def deep_start(k, row):
        scatter(b_send.at[k], b_recv.at[k], b_send_sem.at[k], b_recv_sem.at[k], deep_peer, n_deep, row)

    def deep_done(k):
        drain(b_recv.at[k], b_recv_sem.at[k], n_deep)
        return jnp.sum(b_recv[k], axis=0, keepdims=True)

    base = solve(terms, origin)
    b = assemble(0, [[[trans[c][d] * base[c]] * 2 for d in range(3)] for c in range(2)])

    load = face_load(b)
    inside = solve(terms, load)
    g = contributions(b, inside)
    send(1, g)
    flat_start(0, total_row([inner(b, b), energy(b, load, inside)]))
    w = assemble(1, g)

    g = contributions(w, solve(terms, face_load(w)))
    send(2, g)
    deep_start(0, flat_done(0))
    ww = assemble(2, g)

    first = deep_done(0)
    norm_0 = pick(first, 0)
    alpha_0 = norm_0 / pick(first, 1)

    def blend(u, factor, v):
        return [
            [[u[c][d][s] - factor * v[c][d][s] for s in range(2)] for d in range(3)]
            for c in range(2)
        ]

    r = blend(b, alpha_0, w)
    s = blend(w, alpha_0, ww)
    load = face_load(s)
    flat_start(1, total_row([inner(r, r), inner(r, s), inner(s, s), energy(s, load, solve(terms, load))]))
    deep_start(1, flat_done(1))
    for step in range(ROUNDS):
        for copy in copies(step):
            copy.wait_send()
    drain(a_recv.at[0], a_send_sem.at[0], n_flat)
    drain(b_recv.at[0], b_send_sem.at[0], n_deep)
    drain(a_recv.at[1], a_send_sem.at[1], n_flat)
    sums = deep_done(1)
    rr, rs, ss, sas = (pick(sums, k) for k in range(4))

    beta_0 = rr / norm_0
    alpha_1 = rr / (rs - beta_0 * rr / alpha_0)
    ws = -(rr / alpha_0 + rs) / alpha_0
    norm_2 = -alpha_1 * (rs - alpha_1 * ss - alpha_1 * beta_0 * ws)
    beta_1 = norm_2 / rr
    ratio = alpha_1 * beta_0 / alpha_0
    along = ss - alpha_1 * sas - ratio * (ws - ss)
    energy_2 = -norm_2 / alpha_1 * (1.0 + ratio) - alpha_1 * along
    alpha_2 = norm_2 / (energy_2 - beta_1 * norm_2 / alpha_1)
    on_r = alpha_1 + alpha_2 * (1.0 + beta_1)
    on_s = -alpha_2 * alpha_1
    on_b = alpha_0 + alpha_1 * beta_0 + alpha_2 * beta_1 * beta_0 + on_r
    on_w = -alpha_2 * alpha_1 * beta_0 - alpha_0 * on_r + on_s
    on_ww = -alpha_0 * on_s

    trace = [
        [
            [on_b * b[c][d][k] + on_w * w[c][d][k] + on_ww * ww[c][d][k] for k in range(2)]
            for d in range(3)
        ]
        for c in range(2)
    ]
    load = face_load(trace)
    pressure = solve(terms, [origin[c] + load[c] for c in range(2)])
    flux = [
        [trans[c][d] * (pressure[c] - trace[c][d][k]) for d in range(3) for k in range(2)]
        for c in range(2)
    ]

    results = [*pressure, *flux[0], *flux[1]]
    results += [trace[c][d][1] for d in range(3) for c in range(2)]
    for k, value in enumerate(results):
        for j, piece in enumerate(cut(value)):
            cuts[3 * k + j] = piece
    for k in range(4):
        place[k, 0:ROWS, :] = listed((6, 1, 2, 0)[k])

    def back_step(i, carry):
        lanes = chunk(i)
        at = [place[k, pl.ds(i, 1), :] for k in range(4)]
        hit = [iota((ROWS, LANES), 0) == (at[k] >> 7) for k in range(3)]
        for k in range(4):
            spot[k, :, lanes] = spots(at[k])
        for k in range(42):
            left[ROWS * k : ROWS * (k + 1), lanes] = by_row(hit[0], cuts[k, pl.ds(i, 1), :])
        for k in range(6):
            here = ROWS * (42 + k)
            left[here : here + ROWS, lanes] = by_row(hit[1], cuts[48 + k, pl.ds(i, 1), :])
            here = ROWS * (48 + k)
            left[here : here + ROWS, lanes] = by_row(hit[2], cuts[54 + k, pl.ds(i, 1), :])
        hit_x = iota((24, LANES), 0) == (at[3] >> 7)
        for j in range(3):
            here = ROWS * 54 + 48 * j
            both = (cuts[42 + j, pl.ds(i, 1), :], cuts[45 + j, pl.ds(i, 1), :])
            left[here : here + 48, lanes] = by_row(hit_x, *both)
        return carry

    lax.fori_loop(0, ROWS, back_step, 0)
    moved[0 : ROWS * 42, :] = product(left[0 : ROWS * 42, :], spot[0])
    moved[ROWS * 42 : ROWS * 48, :] = product(left[ROWS * 42 : ROWS * 48, :], spot[1])
    moved[ROWS * 48 : ROWS * 54, :] = product(left[ROWS * 48 : ROWS * 54, :], spot[2])
    lowest = ilist[14, 0:1, :]
    hit_x = iota((24, LANES), 0) == (lowest >> 7)
    edges = [cut(trace[c][0][0][0:1, :]) for c in range(2)]
    edge = jnp.concatenate([by_row(hit_x, edges[0][j], edges[1][j]) for j in range(3)], axis=0)
    of_x = product(left[ROWS * 54 : ROWS * 63, :], spot[3]) + product(edge, spots(lowest))
    of_x = of_x[0:48] + of_x[48:96] + of_x[96:144]

    def whole(k):
        return part(k) + part(k + 1) + part(k + 2)

    for c in range(2):
        pressure_out[pl.ds(c, ROWS, stride=2), :] = whole(3 * c)
        for k in range(6):
            flux_out[pl.ds(32 * k + c, ROWS, stride=2), :] = whole(6 + 18 * c + 3 * k)
        by_face[pl.ds(c, 17, stride=2), :] = of_x[24 * c : 24 * c + 17]
        by_face[pl.ds(34 + c, ROWS, stride=2), :] = whole(42 + 3 * c)
        by_face[pl.ds(66 + c, ROWS, stride=2), :] = whole(48 + 3 * c)
    for i in range(49):
        trace_out[:, LANES * i : LANES * (i + 1)] = by_face[2 * i : 2 * i + 2, :]
    drain(b_recv.at[1], b_send_sem.at[1], n_deep)


def pair_rows(array):
    return array.reshape(2, ROWS, LANES).transpose(1, 0, 2).reshape(2 * ROWS, LANES)


def solution(mesh):
    n_region, n_sub = mesh.shape["region"], mesh.shape["sub"]
    n_flat, n_deep = n_sub // 2, 2 * n_region

    def local(conn_x, conn_y, conn_z, send_y, send_z, perm, storage, sigma, source):
        vmem = pl.BlockSpec(memory_space=pltpu.VMEM)
        dma = pltpu.SemaphoreType.DMA
        sides = perm.transpose(1, 0, 2).reshape(3, 2, ROWS, LANES).transpose(0, 2, 1, 3)
        trace, pressure, flux = pl.pallas_call(
            functools.partial(kernel, n_region, n_sub),
            out_shape=(
                jax.ShapeDtypeStruct((2, NXF + 2 * E_DEV), F32),
                jax.ShapeDtypeStruct((2 * ROWS, LANES), F32),
                jax.ShapeDtypeStruct((12 * ROWS, LANES), F32),
            ),
            in_specs=[pl.BlockSpec(memory_space=pltpu.HBM)] * 9,
            out_specs=(vmem,) * 3,
            scratch_shapes=[
                pltpu.VMEM((2 * ROWS, LANES), I32),
                pltpu.VMEM((2 * ROWS, LANES), I32),
                pltpu.VMEM((2 * ROWS, LANES), I32),
                pltpu.VMEM((4, LANES), I32),
                pltpu.VMEM((1, 64), I32),
                pltpu.VMEM((6 * ROWS, LANES), F32),
                pltpu.VMEM((2 * ROWS, LANES), F32),
                pltpu.VMEM((ROWS, LANES), F32),
                pltpu.VMEM((2 * ROWS, LANES), F32),
                dma((9,)),
                pltpu.VMEM((8, LANES), I32),
                pltpu.VMEM((5, 4 * ROWS, LANES), F32),
                pltpu.VMEM((6, 24, LANES), I32),
                pltpu.VMEM((22, 8, LANES), I32),
                pltpu.VMEM((60, ROWS, LANES), F32),
                pltpu.VMEM((63 * ROWS, E_DEV), jnp.bfloat16),
                pltpu.VMEM((5, LANES, E_DEV), jnp.bfloat16),
                pltpu.VMEM((54 * ROWS, LANES), F32),
                pltpu.VMEM((104, LANES), F32),
                pltpu.VMEM((ROUNDS, 2, 8, LANES), F32),
                pltpu.VMEM((ROUNDS, 2, 8, LANES), F32),
                pltpu.VMEM((ROUNDS, 2, 2, LANES), F32),
                pltpu.VMEM((ROUNDS, 2, 2, LANES), F32),
                dma((ROUNDS, 4)),
                dma((ROUNDS, 4)),
                pltpu.VMEM((2, 8, LANES), F32),
                pltpu.VMEM((2, n_flat, LANES), F32),
                pltpu.VMEM((2, 8, LANES), F32),
                pltpu.VMEM((2, n_deep, LANES), F32),
                dma((2,)),
                dma((2,)),
                dma((2,)),
                dma((2,)),
            ],
            compiler_params=pltpu.CompilerParams(
                collective_id=0, has_side_effects=True, vmem_limit_bytes=32 * 1024 * 1024
            ),
        )(
            pair_rows(conn_x), pair_rows(conn_y), pair_rows(conn_z),
            send_y.reshape(4, LANES), send_z.reshape(1, 64),
            sides.reshape(6 * ROWS, LANES), pair_rows(storage), sigma.reshape(ROWS, LANES),
            pair_rows(source),
        )
        pressure = pressure.reshape(ROWS, 2, LANES).transpose(1, 0, 2).reshape(2, E_DEV)
        flux = flux.reshape(6, ROWS, 2, LANES).transpose(2, 0, 1, 3).reshape(2, 6, E_DEV)
        return trace, pressure, flux

    both = ("region", "sub")
    return jax.shard_map(
        local,
        mesh=mesh,
        in_specs=(
            P(None, both), P(None, both), P(None, both), P(both), P(both),
            P(None, None, both), P(None, both), P(both), P(None, both),
        ),
        out_specs=(P(None, both), P(None, both), P(None, None, both)),
        check_vma=False,
    )
```

time: 65.7 us -> 70.1 us (1.067)
  Pallas kernels: 56.8 us -> 61.2 us
    pallas_call x1, Pallas kernels: 56.8 us -> 61.2 us  [local(): pl.pallas_call(functools.partial(kernel, n_region, n_sub), out_shape=(jax...]
where the time goes in v3:
time: 70.1 us; the launch traced here: 69.5 us
  Pallas kernels  61.2 us (87%)
  local copies, waits for them, and re-layouts  7.62 us (11%)
    pallas_call x1, Pallas kernels, local(): pl.pallas_call(functools.partial(kernel, n_region, n_sub), out_shape=(jax...  61.2 us
    unnamed x21, local copies, waits for them, and re-layouts  7.62 us

profile of v3, /device:TPU:1, one launch (start us, length us, event | category | flops | bytes accessed | tf_op | source)
XLA Modules:
  0.0 69.5 jit_solution(12585763801159186650)
XLA Ops:
  0.6 0.0 copy-start.1
  0.6 0.0 copy-start.8
  0.7 0.7 %copy-done.1 = s32[2,2048]{1,0:T(2,128)S(1)} copy-done((s32[2,2048]{1,0:T(2,128)S(1)}, s32[2,2048]{1,0:T(2,128)}, u32[]{:S(2)}) %copy-start.1) | copy-done | bytes 16408
  1.4 0.0 copy-done.8
  1.4 0.0 copy-start
  1.4 0.8 %copy-done = f32[2,3,2048]{2,0,1:T(2,128)S(1)} copy-done((f32[2,3,2048]{2,0,1:T(2,128)S(1)}, f32[2,3,2048]{2,0,1:T(2,128)}, u32[]{:S(2)}) %copy-start) | copy-done | bytes 49176
  2.2 0.0 copy-start.2
  2.2 0.7 %copy-done.2 = s32[2,2048]{1,0:T(2,128)S(1)} copy-done((s32[2,2048]{1,0:T(2,128)S(1)}, s32[2,2048]{1,0:T(2,128)}, u32[]{:S(2)}) %copy-start.2) | copy-done | bytes 16408
  2.9 0.0 copy-start.3
  2.9 0.7 %copy-done.3 = s32[2,2048]{1,0:T(2,128)S(1)} copy-done((s32[2,2048]{1,0:T(2,128)S(1)}, s32[2,2048]{1,0:T(2,128)}, u32[]{:S(2)}) %copy-start.3) | copy-done | bytes 16408
  3.6 0.0 copy-start.4
  3.6 0.7 %copy-done.4 = f32[2,2048]{1,0:T(2,128)S(1)} copy-done((f32[2,2048]{1,0:T(2,128)S(1)}, f32[2,2048]{1,0:T(2,128)}, u32[]{:S(2)}) %copy-start.4) | copy-done | bytes 16408
  4.3 0.0 copy-start.5
  4.3 0.7 %copy-done.5 = f32[2,2048]{1,0:T(2,128)S(1)} copy-done((f32[2,2048]{1,0:T(2,128)S(1)}, f32[2,2048]{1,0:T(2,128)}, u32[]{:S(2)}) %copy-start.5) | copy-done | bytes 16408
  5.0 0.0 copy-start.6
  5.0 0.7 copy-done.6
  5.7 0.0 copy-start.7
  5.7 0.7 copy-done.7
  6.4 61.2 %shard_map.112 = (f32[2,6272]{1,0:T(2,128)S(1)}, f32[32,128]{1,0:T(8,128)S(1)}, f32[192,128]{1,0:T(8,128)S(1)}) custom-call(s32[32,128]{1,0:T(8,128)S(1)} %bitcast.47, s32[32,128]{1,0:T(8,128)S(1)} %bitcast.48, s32[32,128]{1,0:T(8,128)S(1)} %bitcast.49, s32[4,128]{1,0:T(4,128)S(1)} %bitcast.54, s32[1,64]{1,0:T(1,128)S(1)} %bitcast.55, ...), custom_call_target="tpu_custom_call" | custom-call | tf_op jit(solution)/shard_map/pallas_call | solution.py:542
  67.6 0.6 copy.23
  68.2 0.6 copy.24
  68.8 0.6 copy.25
Async XLA Ops:
  0.6 0.7 %copy-start.1 = (s32[2,2048]{1,0:T(2,128)S(1)}, s32[2,2048]{1,0:T(2,128)}, u32[]{:S(2)}) copy-start(s32[2,2048]{1,0:T(2,128)} %param.9) | copy-start | bytes 49156
  0.6 0.7 %copy-start.8 = (s32[64]{0:T(128)S(1)}, s32[64]{0:T(128)}, u32[]{:S(2)}) copy-start(s32[64]{0:T(128)} %param.13) | copy-start | bytes 772
  1.4 0.8 %copy-start = (f32[2,3,2048]{2,0,1:T(2,128)S(1)}, f32[2,3,2048]{2,0,1:T(2,128)}, u32[]{:S(2)}) copy-start(f32[2,3,2048]{2,0,1:T(2,128)} %param.14) | copy-start | bytes 147460
  2.2 0.7 %copy-start.2 = (s32[2,2048]{1,0:T(2,128)S(1)}, s32[2,2048]{1,0:T(2,128)}, u32[]{:S(2)}) copy-start(s32[2,2048]{1,0:T(2,128)} %param.10) | copy-start | bytes 49156
  2.9 0.7 %copy-start.3 = (s32[2,2048]{1,0:T(2,128)S(1)}, s32[2,2048]{1,0:T(2,128)}, u32[]{:S(2)}) copy-start(s32[2,2048]{1,0:T(2,128)} %param.11) | copy-start | bytes 49156
  3.6 0.7 %copy-start.4 = (f32[2,2048]{1,0:T(2,128)S(1)}, f32[2,2048]{1,0:T(2,128)}, u32[]{:S(2)}) copy-start(f32[2,2048]{1,0:T(2,128)} %param.15) | copy-start | bytes 49156
  4.3 0.7 %copy-start.5 = (f32[2,2048]{1,0:T(2,128)S(1)}, f32[2,2048]{1,0:T(2,128)}, u32[]{:S(2)}) copy-start(f32[2,2048]{1,0:T(2,128)} %param.17) | copy-start | bytes 49156
  5.0 0.7 %copy-start.6 = (f32[2048]{0:T(1024)S(1)}, f32[2048]{0:T(1024)}, u32[]{:S(2)}) copy-start(f32[2048]{0:T(1024)} %param.16) | copy-start | bytes 24580
  5.7 0.7 copy-start.7

commit v4 on v2

--- a/solution.py
+++ b/solution.py
@@ -84,12 +84,23 @@
 
 def kernel(
     n_region, n_sub,
-    conn_x, conn_y, conn_z, send_y, send_z, perm, storage, sigma_ref, source,
+    conn_x_in, conn_y_in, conn_z_in, send_y_in, send_z_in, perm_in, storage_in, sigma_in, source_in,
     trace_out, pressure_out, flux_out,
+    conn_x, conn_y, conn_z, send_y, send_z, perm, storage, sigma_ref, source, in_sem,
     zlist, itable, tables, vtables, by_face,
     y_send, y_recv, z_send, z_recv, halo_send_sem, halo_recv_sem,
     a_send, a_recv, b_send, b_recv, a_send_sem, a_recv_sem, b_send_sem, b_recv_sem,
 ):
+    loads = [
+        pltpu.make_async_copy(there, here, in_sem.at[k])
+        for k, (there, here) in enumerate(
+            (
+                (conn_y_in, conn_y), (conn_z_in, conn_z), (send_y_in, send_y), (send_z_in, send_z),
+                (perm_in, perm), (storage_in, storage), (sigma_in, sigma_ref), (source_in, source),
+                (conn_x_in, conn_x),
+            )
+        )
+    ]
     region, sub = lax.axis_index("region"), lax.axis_index("sub")
     n_flat, n_deep = n_sub // 2, 2 * n_region
     core, deep = lax.rem(sub, 2), lax.rem(lax.div(sub, 2), 2)
@@ -113,10 +124,14 @@
 
     greet((region, sub_up))
     greet((region, sub_down))
+    for load in loads:
+        load.start()
+    for j in sorted(range(1, n_deep), key=lambda j: -min(j, n_deep - j)):
+        greet(deep_peer(j))
     for j in range(1, n_flat):
         greet(flat_peer(j))
-    for j in range(1, n_deep):
-        greet(deep_peer(j))
+    for load in loads:
+        load.wait()
 
     def pair(ref, first=0):
         return [ref[pl.ds(first + k, ROWS, stride=2), :] for k in range(2)]
@@ -259,7 +274,7 @@
     def scatter(send, recv, send_sem, recv_sem, peer, count, row):
         send[0:1, :] = row
         recv[count - 1 : count, :] = row
-        for j in range(1, count):
+        for j in sorted(range(1, count), key=lambda j: -min(j, count - j)):
             pltpu.make_async_remote_copy(
                 src_ref=send.at[pl.ds(0, 1)],
                 dst_ref=recv.at[pl.ds(j - 1, 1)],
@@ -381,9 +396,19 @@
                 jax.ShapeDtypeStruct((2 * ROWS, LANES), F32),
                 jax.ShapeDtypeStruct((12 * ROWS, LANES), F32),
             ),
-            in_specs=[vmem] * 9,
+            in_specs=[pl.BlockSpec(memory_space=pltpu.HBM)] * 9,
             out_specs=(vmem,) * 3,
             scratch_shapes=[
+                pltpu.VMEM((2 * ROWS, LANES), I32),
+                pltpu.VMEM((2 * ROWS, LANES), I32),
+                pltpu.VMEM((2 * ROWS, LANES), I32),
+                pltpu.VMEM((4, LANES), I32),
+                pltpu.VMEM((1, 64), I32),
+                pltpu.VMEM((6 * ROWS, LANES), F32),
+                pltpu.VMEM((2 * ROWS, LANES), F32),
+                pltpu.VMEM((ROWS, LANES), F32),
+                pltpu.VMEM((2 * ROWS, LANES), F32),
+                dma((9,)),
                 pltpu.VMEM((8, LANES), I32),
                 pltpu.VMEM((6, 24, LANES), I32),
                 pltpu.VMEM((12, ROWS, LANES), F32),
@@ -405,7 +430,7 @@
                 dma((2,)),
             ],
             compiler_params=pltpu.CompilerParams(
-                collective_id=0, has_side_effects=True, vmem_limit_bytes=32 * 1024 * 1024
+                collective_id=0, has_side_effects=True, vmem_limit_bytes=60 * 1024 * 1024
             ),
         )(
             pair_rows(conn_x), pair_rows(conn_y), pair_rows(conn_z),

time: 65.7 us -> 62.1 us (0.945)
  local copies, waits for them, and re-layouts: 7.62 us -> 3.43 us
  Pallas kernels: 56.8 us -> 57.6 us
    unnamed x21 -> x5, local copies, waits for them, and re-layouts: 7.62 us -> 3.43 us
    pallas_call x1, Pallas kernels: 56.8 us -> 57.6 us  [local(): pl.pallas_call(functools.partial(kernel, n_region, n_sub), out_shape=(jax...]
where the time goes in v4:
time: 62.1 us; the launch traced here: 61.7 us
  Pallas kernels  57.6 us (93%)
  local copies, waits for them, and re-layouts  3.43 us (6%)
  between operations  0.65 us (1%)
    pallas_call x1, Pallas kernels, local(): pl.pallas_call(functools.partial(kernel, n_region, n_sub), out_shape=(jax...  57.6 us
    unnamed x5, local copies, waits for them, and re-layouts  3.43 us

profile of v4, /device:TPU:1, one launch (start us, length us, event | category | flops | bytes accessed | tf_op | source)
XLA Modules:
  0.0 61.7 jit_solution(17975314407369437185)
XLA Ops:
  0.6 57.6 %shard_map.112 = (f32[2,6272]{1,0:T(2,128)}, f32[32,128]{1,0:T(8,128)}, f32[192,128]{1,0:T(8,128)}) custom-call(s32[32,128]{1,0:T(8,128)} %bitcast.47, s32[32,128]{1,0:T(8,128)} %bitcast.48, s32[32,128]{1,0:T(8,128)} %bitcast.49, s32[4,128]{1,0:T(4,128)} %bitcast.54, s32[1,64]{1,0:T(1,128)} %bitcast.55, f32[96,128]{1,0:T(8,128)} %bitcast.46, ...), custom_call_target="tpu_custom_call" | custom-call | tf_op jit(solution)/shard_map/pallas_call | solution.py:392
  58.3 0.0 copy-start
  58.3 1.5 %copy.23 = f32[2,6272]{1,0:T(2,128)} copy(f32[2,6272]{1,0:T(2,128)} %get-tuple-element.12) | data formatting | bytes 100352
  59.7 1.3 %copy.24 = f32[2,2048]{1,0:T(2,128)} copy(f32[2,2048]{1,0:T(2,128)} %bitcast.52) | data formatting | bytes 32768
  61.1 0.0 copy-done
  61.1 0.6 %copy.25 = f32[2,6,2048]{2,0,1:T(2,128)} copy(f32[2,6,2048]{2,0,1:T(2,128)S(1)} %bitcast.45) | data formatting | bytes 196608
Async XLA Ops:
  58.3 2.8 %copy-start = (f32[192,128]{1,0:T(8,128)S(1)}, f32[192,128]{1,0:T(8,128)}, u32[]{:S(2)}) copy-start(f32[192,128]{1,0:T(8,128)} %get-tuple-element.8) | copy-start | bytes 294916

commit v5 on v2

--- a/solution.py
+++ b/solution.py
@@ -84,10 +84,12 @@
 
 def kernel(
     n_region, n_sub,
-    conn_x, conn_y, conn_z, send_y, send_z, perm, storage, sigma_ref, source,
+    conn_x_in, conn_y_in, conn_z_in, send_y, send_z, perm_in, storage_in, sigma_ref, source_in,
     trace_out, pressure_out, flux_out,
-    zlist, itable, tables, vtables, by_face,
-    y_send, y_recv, z_send, z_recv, halo_send_sem, halo_recv_sem,
+    conn_x, conn_y, conn_z, perm, storage, source,
+    zlist, itable, tables, sides, vtables, by_face, near_cells, far_cells, z_cells,
+    near_send, near_recv, z_send, z_recv, far_send, far_recv, terms_send, terms_recv, far_next,
+    near_sems, z_sems, far_sems,
     a_send, a_recv, b_send, b_recv, a_send_sem, a_recv_sem, b_send_sem, b_recv_sem,
 ):
     region, sub = lax.axis_index("region"), lax.axis_index("sub")
@@ -95,7 +97,8 @@
     core, deep = lax.rem(sub, 2), lax.rem(lax.div(sub, 2), 2)
     flat_me = lax.div(sub, 4) * 2 + core
     deep_me = deep * n_region + region
-    sub_up, sub_down = lax.rem(sub + 1, n_sub), lax.rem(sub + n_sub - 1, n_sub)
+    upper = core == 1
+    far_peer, near_peer = lax.rem(sub + n_sub + 2 * core - 1, n_sub), sub + 1 - 2 * core
     region_up, region_down = lax.rem(region + 1, n_region), lax.rem(region + n_region - 1, n_region)
 
     def flat_peer(offset):
@@ -111,12 +114,24 @@
     def greet(device):
         pl.semaphore_signal(barrier, inc=1, device_id=device, device_id_type=MESH)
 
-    greet((region, sub_up))
-    greet((region, sub_down))
+    greet((region, far_peer))
+    for j in sorted(range(1, n_deep), key=lambda j: -min(j, n_deep - j)):
+        greet(deep_peer(j))
     for j in range(1, n_flat):
         greet(flat_peer(j))
-    for j in range(1, n_deep):
-        greet(deep_peer(j))
+
+    def lanes(i):
+        return slice(LANES * i, LANES * (i + 1))
+
+    for there, here in (
+        (conn_y_in, conn_y), (conn_z_in, conn_z), (conn_x_in, conn_x),
+        (storage_in, storage), (source_in, source),
+    ):
+        for i in range(ROWS):
+            here[2 * i : 2 * i + 2, :] = there[:, lanes(i)]
+    for c in range(2):
+        for i in range(ROWS):
+            perm[pl.ds(2 * i + c, 3, stride=32), :] = perm_in[c, :, lanes(i)]
 
     def pair(ref, first=0):
         return [ref[pl.ds(first + k, ROWS, stride=2), :] for k in range(2)]
@@ -163,54 +178,100 @@
     up_z_cells = at_face(5, zlist[0:1, :])
     down_z_cells = itable[4, ROWS : ROWS + 1, :]
 
+    def by_core(if_upper, if_lower):
+        return jnp.where(upper, if_upper, if_lower)
+
+    for c in range(2):
+        far_cells[4 * c : 4 * c + 4, :] = by_core(up_y_cells, down_y_cells)
+        near_cells[4 * c : 4 * c + 4, :] = by_core(down_y_cells, up_y_cells)
+        z_cells[c : c + 1, :] = up_z_cells
+        z_cells[2 + c : 3 + c, :] = down_z_cells
+
+    def remote(send, recv, sems, device):
+        return pltpu.make_async_remote_copy(
+            src_ref=send,
+            dst_ref=recv,
+            send_sem=sems.at[0],
+            recv_sem=sems.at[1],
+            device_id=device,
+            device_id_type=MESH,
+        )
+
     def copies(step):
-        def one(kind, send, recv, device):
-            return pltpu.make_async_remote_copy(
-                src_ref=send,
-                dst_ref=recv,
-                send_sem=halo_send_sem.at[step, kind],
-                recv_sem=halo_recv_sem.at[step, kind],
-                device_id=device,
-                device_id_type=MESH,
-            )
-
+        near, along = near_sems.at[step], z_sems.at[step]
         return [
-            one(0, y_send.at[step, 0], y_recv.at[step, 0], (region, sub_up)),
-            one(1, y_send.at[step, 1], y_recv.at[step, 1], (region, sub_down)),
-            one(2, z_send.at[step, 0], z_recv.at[step, 0], (region_up, sub)),
-            one(3, z_send.at[step, 1], z_recv.at[step, 1], (region_down, sub)),
+            remote(near_send.at[step], near_recv.at[step], near, (region, near_peer)),
+            remote(z_send.at[step, 0], z_recv.at[step, 0], along.at[0], (region_up, sub)),
+            remote(z_send.at[step, 1], z_recv.at[step, 1], along.at[1], (region_down, sub)),
         ]
 
-    def publish(step, g, wait_first=None):
+    far_first = remote(
+        far_send.at[0, pl.ds(0, 8)], far_recv.at[0, pl.ds(0, 8)], far_sems.at[0], (region, far_peer)
+    )
+    far_second = remote(far_send.at[1], far_recv.at[1], far_sems.at[1], (region, far_peer))
+    far_terms = remote(terms_send, terms_recv, far_sems.at[2], (region, far_peer))
+
+    def side_values(at, cells, pair):
+        for c in range(2):
+            sides[at + c, 0:ROWS, :] = pair[c]
+        second = iota((8, LANES), 0) >= 4
+        rows = [
+            (h, jnp.where(second, sides[at + 1, h : h + 1, :], sides[at, h : h + 1, :]))
+            for h in range(ROWS)
+        ]
+        return lookup(rows, cells[...])
+
+    def fill_far(step, g):
+        pair = [by_core(g[c][1][1], g[c][1][0]) for c in range(2)]
+        far_send[step, 0:8, :] = side_values(0, far_cells, pair)
+
+    def fill_near(step, g):
+        pair = [by_core(g[c][1][0], g[c][1][1]) for c in range(2)]
+        near_send[step] = side_values(2, near_cells, pair)
+        for s in range(2):
+            for c in range(2):
+                sides[4, pl.ds(2 - 2 * s + c, ROWS, stride=4), :] = g[c][2][s]
+        rows = [(h, sides[4, 4 * h : 4 * h + 4, :]) for h in range(ROWS)]
+        z_rows = lookup(rows, z_cells[0:4, :])
+        z_send[step, 0] = z_rows[0:2]
+        z_send[step, 1] = z_rows[2:4]
+
+    def start(step):
+        for copy in copies(step):
+            copy.start()
+
+    def keep(g):
         for d in (1, 2, 0):
             for c in range(2):
                 for s in range(2):
                     tables[c * 6 + d * 2 + s] = g[c][d][s]
-        for c in range(2):
-            here = 4 * c
-            y_send[step, 0, here : here + 4, :] = lookup(table(tables.at[c * 6 + 3]), up_y_cells)
-            y_send[step, 1, here : here + 4, :] = lookup(table(tables.at[c * 6 + 2]), down_y_cells)
-            z_send[step, 0, c : c + 1, :] = lookup(table(tables.at[c * 6 + 5]), up_z_cells)
-            z_send[step, 1, c : c + 1, :] = lookup(table(tables.at[c * 6 + 4]), down_z_cells)
-        if wait_first is not None:
-            wait_first()
-        for copy in copies(step):
-            copy.start()
-
-    greetings = 2 + (n_flat - 1) + (n_deep - 1)
-    publish(0, rhs_g, lambda: pl.semaphore_wait(barrier, greetings))
+
+    greetings = 1 + (n_flat - 1) + (n_deep - 1)
+    fill_far(0, rhs_g)
+    fill_near(0, rhs_g)
+    pl.semaphore_wait(barrier, greetings)
+    far_first.start()
+    start(0)
+    keep(rhs_g)
+    terms_send[0:8, :] = side_values(5, far_cells, [trans[c][1] for c in range(2)])
+    terms_send[8:16, :] = side_values(7, far_cells, (solve_00, solve_01))
+    terms_send[16:24, :] = side_values(9, far_cells, (solve_11, solve_11))
+    far_terms.start()
 
     itable[0] = inverse([(conn_x, 0, 2, ROWS, 0)])
     itable[1] = inverse([(conn_x, 1, 2, ROWS, 0)])
     faces_x, faces_y, faces_z = pair(conn_x), pair(conn_y), pair(conn_z)
     up = [at_face(0, faces_x[1], 17), at_face(2, faces_y[1]), at_face(4, faces_z[1])]
     down = [at_face(1, faces_x[0], 17), own(3, faces_y[0]), own(5, faces_z[0])]
-    last_y, last_z = sub == n_sub - 1, region == n_region - 1
-    up[1] = jnp.where(jnp.logical_and(up[1] >= E_DEV, last_y), -1, up[1])
+    last_z = region == n_region - 1
     up[2] = jnp.where(jnp.logical_and(up[2] >= E_DEV, last_z), -1, up[2])
     first_y = jnp.logical_and(down[1] >= E_DEV, sub == 0)
     first_z = jnp.logical_and(down[2] >= E_DEV, region == 0)
     lone_x = down[0] < 0
+    far_index = by_core(up[1], down[1]) - E_DEV
+    near_index = by_core(down[1], up[1]) - E_DEV
+    at_far = far_index >= 0
+    far_index = jnp.where(sub == n_sub - 1, -1, far_index)
 
     def assemble(step, g):
         out = [[[None, None] for _ in range(3)] for _ in range(2)]
@@ -222,15 +283,20 @@
         for copy in copies(step):
             copy.wait_recv()
         for c in range(2):
-            from_below_y = table(y_recv.at[step, 0, pl.ds(4 * c, 4)], 4, ROWS)
-            from_above_y = table(y_recv.at[step, 1, pl.ds(4 * c, 4)], 4, ROWS)
+            near = lookup(table(near_recv.at[step, pl.ds(4 * c, 4)], 4), near_index)
+            out[c][1][1] = out[c][1][1] + by_core(0.0, near)
+            out[c][1][0] = out[c][1][0] + by_core(near, 0.0)
             from_below_z = table(z_recv.at[step, 0, pl.ds(c, 1)], 1, ROWS)
             from_above_z = table(z_recv.at[step, 1, pl.ds(c, 1)], 1, ROWS)
-            out[c][1][1] = out[c][1][1] + lookup(from_above_y, up[1])
             out[c][2][1] = out[c][2][1] + lookup(from_above_z, up[2])
-            out[c][1][0] = jnp.where(first_y, 0.0, out[c][1][0] + lookup(from_below_y, down[1]))
             out[c][2][0] = jnp.where(first_z, 0.0, out[c][2][0] + lookup(from_below_z, down[2]))
         return out
+
+    def add_far(out, rows):
+        for c in range(2):
+            far = lookup(table(rows.at[pl.ds(4 * c, 4)], 4), far_index)
+            out[c][1][1] = out[c][1][1] + by_core(far, 0.0)
+            out[c][1][0] = jnp.where(first_y, 0.0, out[c][1][0] + by_core(0.0, far))
 
     def by_faces(number, v):
         for c in range(2):
@@ -288,22 +354,50 @@
         return jnp.sum(b_recv[k], axis=0, keepdims=True)
 
     b = assemble(0, rhs_g)
+    far_first.wait_recv()
+    add_far(b, far_recv.at[0])
 
     load_b = face_load(b)
     inside_b = solve(load_b)
     g_b = contributions(b, inside_b)
-    publish(1, g_b)
+    fill_near(1, g_b)
+    start(1)
+    keep(g_b)
+    fill_far(1, g_b)
     flat_start(0, total_row([inner(b, b), energy(b, load_b, inside_b)]))
+    w = assemble(1, g_b)
+
+    def without_far(part, here):
+        return jnp.where(jnp.logical_and(at_far, here), 0.0, part)
+
+    apart = [
+        [w[c][0], [without_far(w[c][1][0], core == 0), without_far(w[c][1][1], upper)], w[c][2]]
+        for c in range(2)
+    ]
+    far_send[1, 8:16, :] = side_values(0, far_cells, face_load(apart))
+    far_second.start()
     by_faces(0, b)
-    w = assemble(1, g_b)
+    deep_start(0, flat_done(0))
+    far_terms.wait_recv()
+    far_second.wait_recv()
+    add_far(w, far_recv.at[1])
+
+    far_w = far_send[1, 0:8, :] + far_recv[1, 0:8, :]
+    far_trans = terms_recv[0:8, :]
+    far_load = far_recv[1, 8:16, :] + far_trans * far_w
+    load_0, load_1 = far_load[0:4], far_load[4:8]
+    term_00, term_01, term_11 = (terms_recv[k : k + 4, :] for k in (8, 12, 16))
+    far_next[0:4, :] = far_trans[0:4] * (far_w[0:4] - (term_00 * load_0 + term_01 * load_1))
+    far_next[4:8, :] = far_trans[4:8] * (far_w[4:8] - (term_01 * load_0 + term_11 * load_1))
 
     load_w = face_load(w)
     inside_w = solve(load_w)
     g_w = contributions(w, inside_w)
-    publish(2, g_w)
-    deep_start(0, flat_done(0))
-    by_faces(1, w)
+    fill_near(2, g_w)
+    start(2)
+    keep(g_w)
     ww = assemble(2, g_w)
+    add_far(ww, far_next)
 
     first = deep_done(0)
     norm_0 = pick(first, 0)
@@ -322,11 +416,14 @@
     load_ww = face_load(ww)
     inside_ww = solve(load_ww)
     g_ww = contributions(ww, inside_ww)
+    by_faces(1, w)
+    deep_start(1, flat_done(1))
     by_faces(2, ww)
-    deep_start(1, flat_done(1))
     for step in range(ROUNDS):
         for copy in copies(step):
             copy.wait_send()
+    for copy in (far_first, far_second, far_terms):
+        copy.wait_send()
     drain(a_recv.at[0], a_send_sem.at[0], n_flat)
     drain(b_recv.at[0], b_send_sem.at[0], n_deep)
     drain(a_recv.at[1], a_send_sem.at[1], n_flat)
@@ -362,10 +459,6 @@
     drain(b_recv.at[1], b_send_sem.at[1], n_deep)
 
 
-def pair_rows(array):
-    return array.reshape(2, ROWS, LANES).transpose(1, 0, 2).reshape(2 * ROWS, LANES)
-
-
 def solution(mesh):
     n_region, n_sub = mesh.shape["region"], mesh.shape["sub"]
     n_flat, n_deep = n_sub // 2, 2 * n_region
@@ -373,7 +466,6 @@
     def local(conn_x, conn_y, conn_z, send_y, send_z, perm, storage, sigma, source):
         vmem = pl.BlockSpec(memory_space=pltpu.VMEM)
         dma = pltpu.SemaphoreType.DMA
-        sides = perm.transpose(1, 0, 2).reshape(3, 2, ROWS, LANES).transpose(0, 2, 1, 3)
         trace, pressure, flux = pl.pallas_call(
             functools.partial(kernel, n_region, n_sub),
             out_shape=(
@@ -384,17 +476,33 @@
             in_specs=[vmem] * 9,
             out_specs=(vmem,) * 3,
             scratch_shapes=[
+                pltpu.VMEM((2 * ROWS, LANES), I32),
+                pltpu.VMEM((2 * ROWS, LANES), I32),
+                pltpu.VMEM((2 * ROWS, LANES), I32),
+                pltpu.VMEM((6 * ROWS, LANES), F32),
+                pltpu.VMEM((2 * ROWS, LANES), F32),
+                pltpu.VMEM((2 * ROWS, LANES), F32),
                 pltpu.VMEM((8, LANES), I32),
                 pltpu.VMEM((6, 24, LANES), I32),
                 pltpu.VMEM((12, ROWS, LANES), F32),
+                pltpu.VMEM((11, 4 * ROWS, LANES), F32),
                 pltpu.VMEM((3, 8, ROWS, LANES), F32),
                 pltpu.VMEM((3, 104, LANES), F32),
-                pltpu.VMEM((ROUNDS, 2, 8, LANES), F32),
-                pltpu.VMEM((ROUNDS, 2, 8, LANES), F32),
+                pltpu.VMEM((8, LANES), I32),
+                pltpu.VMEM((8, LANES), I32),
+                pltpu.VMEM((8, LANES), I32),
+                pltpu.VMEM((ROUNDS, 8, LANES), F32),
+                pltpu.VMEM((ROUNDS, 8, LANES), F32),
                 pltpu.VMEM((ROUNDS, 2, 2, LANES), F32),
                 pltpu.VMEM((ROUNDS, 2, 2, LANES), F32),
-                dma((ROUNDS, 4)),
-                dma((ROUNDS, 4)),
+                pltpu.VMEM((2, 16, LANES), F32),
+                pltpu.VMEM((2, 16, LANES), F32),
+                pltpu.VMEM((24, LANES), F32),
+                pltpu.VMEM((24, LANES), F32),
+                pltpu.VMEM((8, LANES), F32),
+                dma((ROUNDS, 2)),
+                dma((ROUNDS, 2, 2)),
+                dma((3, 2)),
                 pltpu.VMEM((2, 8, LANES), F32),
                 pltpu.VMEM((2, n_flat, LANES), F32),
                 pltpu.VMEM((2, 8, LANES), F32),
@@ -408,10 +516,8 @@
                 collective_id=0, has_side_effects=True, vmem_limit_bytes=32 * 1024 * 1024
             ),
         )(
-            pair_rows(conn_x), pair_rows(conn_y), pair_rows(conn_z),
-            send_y.reshape(4, LANES), send_z.reshape(1, 64),
-            sides.reshape(6 * ROWS, LANES), pair_rows(storage), sigma.reshape(ROWS, LANES),
-            pair_rows(source),
+            conn_x, conn_y, conn_z, send_y.reshape(4, LANES), send_z.reshape(1, 64),
+            perm, storage, sigma.reshape(ROWS, LANES), source,
         )
         pressure = pressure.reshape(ROWS, 2, LANES).transpose(1, 0, 2).reshape(2, E_DEV)
         flux = flux.reshape(6, ROWS, 2, LANES).transpose(2, 0, 1, 3).reshape(2, 6, E_DEV)

time: 65.7 us -> 59.5 us (0.906)
  local copies, waits for them, and re-layouts: 7.62 us -> 2.78 us
  Pallas kernels: 56.8 us -> 55.7 us
    unnamed x21 -> x20, local copies, waits for them, and re-layouts: 7.62 us -> 2.78 us
    pallas_call x1, Pallas kernels: 56.8 us -> 55.7 us  [local(): pl.pallas_call(functools.partial(kernel, n_region, n_sub), out_shape=(jax...]
where the time goes in v5:
time: 59.5 us; the launch traced here: 59.3 us
  Pallas kernels  55.7 us (94%)
  local copies, waits for them, and re-layouts  2.78 us (5%)
  between operations  0.77 us (1%)
    pallas_call x1, Pallas kernels, local(): pl.pallas_call(functools.partial(kernel, n_region, n_sub), out_shape=(jax...  55.7 us
    unnamed x20, local copies, waits for them, and re-layouts  2.78 us

profile of v5, /device:TPU:1, one launch (start us, length us, event | category | flops | bytes accessed | tf_op | source)
XLA Modules:
  0.0 59.3 jit_solution(5676075209314430686)
XLA Ops:
  0.6 0.0 copy-start
  0.6 0.0 copy-start.1
  0.7 0.0 copy-start.2
  0.7 0.0 copy-start.3
  0.7 0.0 copy-start.4
  0.7 0.0 copy-start.5
  0.7 0.0 copy-start.6
  0.7 0.0 copy-start.7
  0.7 0.9 %copy.12.perm_in = f32[2,3,2048]{2,1,0:T(4,128)S(1)} copy(f32[2,3,2048]{2,0,1:T(2,128)} %param.14) | data formatting | bytes 98304 | tf_op args[5]
  1.6 0.0 copy-done
  1.6 0.0 copy-done.1
  1.6 0.0 copy-done.2
  1.6 0.0 copy-done.3
  1.6 0.0 copy-done.4
  1.6 0.0 copy-done.5
  1.7 0.0 copy-done.6
  1.7 0.0 copy-done.7
  1.7 55.7 %shard_map.112 = (f32[2,6272]{1,0:T(2,128)S(1)}, f32[32,128]{1,0:T(8,128)S(1)}, f32[192,128]{1,0:T(8,128)S(1)}) custom-call(s32[2,2048]{1,0:T(2,128)S(1)} %copy-done, s32[2,2048]{1,0:T(2,128)S(1)} %copy-done.1, s32[2,2048]{1,0:T(2,128)S(1)} %copy-done.2, s32[4,128]{1,0:T(4,128)S(1)} %bitcast.16, s32[1,64]{1,0:T(1,128)S(1)} %bitcast.17, ...), custom_call_target="tpu_custom_call" | custom-call | tf_op jit(solution)/shard_map/pallas_call | solution.py:469
  57.4 0.6 %copy.18 = f32[2,6272]{1,0:T(2,128)} copy(f32[2,6272]{1,0:T(2,128)S(1)} %get-tuple-element.12) | data formatting | bytes 100352
  58.1 0.6 %copy.19 = f32[2,2048]{1,0:T(2,128)} copy(f32[2,2048]{1,0:T(2,128)S(1)} %bitcast.14) | data formatting | bytes 32768
  58.7 0.6 %copy.20 = f32[2,6,2048]{2,0,1:T(2,128)} copy(f32[2,6,2048]{2,0,1:T(2,128)S(1)} %bitcast.13) | data formatting | bytes 196608
Async XLA Ops:
  0.6 1.0 %copy-start = (s32[2,2048]{1,0:T(2,128)S(1)}, s32[2,2048]{1,0:T(2,128)}, u32[]{:S(2)}) copy-start(s32[2,2048]{1,0:T(2,128)} %conn_x_in.1) | copy-start | bytes 49156
  0.6 1.0 %copy-start.1 = (s32[2,2048]{1,0:T(2,128)S(1)}, s32[2,2048]{1,0:T(2,128)}, u32[]{:S(2)}) copy-start(s32[2,2048]{1,0:T(2,128)} %conn_y_in.1) | copy-start | bytes 49156
  0.7 1.0 %copy-start.2 = (s32[2,2048]{1,0:T(2,128)S(1)}, s32[2,2048]{1,0:T(2,128)}, u32[]{:S(2)}) copy-start(s32[2,2048]{1,0:T(2,128)} %conn_z_in.1) | copy-start | bytes 49156
  0.7 1.0 %copy-start.3 = (f32[2,2048]{1,0:T(2,128)S(1)}, f32[2,2048]{1,0:T(2,128)}, u32[]{:S(2)}) copy-start(f32[2,2048]{1,0:T(2,128)} %storage_in.1) | copy-start | bytes 49156
  0.7 1.0 %copy-start.4 = (f32[2,2048]{1,0:T(2,128)S(1)}, f32[2,2048]{1,0:T(2,128)}, u32[]{:S(2)}) copy-start(f32[2,2048]{1,0:T(2,128)} %source_in.1) | copy-start | bytes 49156
  0.7 1.0 %copy-start.5 = (f32[2048]{0:T(1024)S(1)}, f32[2048]{0:T(1024)}, u32[]{:S(2)}) copy-start(f32[2048]{0:T(1024)} %param.16) | copy-start | bytes 24580
  0.7 1.0 %copy-start.6 = (s32[512]{0:T(512)S(1)}, s32[512]{0:T(512)}, u32[]{:S(2)}) copy-start(s32[512]{0:T(512)} %param.12) | copy-start | bytes 6148
  0.7 1.0 %copy-start.7 = (s32[64]{0:T(128)S(1)}, s32[64]{0:T(128)}, u32[]{:S(2)}) copy-start(s32[64]{0:T(128)} %param.13) | copy-start | bytes 772

commit v6 on v5

--- a/solution.py
+++ b/solution.py
@@ -21,23 +21,28 @@
     return lax.broadcasted_iota(I32, shape, dim)
 
 
-def inverse(pieces):
-    total = None
-    for ref, row, stride, count, first in pieces:
-        for start in range(0, count, 2):
-            spots, hits = [], []
-            for i in range(start, min(start + 2, count)):
-                face = ref[row + stride * i : row + stride * i + 1, :]
-                cell = iota((1, LANES), 1) + (first + LANES * i)
-                spots.append(jnp.where(iota((LANES, LANES), 0) == (face & 127), 1.0, 0.0))
-                hit = iota((24, LANES), 0) == (face >> 7)
-                low = jnp.where(hit, (cell & 127).astype(F32), 0.0)
-                high = jnp.where(hit, ((cell >> 7) + 1).astype(F32), 0.0)
-                hits.append(jnp.concatenate([low, high], axis=0))
-            left = jnp.concatenate(hits, axis=1).astype(jnp.bfloat16)
-            spot = jnp.concatenate(spots, axis=1).astype(jnp.bfloat16)
-            part = lax.dot_general(left, spot, (((1,), (1,)), ((), ())), preferred_element_type=F32)
-            total = part if total is None else total + part
+def inverse(ref, side, more=()):
+    def columns(face, number):
+        spot = jnp.where(iota((LANES, LANES), 0) == (face & 127), 1.0, 0.0)
+        hit = iota((24, LANES), 0) == (face >> 7)
+        low = jnp.where(hit, iota((1, LANES), 1).astype(F32), 0.0)
+        high = jnp.where(hit, (number + 1).astype(F32), 0.0)
+        return jnp.concatenate([low, high], axis=0), spot
+
+    def part(pairs):
+        left = jnp.concatenate([pair[0] for pair in pairs], axis=1).astype(jnp.bfloat16)
+        right = jnp.concatenate([pair[1] for pair in pairs], axis=1).astype(jnp.bfloat16)
+        return lax.dot_general(left, right, (((1,), (1,)), ((), ())), preferred_element_type=F32)
+
+    def step(i, total):
+        rows = [4 * i + u for u in range(4)]
+        return total + part([columns(ref[pl.ds(2 * r + side, 1), :], r) for r in rows])
+
+    total = lax.fori_loop(0, ROWS // 4, step, jnp.zeros((48, LANES), F32))
+    for other, count in more:
+        total = total + part(
+            [columns(other[h : h + 1, :], jnp.int32(ROWS + h)) for h in range(count)]
+        )
     whole = total.astype(I32)
     return (whole[24:] - 1) * 128 + whole[:24]
 
@@ -63,6 +68,23 @@
         found = lane_gather(wide, lane)
         out = jnp.where(high == number, found, jnp.zeros_like(found) if out is None else out)
     return out
+
+
+def lookup_all(jobs, missing):
+    lanes = [index & 127 for _, index in jobs]
+    highs = [index >> 7 for _, index in jobs]
+
+    def step(i, found):
+        for u in range(4):
+            row = 4 * i + u
+            values = [
+                lane_gather(jnp.broadcast_to(ref[pl.ds(row, 1), :], index.shape), lane)
+                for (ref, index), lane in zip(jobs, lanes)
+            ]
+            found = [jnp.where(high == row, v, f) for high, v, f in zip(highs, values, found)]
+        return found
+
+    return lax.fori_loop(0, ROWS // 4, step, [jnp.full(i.shape, missing, r.dtype) for r, i in jobs])
 
 
 def table(ref, count=ROWS, first=0):
@@ -115,10 +137,8 @@
         pl.semaphore_signal(barrier, inc=1, device_id=device, device_id_type=MESH)
 
     greet((region, far_peer))
-    for j in sorted(range(1, n_deep), key=lambda j: -min(j, n_deep - j)):
-        greet(deep_peer(j))
-    for j in range(1, n_flat):
-        greet(flat_peer(j))
+    lax.fori_loop(1, n_deep, lambda j, c: (greet(deep_peer(j)), c)[1], 0)
+    lax.fori_loop(1, n_flat, lambda j, c: (greet(flat_peer(j)), c)[1], 0)
 
     def lanes(i):
         return slice(LANES * i, LANES * (i + 1))
@@ -164,15 +184,12 @@
     def at_face(which, face, count=ROWS):
         return lookup(table(itable.at[which], count), face, jnp.full(face.shape, -1, I32))
 
-    def own(which, face):
-        return jnp.where(face >= E_DEV, face, at_face(which, face))
-
     zlist[0:1, :] = jnp.full((1, LANES), -1, I32)
     zlist[0:1, 0:64] = send_z[...]
-    itable[2] = inverse([(conn_y, 0, 2, ROWS, 0), (send_y, 0, 1, 4, E_DEV)])
-    itable[3] = inverse([(conn_y, 1, 2, ROWS, 0)])
-    itable[4] = inverse([(conn_z, 0, 2, ROWS, 0), (zlist, 0, 1, 1, E_DEV)])
-    itable[5] = inverse([(conn_z, 1, 2, ROWS, 0)])
+    itable[2] = inverse(conn_y, 0, [(send_y, 4)])
+    itable[3] = inverse(conn_y, 1)
+    itable[4] = inverse(conn_z, 0, [(zlist, 1)])
+    itable[5] = inverse(conn_z, 1)
     up_y_cells = at_face(3, send_y[...])
     down_y_cells = itable[2, ROWS : ROWS + 4, :]
     up_z_cells = at_face(5, zlist[0:1, :])
@@ -258,11 +275,16 @@
     terms_send[16:24, :] = side_values(9, far_cells, (solve_11, solve_11))
     far_terms.start()
 
-    itable[0] = inverse([(conn_x, 0, 2, ROWS, 0)])
-    itable[1] = inverse([(conn_x, 1, 2, ROWS, 0)])
+    itable[0] = inverse(conn_x, 0)
+    itable[1] = inverse(conn_x, 1)
     faces_x, faces_y, faces_z = pair(conn_x), pair(conn_y), pair(conn_z)
-    up = [at_face(0, faces_x[1], 17), at_face(2, faces_y[1]), at_face(4, faces_z[1])]
-    down = [at_face(1, faces_x[0], 17), own(3, faces_y[0]), own(5, faces_z[0])]
+    asked = (faces_x[1], faces_y[1], faces_z[1], faces_x[0], faces_y[0], faces_z[0])
+    found = lookup_all([(itable.at[k], face) for k, face in zip((0, 2, 4, 1, 3, 5), asked)], -1)
+    up, down = list(found[:3]), list(found[3:])
+    up[0] = lookup([(16, itable[0, 16:17, :])], asked[0], up[0])
+    down[0] = lookup([(16, itable[1, 16:17, :])], asked[3], down[0])
+    down[1] = jnp.where(asked[4] >= E_DEV, asked[4], down[1])
+    down[2] = jnp.where(asked[5] >= E_DEV, asked[5], down[2])
     last_z = region == n_region - 1
     up[2] = jnp.where(jnp.logical_and(up[2] >= E_DEV, last_z), -1, up[2])
     first_y = jnp.logical_and(down[1] >= E_DEV, sub == 0)
@@ -275,11 +297,14 @@
 
     def assemble(step, g):
         out = [[[None, None] for _ in range(3)] for _ in range(2)]
+        across = lookup_all(
+            [(tables.at[k], (up if k % 2 == 0 else down)[k % 6 // 2]) for k in range(12)], 0.0
+        )
         for c in range(2):
             for d in range(3):
                 at = c * 6 + d * 2
-                out[c][d][1] = g[c][d][1] + lookup(table(tables.at[at]), up[d])
-                out[c][d][0] = g[c][d][0] + lookup(table(tables.at[at + 1]), down[d])
+                out[c][d][1] = g[c][d][1] + across[at]
+                out[c][d][0] = g[c][d][0] + across[at + 1]
         for copy in copies(step):
             copy.wait_recv()
         for c in range(2):
@@ -299,15 +324,20 @@
             out[c][1][0] = jnp.where(first_y, 0.0, out[c][1][0] + by_core(0.0, far))
 
     def by_faces(number, v):
+        jobs = []
         for c in range(2):
             parts = (v[c][0][0], v[c][0][1], v[c][1][1], v[c][2][1])
             for k, part in enumerate(parts):
                 vtables[number, c * 4 + k] = part
-            x_low, x_up, y_up, z_up = (table(vtables.at[number, c * 4 + k]) for k in range(4))
-            by_x = jnp.where(itable[1] < 0, lookup(x_low, itable[0]), lookup(x_up, itable[1]))
+                index = (itable[0], itable[1], itable[3, 0:ROWS, :], itable[5, 0:ROWS, :])[k]
+                jobs.append((vtables.at[number, c * 4 + k], index))
+        found = lookup_all(jobs, 0.0)
+        for c in range(2):
+            x_low, x_up, y_up, z_up = found[4 * c : 4 * c + 4]
+            by_x = jnp.where(itable[1] < 0, x_low, x_up)
             by_face[number, pl.ds(c, 17, stride=2), :] = by_x[0:17]
-            by_face[number, pl.ds(34 + c, ROWS, stride=2), :] = lookup(y_up, itable[3, 0:ROWS, :])
-            by_face[number, pl.ds(66 + c, ROWS, stride=2), :] = lookup(z_up, itable[5, 0:ROWS, :])
+            by_face[number, pl.ds(34 + c, ROWS, stride=2), :] = y_up
+            by_face[number, pl.ds(66 + c, ROWS, stride=2), :] = z_up
 
     def inner(u, v):
         total = sum(u[c][d][1] * v[c][d][1] for c in range(2) for d in range(3))
@@ -325,7 +355,8 @@
     def scatter(send, recv, send_sem, recv_sem, peer, count, row):
         send[0:1, :] = row
         recv[count - 1 : count, :] = row
-        for j in range(1, count):
+
+        def one(j, carry):
             pltpu.make_async_remote_copy(
                 src_ref=send.at[pl.ds(0, 1)],
                 dst_ref=recv.at[pl.ds(j - 1, 1)],
@@ -334,6 +365,9 @@
                 device_id=peer(j),
                 device_id_type=MESH,
             ).start()
+            return carry
+
+        lax.fori_loop(1, count, one, 0)
 
     def drain(buffer, sem, count):
         rows = buffer.at[pl.ds(0, count - 1)]

time: 59.5 us -> 59.6 us (level)
  no operation moved by 1% of the time
where the time goes in v6:
time: 59.6 us; the launch traced here: 59.3 us
  Pallas kernels  55.7 us (93%)
  local copies, waits for them, and re-layouts  2.78 us (5%)
  between operations  0.77 us (1%)
    pallas_call x1, Pallas kernels, local(): pl.pallas_call(functools.partial(kernel, n_region, n_sub), out_shape=(jax...  55.7 us
    unnamed x20, local copies, waits for them, and re-layouts  2.78 us

profile of v6, /device:TPU:1, one launch (start us, length us, event | category | flops | bytes accessed | tf_op | source)
XLA Modules:
  0.0 59.3 jit_solution(15674619598537481272)
XLA Ops:
  0.6 0.0 copy-start
  0.6 0.0 copy-start.1
  0.7 0.0 copy-start.2
  0.7 0.0 copy-start.3
  0.7 0.0 copy-start.4
  0.7 0.0 copy-start.5
  0.7 0.0 copy-start.6
  0.7 0.0 copy-start.7
  0.7 0.9 %copy.12.perm_in = f32[2,3,2048]{2,1,0:T(4,128)S(1)} copy(f32[2,3,2048]{2,0,1:T(2,128)} %param.14) | data formatting | bytes 98304 | tf_op args[5]
  1.6 0.0 copy-done
  1.6 0.0 copy-done.1
  1.6 0.0 copy-done.2
  1.6 0.0 copy-done.3
  1.6 0.0 copy-done.4
  1.6 0.0 copy-done.5
  1.7 0.0 copy-done.6
  1.7 0.0 copy-done.7
  1.7 55.7 %shard_map.112 = (f32[2,6272]{1,0:T(2,128)S(1)}, f32[32,128]{1,0:T(8,128)S(1)}, f32[192,128]{1,0:T(8,128)S(1)}) custom-call(s32[2,2048]{1,0:T(2,128)S(1)} %copy-done, s32[2,2048]{1,0:T(2,128)S(1)} %copy-done.1, s32[2,2048]{1,0:T(2,128)S(1)} %copy-done.2, s32[4,128]{1,0:T(4,128)S(1)} %bitcast.16, s32[1,64]{1,0:T(1,128)S(1)} %bitcast.17, ...), custom_call_target="tpu_custom_call" | custom-call | tf_op jit(solution)/shard_map/pallas_call | solution.py:503
  57.4 0.6 %copy.18 = f32[2,6272]{1,0:T(2,128)} copy(f32[2,6272]{1,0:T(2,128)S(1)} %get-tuple-element.12) | data formatting | bytes 100352
  58.0 0.6 %copy.19 = f32[2,2048]{1,0:T(2,128)} copy(f32[2,2048]{1,0:T(2,128)S(1)} %bitcast.14) | data formatting | bytes 32768
  58.6 0.6 %copy.20 = f32[2,6,2048]{2,0,1:T(2,128)} copy(f32[2,6,2048]{2,0,1:T(2,128)S(1)} %bitcast.13) | data formatting | bytes 196608
Async XLA Ops:
  0.6 1.0 %copy-start = (s32[2,2048]{1,0:T(2,128)S(1)}, s32[2,2048]{1,0:T(2,128)}, u32[]{:S(2)}) copy-start(s32[2,2048]{1,0:T(2,128)} %conn_x_in.1) | copy-start | bytes 49156
  0.6 1.0 %copy-start.1 = (s32[2,2048]{1,0:T(2,128)S(1)}, s32[2,2048]{1,0:T(2,128)}, u32[]{:S(2)}) copy-start(s32[2,2048]{1,0:T(2,128)} %conn_y_in.1) | copy-start | bytes 49156
  0.7 1.0 %copy-start.2 = (s32[2,2048]{1,0:T(2,128)S(1)}, s32[2,2048]{1,0:T(2,128)}, u32[]{:S(2)}) copy-start(s32[2,2048]{1,0:T(2,128)} %conn_z_in.1) | copy-start | bytes 49156
  0.7 1.0 %copy-start.3 = (f32[2,2048]{1,0:T(2,128)S(1)}, f32[2,2048]{1,0:T(2,128)}, u32[]{:S(2)}) copy-start(f32[2,2048]{1,0:T(2,128)} %storage_in.1) | copy-start | bytes 49156
  0.7 1.0 %copy-start.4 = (f32[2,2048]{1,0:T(2,128)S(1)}, f32[2,2048]{1,0:T(2,128)}, u32[]{:S(2)}) copy-start(f32[2,2048]{1,0:T(2,128)} %source_in.1) | copy-start | bytes 49156
  0.7 1.0 %copy-start.5 = (f32[2048]{0:T(1024)S(1)}, f32[2048]{0:T(1024)}, u32[]{:S(2)}) copy-start(f32[2048]{0:T(1024)} %param.16) | copy-start | bytes 24580
  0.7 1.0 %copy-start.6 = (s32[512]{0:T(512)S(1)}, s32[512]{0:T(512)}, u32[]{:S(2)}) copy-start(s32[512]{0:T(512)} %param.12) | copy-start | bytes 6148
  0.7 1.0 %copy-start.7 = (s32[64]{0:T(128)S(1)}, s32[64]{0:T(128)}, u32[]{:S(2)}) copy-start(s32[64]{0:T(128)} %param.13) | copy-start | bytes 772

commit v7 on v6

--- a/solution.py
+++ b/solution.py
@@ -1,4 +1,5 @@
 import functools
+import math
 
 import jax
 import jax.numpy as jnp
@@ -112,12 +113,14 @@
     zlist, itable, tables, sides, vtables, by_face, near_cells, far_cells, z_cells,
     near_send, near_recv, z_send, z_recv, far_send, far_recv, terms_send, terms_recv, far_next,
     near_sems, z_sems, far_sems,
-    a_send, a_recv, b_send, b_recv, a_send_sem, a_recv_sem, b_send_sem, b_recv_sem,
+    row_send, flat_recv, side_recv, deep_recv, sum_sems,
 ):
     region, sub = lax.axis_index("region"), lax.axis_index("sub")
-    n_flat, n_deep = n_sub // 2, 2 * n_region
+    n_side = math.isqrt(n_sub // 4)
+    n_flat, n_deep = 2 * n_side, 2 * n_region
     core, deep = lax.rem(sub, 2), lax.rem(lax.div(sub, 2), 2)
-    flat_me = lax.div(sub, 4) * 2 + core
+    place_x, place_y = lax.div(sub, 4 * n_side), lax.rem(lax.div(sub, 4), n_side)
+    flat_me = place_x * 2 + core
     deep_me = deep * n_region + region
     upper = core == 1
     far_peer, near_peer = lax.rem(sub + n_sub + 2 * core - 1, n_sub), sub + 1 - 2 * core
@@ -125,7 +128,12 @@
 
     def flat_peer(offset):
         peer = lax.rem(flat_me + offset, n_flat)
-        return (region, lax.div(peer, 2) * 4 + deep * 2 + lax.rem(peer, 2))
+        column = lax.div(peer, 2) * n_side + place_y
+        return (region, column * 4 + deep * 2 + lax.rem(peer, 2))
+
+    def side_peer(offset):
+        column = place_x * n_side + lax.rem(place_y + offset, n_side)
+        return (region, column * 4 + deep * 2 + core)
 
     def deep_peer(offset):
         peer = lax.rem(deep_me + offset, n_deep)
@@ -137,8 +145,9 @@
         pl.semaphore_signal(barrier, inc=1, device_id=device, device_id_type=MESH)
 
     greet((region, far_peer))
-    lax.fori_loop(1, n_deep, lambda j, c: (greet(deep_peer(j)), c)[1], 0)
-    lax.fori_loop(1, n_flat, lambda j, c: (greet(flat_peer(j)), c)[1], 0)
+    for peer, count in ((deep_peer, n_deep), (flat_peer, n_flat), (side_peer, n_side)):
+        for j in range(1, count):
+            greet(peer(j))
 
     def lanes(i):
         return slice(LANES * i, LANES * (i + 1))
@@ -263,7 +272,7 @@
                 for s in range(2):
                     tables[c * 6 + d * 2 + s] = g[c][d][s]
 
-    greetings = 1 + (n_flat - 1) + (n_deep - 1)
+    greetings = 1 + (n_flat - 1) + (n_deep - 1) + (n_side - 1)
     fill_far(0, rhs_g)
     fill_near(0, rhs_g)
     pl.semaphore_wait(barrier, greetings)
@@ -295,7 +304,7 @@
     at_far = far_index >= 0
     far_index = jnp.where(sub == n_sub - 1, -1, far_index)
 
-    def assemble(step, g):
+    def assemble(step, g, meanwhile=None):
         out = [[[None, None] for _ in range(3)] for _ in range(2)]
         across = lookup_all(
             [(tables.at[k], (up if k % 2 == 0 else down)[k % 6 // 2]) for k in range(12)], 0.0
@@ -305,6 +314,8 @@
                 at = c * 6 + d * 2
                 out[c][d][1] = g[c][d][1] + across[at]
                 out[c][d][0] = g[c][d][0] + across[at + 1]
+        if meanwhile is not None:
+            meanwhile(out)
         for copy in copies(step):
             copy.wait_recv()
         for c in range(2):
@@ -352,42 +363,39 @@
         )
         return total - (load[0] * solved[0] + load[1] * solved[1])
 
-    def scatter(send, recv, send_sem, recv_sem, peer, count, row):
-        send[0:1, :] = row
-        recv[count - 1 : count, :] = row
-
-        def one(j, carry):
+    stages = (
+        (flat_recv, flat_peer, n_flat), (side_recv, side_peer, n_side), (deep_recv, deep_peer, n_deep)
+    )
+
+    def sum_start(k, stage, row):
+        recv, peer, count = stages[stage]
+        row_send[k, stage, 0:1, :] = row
+        recv[k, count - 1 : count, :] = row
+        for j in sorted(range(1, count), key=lambda j: -min(j, count - j)):
             pltpu.make_async_remote_copy(
-                src_ref=send.at[pl.ds(0, 1)],
-                dst_ref=recv.at[pl.ds(j - 1, 1)],
-                send_sem=send_sem,
-                recv_sem=recv_sem,
+                src_ref=row_send.at[k, stage, pl.ds(0, 1)],
+                dst_ref=recv.at[k, pl.ds(j - 1, 1)],
+                send_sem=sum_sems.at[k, stage, 0],
+                recv_sem=sum_sems.at[k, stage, 1],
                 device_id=peer(j),
                 device_id_type=MESH,
             ).start()
-            return carry
-
-        lax.fori_loop(1, count, one, 0)
-
-    def drain(buffer, sem, count):
-        rows = buffer.at[pl.ds(0, count - 1)]
-        pltpu.make_async_copy(rows, rows, sem).wait()
-
-    def flat_start(k, row):
-        scatter(a_send.at[k], a_recv.at[k], a_send_sem.at[k], a_recv_sem.at[k], flat_peer, n_flat, row)
-
-    def flat_done(k):
-        drain(a_recv.at[k], a_recv_sem.at[k], n_flat)
-        return jnp.sum(a_recv[k], axis=0, keepdims=True)
-
-    def deep_start(k, row):
-        scatter(b_send.at[k], b_recv.at[k], b_send_sem.at[k], b_recv_sem.at[k], deep_peer, n_deep, row)
-
-    def deep_done(k):
-        drain(b_recv.at[k], b_recv_sem.at[k], n_deep)
-        return jnp.sum(b_recv[k], axis=0, keepdims=True)
-
-    b = assemble(0, rhs_g)
+
+    def drain(k, stage, which):
+        recv, _, count = stages[stage]
+        if count > 1:
+            rows = recv.at[k, pl.ds(0, count - 1)]
+            pltpu.make_async_copy(rows, rows, sum_sems.at[k, stage, which]).wait()
+
+    def sum_done(k, stage):
+        drain(k, stage, 1)
+        return jnp.sum(stages[stage][0][k], axis=0, keepdims=True)
+
+    def estimate(rough):
+        load = face_load(rough)
+        sum_start(0, 0, total_row([inner(rough, rough), energy(rough, load, solve(load))]))
+
+    b = assemble(0, rhs_g, estimate)
     far_first.wait_recv()
     add_far(b, far_recv.at[0])
 
@@ -398,7 +406,7 @@
     start(1)
     keep(g_b)
     fill_far(1, g_b)
-    flat_start(0, total_row([inner(b, b), energy(b, load_b, inside_b)]))
+    sum_start(0, 1, sum_done(0, 0))
     w = assemble(1, g_b)
 
     def without_far(part, here):
@@ -411,7 +419,7 @@
     far_send[1, 8:16, :] = side_values(0, far_cells, face_load(apart))
     far_second.start()
     by_faces(0, b)
-    deep_start(0, flat_done(0))
+    sum_start(0, 2, sum_done(0, 1))
     far_terms.wait_recv()
     far_second.wait_recv()
     add_far(w, far_recv.at[1])
@@ -433,9 +441,8 @@
     ww = assemble(2, g_w)
     add_far(ww, far_next)
 
-    first = deep_done(0)
-    norm_0 = pick(first, 0)
-    alpha_0 = norm_0 / pick(first, 1)
+    first = sum_done(0, 2)
+    scale = pick(first, 0) / pick(first, 1)
 
     def blend(u, factor, v):
         return [
@@ -443,26 +450,38 @@
             for c in range(2)
         ]
 
-    r = blend(b, alpha_0, w)
-    s = blend(w, alpha_0, ww)
+    r = blend(b, scale, w)
+    s = blend(w, scale, ww)
     load = face_load(s)
-    flat_start(1, total_row([inner(r, r), inner(r, s), inner(s, s), energy(s, load, solve(load))]))
+    parts = [inner(b, b), inner(b, r), inner(r, r), inner(r, s), inner(s, s)]
+    sum_start(1, 0, total_row([*parts, energy(s, load, solve(load))]))
     load_ww = face_load(ww)
     inside_ww = solve(load_ww)
     g_ww = contributions(ww, inside_ww)
     by_faces(1, w)
-    deep_start(1, flat_done(1))
+    sum_start(1, 1, sum_done(1, 0))
     by_faces(2, ww)
+    sum_start(1, 2, sum_done(1, 1))
     for step in range(ROUNDS):
         for copy in copies(step):
             copy.wait_send()
     for copy in (far_first, far_second, far_terms):
         copy.wait_send()
-    drain(a_recv.at[0], a_send_sem.at[0], n_flat)
-    drain(b_recv.at[0], b_send_sem.at[0], n_deep)
-    drain(a_recv.at[1], a_send_sem.at[1], n_flat)
-    sums = deep_done(1)
-    rr, rs, ss, sas = (pick(sums, k) for k in range(4))
+    for k, stage in ((0, 0), (0, 1), (0, 2), (1, 0), (1, 1)):
+        drain(k, stage, 0)
+    sums = sum_done(1, 2)
+    bb, br, rr_, rs_, ss_, sas_ = (pick(sums, k) for k in range(6))
+
+    norm_0 = bb
+    near, away = bb / (bb - br), -br / (bb - br)
+    tilt = away / scale
+    alpha_0 = scale * near
+    rr = near * (near * rr_ + away * br)
+    bs, bw = (br - rr_) / scale, bb - 2.0 * br + rr_
+    rs = near * (near * rs_ + tilt * (br - rr_)) + away * (near * bs + tilt * (bb - br))
+    ss = near * near * ss_ + 2.0 * near * tilt * (bs - rs_) + tilt * tilt * bw
+    sas = near * near * sas_ + 2.0 * near * tilt * ((bs - rs_) / scale - ss_)
+    sas = sas + tilt * tilt * (bw / scale - (bs - rs_))
 
     beta_0 = rr / norm_0
     alpha_1 = rr / (rs - beta_0 * rr / alpha_0)
@@ -490,12 +509,13 @@
     by_face[0] = on_b * by_face[0] + on_w * by_face[1] + on_ww * by_face[2]
     for i in range(49):
         trace_out[:, LANES * i : LANES * (i + 1)] = by_face[0, 2 * i : 2 * i + 2, :]
-    drain(b_recv.at[1], b_send_sem.at[1], n_deep)
+    drain(1, 2, 0)
 
 
 def solution(mesh):
     n_region, n_sub = mesh.shape["region"], mesh.shape["sub"]
-    n_flat, n_deep = n_sub // 2, 2 * n_region
+    n_side = math.isqrt(n_sub // 4)
+    n_flat, n_deep = 2 * n_side, 2 * n_region
 
     def local(conn_x, conn_y, conn_z, send_y, send_z, perm, storage, sigma, source):
         vmem = pl.BlockSpec(memory_space=pltpu.VMEM)
@@ -537,14 +557,11 @@
                 dma((ROUNDS, 2)),
                 dma((ROUNDS, 2, 2)),
                 dma((3, 2)),
-                pltpu.VMEM((2, 8, LANES), F32),
+                pltpu.VMEM((2, 3, 8, LANES), F32),
                 pltpu.VMEM((2, n_flat, LANES), F32),
-                pltpu.VMEM((2, 8, LANES), F32),
+                pltpu.VMEM((2, n_side, LANES), F32),
                 pltpu.VMEM((2, n_deep, LANES), F32),
-                dma((2,)),
-                dma((2,)),
-                dma((2,)),
-                dma((2,)),
+                dma((2, 3, 2)),
             ],
             compiler_params=pltpu.CompilerParams(
                 collective_id=0, has_side_effects=True, vmem_limit_bytes=32 * 1024 * 1024

time: 59.6 us -> 61.3 us (1.029)
  Pallas kernels: 55.7 us -> 56.9 us
    pallas_call x1, Pallas kernels: 55.7 us -> 56.9 us  [local(): pl.pallas_call(functools.partial(kernel, n_region, n_sub), out_shape=(jax...]
where the time goes in v7:
time: 61.3 us; the launch traced here: 60.5 us
  Pallas kernels  56.9 us (93%)
  local copies, waits for them, and re-layouts  2.78 us (5%)
  between operations  0.77 us (1%)
    pallas_call x1, Pallas kernels, local(): pl.pallas_call(functools.partial(kernel, n_region, n_sub), out_shape=(jax...  56.9 us
    unnamed x20, local copies, waits for them, and re-layouts  2.78 us

profile of v7, /device:TPU:1, one launch (start us, length us, event | category | flops | bytes accessed | tf_op | source)
XLA Modules:
  0.0 60.5 jit_solution(11746796334105114673)
XLA Ops:
  0.6 0.0 copy-start
  0.6 0.0 copy-start.1
  0.7 0.0 copy-start.2
  0.7 0.0 copy-start.3
  0.7 0.0 copy-start.4
  0.7 0.0 copy-start.5
  0.7 0.0 copy-start.6
  0.7 0.0 copy-start.7
  0.7 0.9 %copy.12.perm_in = f32[2,3,2048]{2,1,0:T(4,128)S(1)} copy(f32[2,3,2048]{2,0,1:T(2,128)} %param.14) | data formatting | bytes 98304 | tf_op args[5]
  1.6 0.0 copy-done
  1.6 0.0 copy-done.1
  1.6 0.0 copy-done.2
  1.6 0.0 copy-done.3
  1.6 0.0 copy-done.4
  1.6 0.0 copy-done.5
  1.7 0.0 copy-done.6
  1.7 0.0 copy-done.7
  1.7 56.9 %shard_map.112 = (f32[2,6272]{1,0:T(2,128)S(1)}, f32[32,128]{1,0:T(8,128)S(1)}, f32[192,128]{1,0:T(8,128)S(1)}) custom-call(s32[2,2048]{1,0:T(2,128)S(1)} %copy-done, s32[2,2048]{1,0:T(2,128)S(1)} %copy-done.1, s32[2,2048]{1,0:T(2,128)S(1)} %copy-done.2, s32[4,128]{1,0:T(4,128)S(1)} %bitcast.16, s32[1,64]{1,0:T(1,128)S(1)} %bitcast.17, ...), custom_call_target="tpu_custom_call" | custom-call | tf_op jit(solution)/shard_map/pallas_call | solution.py:523
  58.6 0.6 %copy.18 = f32[2,6272]{1,0:T(2,128)} copy(f32[2,6272]{1,0:T(2,128)S(1)} %get-tuple-element.12) | data formatting | bytes 100352
  59.2 0.6 %copy.19 = f32[2,2048]{1,0:T(2,128)} copy(f32[2,2048]{1,0:T(2,128)S(1)} %bitcast.14) | data formatting | bytes 32768
  59.8 0.6 %copy.20 = f32[2,6,2048]{2,0,1:T(2,128)} copy(f32[2,6,2048]{2,0,1:T(2,128)S(1)} %bitcast.13) | data formatting | bytes 196608
Async XLA Ops:
  0.6 1.0 %copy-start = (s32[2,2048]{1,0:T(2,128)S(1)}, s32[2,2048]{1,0:T(2,128)}, u32[]{:S(2)}) copy-start(s32[2,2048]{1,0:T(2,128)} %conn_x_in.1) | copy-start | bytes 49156
  0.6 1.0 %copy-start.1 = (s32[2,2048]{1,0:T(2,128)S(1)}, s32[2,2048]{1,0:T(2,128)}, u32[]{:S(2)}) copy-start(s32[2,2048]{1,0:T(2,128)} %conn_y_in.1) | copy-start | bytes 49156
  0.7 1.0 %copy-start.2 = (s32[2,2048]{1,0:T(2,128)S(1)}, s32[2,2048]{1,0:T(2,128)}, u32[]{:S(2)}) copy-start(s32[2,2048]{1,0:T(2,128)} %conn_z_in.1) | copy-start | bytes 49156
  0.7 1.0 %copy-start.3 = (f32[2,2048]{1,0:T(2,128)S(1)}, f32[2,2048]{1,0:T(2,128)}, u32[]{:S(2)}) copy-start(f32[2,2048]{1,0:T(2,128)} %storage_in.1) | copy-start | bytes 49156
  0.7 1.0 %copy-start.4 = (f32[2,2048]{1,0:T(2,128)S(1)}, f32[2,2048]{1,0:T(2,128)}, u32[]{:S(2)}) copy-start(f32[2,2048]{1,0:T(2,128)} %source_in.1) | copy-start | bytes 49156
  0.7 1.0 %copy-start.5 = (f32[2048]{0:T(1024)S(1)}, f32[2048]{0:T(1024)}, u32[]{:S(2)}) copy-start(f32[2048]{0:T(1024)} %param.16) | copy-start | bytes 24580
  0.7 1.0 %copy-start.6 = (s32[512]{0:T(512)S(1)}, s32[512]{0:T(512)}, u32[]{:S(2)}) copy-start(s32[512]{0:T(512)} %param.12) | copy-start | bytes 6148
  0.7 1.0 %copy-start.7 = (s32[64]{0:T(128)S(1)}, s32[64]{0:T(128)}, u32[]{:S(2)}) copy-start(s32[64]{0:T(128)} %param.13) | copy-start | bytes 772

commit v8 on v7

--- a/solution.py
+++ b/solution.py
@@ -1,5 +1,4 @@
 import functools
-import math
 
 import jax
 import jax.numpy as jnp
@@ -113,14 +112,12 @@
     zlist, itable, tables, sides, vtables, by_face, near_cells, far_cells, z_cells,
     near_send, near_recv, z_send, z_recv, far_send, far_recv, terms_send, terms_recv, far_next,
     near_sems, z_sems, far_sems,
-    row_send, flat_recv, side_recv, deep_recv, sum_sems,
+    row_send, flat_recv, deep_recv, sum_sems,
 ):
     region, sub = lax.axis_index("region"), lax.axis_index("sub")
-    n_side = math.isqrt(n_sub // 4)
-    n_flat, n_deep = 2 * n_side, 2 * n_region
+    n_flat, n_deep = n_sub // 2, 2 * n_region
     core, deep = lax.rem(sub, 2), lax.rem(lax.div(sub, 2), 2)
-    place_x, place_y = lax.div(sub, 4 * n_side), lax.rem(lax.div(sub, 4), n_side)
-    flat_me = place_x * 2 + core
+    flat_me = lax.div(sub, 4) * 2 + core
     deep_me = deep * n_region + region
     upper = core == 1
     far_peer, near_peer = lax.rem(sub + n_sub + 2 * core - 1, n_sub), sub + 1 - 2 * core
@@ -128,12 +125,7 @@
 
     def flat_peer(offset):
         peer = lax.rem(flat_me + offset, n_flat)
-        column = lax.div(peer, 2) * n_side + place_y
-        return (region, column * 4 + deep * 2 + lax.rem(peer, 2))
-
-    def side_peer(offset):
-        column = place_x * n_side + lax.rem(place_y + offset, n_side)
-        return (region, column * 4 + deep * 2 + core)
+        return (region, lax.div(peer, 2) * 4 + deep * 2 + lax.rem(peer, 2))
 
     def deep_peer(offset):
         peer = lax.rem(deep_me + offset, n_deep)
@@ -145,9 +137,8 @@
         pl.semaphore_signal(barrier, inc=1, device_id=device, device_id_type=MESH)
 
     greet((region, far_peer))
-    for peer, count in ((deep_peer, n_deep), (flat_peer, n_flat), (side_peer, n_side)):
-        for j in range(1, count):
-            greet(peer(j))
+    for peer, count in ((deep_peer, n_deep), (flat_peer, n_flat)):
+        lax.fori_loop(1, count, lambda j, c, peer=peer: (greet(peer(j)), c)[1], 0)
 
     def lanes(i):
         return slice(LANES * i, LANES * (i + 1))
@@ -272,7 +263,7 @@
                 for s in range(2):
                     tables[c * 6 + d * 2 + s] = g[c][d][s]
 
-    greetings = 1 + (n_flat - 1) + (n_deep - 1) + (n_side - 1)
+    greetings = 1 + (n_flat - 1) + (n_deep - 1)
     fill_far(0, rhs_g)
     fill_near(0, rhs_g)
     pl.semaphore_wait(barrier, greetings)
@@ -363,15 +354,14 @@
         )
         return total - (load[0] * solved[0] + load[1] * solved[1])
 
-    stages = (
-        (flat_recv, flat_peer, n_flat), (side_recv, side_peer, n_side), (deep_recv, deep_peer, n_deep)
-    )
+    stages = ((flat_recv, flat_peer, n_flat), (deep_recv, deep_peer, n_deep))
 
     def sum_start(k, stage, row):
         recv, peer, count = stages[stage]
         row_send[k, stage, 0:1, :] = row
         recv[k, count - 1 : count, :] = row
-        for j in sorted(range(1, count), key=lambda j: -min(j, count - j)):
+
+        def one(j, carry):
             pltpu.make_async_remote_copy(
                 src_ref=row_send.at[k, stage, pl.ds(0, 1)],
                 dst_ref=recv.at[k, pl.ds(j - 1, 1)],
@@ -380,12 +370,14 @@
                 device_id=peer(j),
                 device_id_type=MESH,
             ).start()
+            return carry
+
+        lax.fori_loop(1, count, one, 0)
 
     def drain(k, stage, which):
         recv, _, count = stages[stage]
-        if count > 1:
-            rows = recv.at[k, pl.ds(0, count - 1)]
-            pltpu.make_async_copy(rows, rows, sum_sems.at[k, stage, which]).wait()
+        rows = recv.at[k, pl.ds(0, count - 1)]
+        pltpu.make_async_copy(rows, rows, sum_sems.at[k, stage, which]).wait()
 
     def sum_done(k, stage):
         drain(k, stage, 1)
@@ -419,7 +411,6 @@
     far_send[1, 8:16, :] = side_values(0, far_cells, face_load(apart))
     far_second.start()
     by_faces(0, b)
-    sum_start(0, 2, sum_done(0, 1))
     far_terms.wait_recv()
     far_second.wait_recv()
     add_far(w, far_recv.at[1])
@@ -441,7 +432,7 @@
     ww = assemble(2, g_w)
     add_far(ww, far_next)
 
-    first = sum_done(0, 2)
+    first = sum_done(0, 1)
     scale = pick(first, 0) / pick(first, 1)
 
     def blend(u, factor, v):
@@ -461,15 +452,14 @@
     by_faces(1, w)
     sum_start(1, 1, sum_done(1, 0))
     by_faces(2, ww)
-    sum_start(1, 2, sum_done(1, 1))
     for step in range(ROUNDS):
         for copy in copies(step):
             copy.wait_send()
     for copy in (far_first, far_second, far_terms):
         copy.wait_send()
-    for k, stage in ((0, 0), (0, 1), (0, 2), (1, 0), (1, 1)):
+    for k, stage in ((0, 0), (0, 1), (1, 0)):
         drain(k, stage, 0)
-    sums = sum_done(1, 2)
+    sums = sum_done(1, 1)
     bb, br, rr_, rs_, ss_, sas_ = (pick(sums, k) for k in range(6))
 
     norm_0 = bb
@@ -509,24 +499,33 @@
     by_face[0] = on_b * by_face[0] + on_w * by_face[1] + on_ww * by_face[2]
     for i in range(49):
         trace_out[:, LANES * i : LANES * (i + 1)] = by_face[0, 2 * i : 2 * i + 2, :]
-    drain(1, 2, 0)
+    drain(1, 1, 0)
+
+
+def hand_on(*refs):
+    sems = refs[6]
+    moves = [pltpu.make_async_copy(refs[k], refs[3 + k], sems.at[k]) for k in range(3)]
+    for move in moves:
+        move.start()
+    for move in moves:
+        move.wait()
 
 
 def solution(mesh):
     n_region, n_sub = mesh.shape["region"], mesh.shape["sub"]
-    n_side = math.isqrt(n_sub // 4)
-    n_flat, n_deep = 2 * n_side, 2 * n_region
+    n_flat, n_deep = n_sub // 2, 2 * n_region
 
     def local(conn_x, conn_y, conn_z, send_y, send_z, perm, storage, sigma, source):
         vmem = pl.BlockSpec(memory_space=pltpu.VMEM)
         dma = pltpu.SemaphoreType.DMA
-        trace, pressure, flux = pl.pallas_call(
+        shapes = (
+            jax.ShapeDtypeStruct((2, NXF + 2 * E_DEV), F32),
+            jax.ShapeDtypeStruct((2 * ROWS, LANES), F32),
+            jax.ShapeDtypeStruct((12 * ROWS, LANES), F32),
+        )
+        results = pl.pallas_call(
             functools.partial(kernel, n_region, n_sub),
-            out_shape=(
-                jax.ShapeDtypeStruct((2, NXF + 2 * E_DEV), F32),
-                jax.ShapeDtypeStruct((2 * ROWS, LANES), F32),
-                jax.ShapeDtypeStruct((12 * ROWS, LANES), F32),
-            ),
+            out_shape=shapes,
             in_specs=[vmem] * 9,
             out_specs=(vmem,) * 3,
             scratch_shapes=[
@@ -557,11 +556,10 @@
                 dma((ROUNDS, 2)),
                 dma((ROUNDS, 2, 2)),
                 dma((3, 2)),
-                pltpu.VMEM((2, 3, 8, LANES), F32),
+                pltpu.VMEM((2, 2, 8, LANES), F32),
                 pltpu.VMEM((2, n_flat, LANES), F32),
-                pltpu.VMEM((2, n_side, LANES), F32),
                 pltpu.VMEM((2, n_deep, LANES), F32),
-                dma((2, 3, 2)),
+                dma((2, 2, 2)),
             ],
             compiler_params=pltpu.CompilerParams(
                 collective_id=0, has_side_effects=True, vmem_limit_bytes=32 * 1024 * 1024
@@ -570,6 +568,14 @@
             conn_x, conn_y, conn_z, send_y.reshape(4, LANES), send_z.reshape(1, 64),
             perm, storage, sigma.reshape(ROWS, LANES), source,
         )
+        anywhere = pl.BlockSpec(memory_space=pl.ANY)
+        trace, pressure, flux = pl.pallas_call(
+            hand_on,
+            out_shape=shapes,
+            in_specs=[anywhere] * 3,
+            out_specs=(anywhere,) * 3,
+            scratch_shapes=[dma((3,))],
+        )(*results)
         pressure = pressure.reshape(ROWS, 2, LANES).transpose(1, 0, 2).reshape(2, E_DEV)
         flux = flux.reshape(6, ROWS, 2, LANES).transpose(2, 0, 1, 3).reshape(2, 6, E_DEV)
         return trace, pressure, flux

time: 61.3 us -> 65.7 us (1.072)
  Pallas kernels: 56.9 us -> 61.9 us
    pallas_call x1 -> x2, Pallas kernels: 56.9 us -> 61.9 us  [the longest x1 55.8 us: local(): pl.pallas_call(functools.partial(kernel, n_region, n_sub), out_shape=shap...]
    unnamed x20 -> x23, local copies, waits for them, and re-layouts: 2.78 us -> 2.76 us
where the time goes in v8:
time: 65.7 us; the launch traced here: 65.4 us
  Pallas kernels  61.9 us (94%)
  local copies, waits for them, and re-layouts  2.76 us (4%)
  between operations  0.78 us (1%)
    pallas_call x1, Pallas kernels, local(): pl.pallas_call(functools.partial(kernel, n_region, n_sub), out_shape=shap...  55.8 us
    pallas_call x1, Pallas kernels, local(): pl.pallas_call(hand_on, out_shape=shapes, in_specs=[anywhere] * 3, out_sp...  6.12 us
    unnamed x23, local copies, waits for them, and re-layouts  2.76 us

profile of v8, /device:TPU:1, one launch (start us, length us, event | category | flops | bytes accessed | tf_op | source)
XLA Modules:
  0.0 65.4 jit_solution(11535590885099238481)
XLA Ops:
  0.6 0.0 copy-start.2
  0.6 0.0 copy-start.3
  0.7 0.0 copy-start.4
  0.7 0.0 copy-start.5
  0.7 0.0 copy-start.6
  0.7 0.0 copy-start.8
  0.7 0.0 copy-start.9
  0.7 0.0 copy-start.10
  0.7 0.9 %copy.12.perm_in = f32[2,3,2048]{2,1,0:T(4,128)S(1)} copy(f32[2,3,2048]{2,0,1:T(2,128)} %param.14) | data formatting | bytes 98304 | tf_op args[5]
  1.6 0.0 copy-done.2
  1.6 0.0 copy-done.3
  1.6 0.0 copy-done.4
  1.6 0.0 copy-done.5
  1.6 0.0 copy-done.6
  1.6 0.0 copy-done.8
  1.7 0.0 copy-done.9
  1.7 0.0 copy-done.10
  1.7 55.8 %shard_map.112 = (f32[2,6272]{1,0:T(2,128)S(1)}, f32[32,128]{1,0:T(8,128)S(1)}, f32[192,128]{1,0:T(8,128)S(1)}) custom-call(s32[2,2048]{1,0:T(2,128)S(1)} %copy-done.2, s32[2,2048]{1,0:T(2,128)S(1)} %copy-done.3, s32[2,2048]{1,0:T(2,128)S(1)} %copy-done.4, s32[4,128]{1,0:T(4,128)S(1)} %bitcast.14, s32[1,64]{1,0:T(1,128)S(1)} %bitcast.15, ...), custom_call_target="tpu_custom_call" | custom-call | tf_op jit(solution)/shard_map/pallas_call | solution.py:526
  57.4 0.0 copy-start
  57.5 0.6 copy-done
  58.1 0.0 copy-start.1
  58.1 0.6 copy-done.1
  58.7 0.0 copy-start.7
  58.7 0.6 copy-done.7
  59.3 6.1 %shard_map.113 = (f32[2,6272]{1,0:T(2,128)}, f32[32,128]{1,0:T(8,128)}, f32[192,128]{1,0:T(8,128)}) custom-call(f32[2,6272]{1,0:T(2,128)} %copy-done.1, f32[32,128]{1,0:T(8,128)} %copy-done.7, f32[192,128]{1,0:T(8,128)} %copy-done), custom_call_target="tpu_custom_call" | custom-call | tf_op jit(solution)/shard_map/pallas_call | solution.py:572
Async XLA Ops:
  0.6 1.0 %copy-start.2 = (s32[2,2048]{1,0:T(2,128)S(1)}, s32[2,2048]{1,0:T(2,128)}, u32[]{:S(2)}) copy-start(s32[2,2048]{1,0:T(2,128)} %conn_x_in.1) | copy-start | bytes 49156
  0.6 1.0 %copy-start.3 = (s32[2,2048]{1,0:T(2,128)S(1)}, s32[2,2048]{1,0:T(2,128)}, u32[]{:S(2)}) copy-start(s32[2,2048]{1,0:T(2,128)} %conn_y_in.1) | copy-start | bytes 49156
  0.7 1.0 %copy-start.4 = (s32[2,2048]{1,0:T(2,128)S(1)}, s32[2,2048]{1,0:T(2,128)}, u32[]{:S(2)}) copy-start(s32[2,2048]{1,0:T(2,128)} %conn_z_in.1) | copy-start | bytes 49156
  0.7 1.0 %copy-start.5 = (f32[2,2048]{1,0:T(2,128)S(1)}, f32[2,2048]{1,0:T(2,128)}, u32[]{:S(2)}) copy-start(f32[2,2048]{1,0:T(2,128)} %storage_in.1) | copy-start | bytes 49156
  0.7 1.0 %copy-start.6 = (f32[2,2048]{1,0:T(2,128)S(1)}, f32[2,2048]{1,0:T(2,128)}, u32[]{:S(2)}) copy-start(f32[2,2048]{1,0:T(2,128)} %source_in.1) | copy-start | bytes 49156
  0.7 1.0 %copy-start.8 = (f32[2048]{0:T(1024)S(1)}, f32[2048]{0:T(1024)}, u32[]{:S(2)}) copy-start(f32[2048]{0:T(1024)} %param.16) | copy-start | bytes 24580
  0.7 1.0 %copy-start.9 = (s32[512]{0:T(512)S(1)}, s32[512]{0:T(512)}, u32[]{:S(2)}) copy-start(s32[512]{0:T(512)} %param.12) | copy-start | bytes 6148
  0.7 1.0 %copy-start.10 = (s32[64]{0:T(128)S(1)}, s32[64]{0:T(128)}, u32[]{:S(2)}) copy-start(s32[64]{0:T(128)} %param.13) | copy-start | bytes 772
  57.4 0.6 copy-start
  58.1 0.6 copy-start.1
  58.7 0.6 copy-start.7

commit v9 on v8

--- a/solution.py
+++ b/solution.py
@@ -449,8 +449,8 @@
     load_ww = face_load(ww)
     inside_ww = solve(load_ww)
     g_ww = contributions(ww, inside_ww)
+    sum_start(1, 1, sum_done(1, 0))
     by_faces(1, w)
-    sum_start(1, 1, sum_done(1, 0))
     by_faces(2, ww)
     for step in range(ROUNDS):
         for copy in copies(step):
@@ -502,15 +502,6 @@
     drain(1, 1, 0)
 
 
-def hand_on(*refs):
-    sems = refs[6]
-    moves = [pltpu.make_async_copy(refs[k], refs[3 + k], sems.at[k]) for k in range(3)]
-    for move in moves:
-        move.start()
-    for move in moves:
-        move.wait()
-
-
 def solution(mesh):
     n_region, n_sub = mesh.shape["region"], mesh.shape["sub"]
     n_flat, n_deep = n_sub // 2, 2 * n_region
@@ -523,7 +514,7 @@
             jax.ShapeDtypeStruct((2 * ROWS, LANES), F32),
             jax.ShapeDtypeStruct((12 * ROWS, LANES), F32),
         )
-        results = pl.pallas_call(
+        trace, pressure, flux = pl.pallas_call(
             functools.partial(kernel, n_region, n_sub),
             out_shape=shapes,
             in_specs=[vmem] * 9,
@@ -568,14 +559,6 @@
             conn_x, conn_y, conn_z, send_y.reshape(4, LANES), send_z.reshape(1, 64),
             perm, storage, sigma.reshape(ROWS, LANES), source,
         )
-        anywhere = pl.BlockSpec(memory_space=pl.ANY)
-        trace, pressure, flux = pl.pallas_call(
-            hand_on,
-            out_shape=shapes,
-            in_specs=[anywhere] * 3,
-            out_specs=(anywhere,) * 3,
-            scratch_shapes=[dma((3,))],
-        )(*results)
         pressure = pressure.reshape(ROWS, 2, LANES).transpose(1, 0, 2).reshape(2, E_DEV)
         flux = flux.reshape(6, ROWS, 2, LANES).transpose(2, 0, 1, 3).reshape(2, 6, E_DEV)
         return trace, pressure, flux

time: 65.7 us -> 59.6 us (0.907)
  Pallas kernels: 61.9 us -> 55.8 us
    pallas_call x1 -> x0, Pallas kernels: 6.12 us -> none  [local(): pl.pallas_call(hand_on, out_shape=shapes, in_specs=[anywhere] * 3, out_sp...]
    unnamed x23 -> x20, local copies, waits for them, and re-layouts: 2.76 us -> 2.78 us
where the time goes in v9:
time: 59.6 us; the launch traced here: 59.3 us
  Pallas kernels  55.8 us (94%)
  local copies, waits for them, and re-layouts  2.78 us (5%)
  between operations  0.77 us (1%)
    pallas_call x1, Pallas kernels, local(): pl.pallas_call(functools.partial(kernel, n_region, n_sub), out_shape=shap...  55.8 us
    unnamed x20, local copies, waits for them, and re-layouts  2.78 us

profile of v9, /device:TPU:1, one launch (start us, length us, event | category | flops | bytes accessed | tf_op | source)
XLA Modules:
  0.0 59.3 jit_solution(13308926480222911196)
XLA Ops:
  0.6 0.0 copy-start
  0.6 0.0 copy-start.1
  0.7 0.0 copy-start.2
  0.7 0.0 copy-start.3
  0.7 0.0 copy-start.4
  0.7 0.0 copy-start.5
  0.7 0.0 copy-start.6
  0.7 0.0 copy-start.7
  0.7 0.9 %copy.12.perm_in = f32[2,3,2048]{2,1,0:T(4,128)S(1)} copy(f32[2,3,2048]{2,0,1:T(2,128)} %param.14) | data formatting | bytes 98304 | tf_op args[5]
  1.6 0.0 copy-done
  1.6 0.0 copy-done.1
  1.6 0.0 copy-done.2
  1.6 0.0 copy-done.3
  1.6 0.0 copy-done.4
  1.6 0.0 copy-done.5
  1.7 0.0 copy-done.6
  1.7 0.0 copy-done.7
  1.7 55.8 %shard_map.112 = (f32[2,6272]{1,0:T(2,128)S(1)}, f32[32,128]{1,0:T(8,128)S(1)}, f32[192,128]{1,0:T(8,128)S(1)}) custom-call(s32[2,2048]{1,0:T(2,128)S(1)} %copy-done, s32[2,2048]{1,0:T(2,128)S(1)} %copy-done.1, s32[2,2048]{1,0:T(2,128)S(1)} %copy-done.2, s32[4,128]{1,0:T(4,128)S(1)} %bitcast.16, s32[1,64]{1,0:T(1,128)S(1)} %bitcast.17, ...), custom_call_target="tpu_custom_call" | custom-call | tf_op jit(solution)/shard_map/pallas_call | solution.py:517
  57.4 0.6 %copy.18 = f32[2,6272]{1,0:T(2,128)} copy(f32[2,6272]{1,0:T(2,128)S(1)} %get-tuple-element.12) | data formatting | bytes 100352
  58.1 0.6 %copy.19 = f32[2,2048]{1,0:T(2,128)} copy(f32[2,2048]{1,0:T(2,128)S(1)} %bitcast.14) | data formatting | bytes 32768
  58.7 0.6 %copy.20 = f32[2,6,2048]{2,0,1:T(2,128)} copy(f32[2,6,2048]{2,0,1:T(2,128)S(1)} %bitcast.13) | data formatting | bytes 196608
Async XLA Ops:
  0.6 1.0 %copy-start = (s32[2,2048]{1,0:T(2,128)S(1)}, s32[2,2048]{1,0:T(2,128)}, u32[]{:S(2)}) copy-start(s32[2,2048]{1,0:T(2,128)} %conn_x_in.1) | copy-start | bytes 49156
  0.6 1.0 %copy-start.1 = (s32[2,2048]{1,0:T(2,128)S(1)}, s32[2,2048]{1,0:T(2,128)}, u32[]{:S(2)}) copy-start(s32[2,2048]{1,0:T(2,128)} %conn_y_in.1) | copy-start | bytes 49156
  0.7 1.0 %copy-start.2 = (s32[2,2048]{1,0:T(2,128)S(1)}, s32[2,2048]{1,0:T(2,128)}, u32[]{:S(2)}) copy-start(s32[2,2048]{1,0:T(2,128)} %conn_z_in.1) | copy-start | bytes 49156
  0.7 1.0 %copy-start.3 = (f32[2,2048]{1,0:T(2,128)S(1)}, f32[2,2048]{1,0:T(2,128)}, u32[]{:S(2)}) copy-start(f32[2,2048]{1,0:T(2,128)} %storage_in.1) | copy-start | bytes 49156
  0.7 1.0 %copy-start.4 = (f32[2,2048]{1,0:T(2,128)S(1)}, f32[2,2048]{1,0:T(2,128)}, u32[]{:S(2)}) copy-start(f32[2,2048]{1,0:T(2,128)} %source_in.1) | copy-start | bytes 49156
  0.7 1.0 %copy-start.5 = (f32[2048]{0:T(1024)S(1)}, f32[2048]{0:T(1024)}, u32[]{:S(2)}) copy-start(f32[2048]{0:T(1024)} %param.16) | copy-start | bytes 24580
  0.7 1.0 %copy-start.6 = (s32[512]{0:T(512)S(1)}, s32[512]{0:T(512)}, u32[]{:S(2)}) copy-start(s32[512]{0:T(512)} %param.12) | copy-start | bytes 6148
  0.7 1.0 %copy-start.7 = (s32[64]{0:T(128)S(1)}, s32[64]{0:T(128)}, u32[]{:S(2)}) copy-start(s32[64]{0:T(128)} %param.13) | copy-start | bytes 772
